TPU v7x, 32 devices: a whole 2x2x4 slice. The times are simulated.
32 devices in a mesh: groups: 2 (over x), lon: 16 (over z, y, core).
Axes of the slice: x: 2, y: 2, z: 4, core: 2. Of those that a mesh axis runs over, the one named last changes fastest.
Arguments:
- queries: bfloat16 [96, 192, 512], P('groups', 'lon'), parts along dimension 0, may hold values from -8 to 8
- key_vectors: bfloat16 [96, 192, 512], P('groups', 'lon'), parts along dimension 0, may hold values from -8 to 8
- value_vectors: bfloat16 [96, 192, 512], P('groups', 'lon'), parts along dimension 0, may hold values from -6 to 6
- out_weight: bfloat16 [512, 512], replicated, may hold values from -0.25 to 0.25
- lat_window: int32 [96], P('groups'), parts along dimension 0, may hold values from 0 to 5, as said below
- lon_offset: int32 [96], P('groups'), parts along dimension 0, may hold values from 0 to 11, as said below
- cotangent: bfloat16 [96, 192, 512], P('groups', 'lon'), parts along dimension 0, may hold values from -6 to 6
Outputs:
- block_out: bfloat16 [96, 192, 512], P('groups', 'lon'), parts along dimension 0
- grad_queries: bfloat16 [96, 192, 512], P('groups', 'lon'), parts along dimension 0
- grad_keys: bfloat16 [96, 192, 512], P('groups', 'lon'), parts along dimension 0
- grad_values: bfloat16 [96, 192, 512], P('groups', 'lon'), parts along dimension 0
- grad_out_weight: float32 [1024, 512], P('groups'), parts along dimension 0
There are 2 independent parts, one for each index of `groups`. A program takes and returns all parts, laid end to end along the dimension named above; an argument that names none is the same for every part. Nothing has to cross between parts.
Inputs may be any that keep to these rules, and one draw needn't show every extreme that they name: `lat_window`: each aligned block of 24 rows holds three latitude windows of consecutive rows, numbered in order, one of them 12 rows long. `lon_offset`: the same for all rows of one latitude window; 11 in some window of every draw.
All inputs are finite; a program needn't handle non-finite values.
Results may differ from a plain program's by a relative error of at most 0.017.
Values may be sent and summed in bfloat16 or wider, within the bound.
No kernel may reach another device: no remote copies, remote signals or barrier semaphores. Data moves between devices by JAX's collectives and lax.ppermute only.
A program may use at most 128 MiB of HBM per device.

v0:
```python
import jax
import jax.numpy as jnp
from jax import lax
from jax.sharding import PartitionSpec as P

HD = 32
WIN = 12


def passed_along(value, axis, steps):
    count = lax.axis_size(axis)
    pairs = [(source, (source + steps) % count) for source in range(count)]
    return lax.ppermute(value, axis, pairs)


def to_blocks(source, head_count):
    row_count, col_count, channels = source.shape
    shaped = source.reshape(
        row_count // (2 * WIN), 2 * WIN, col_count // WIN, WIN, head_count, channels // head_count
    )
    shaped = shaped.transpose(0, 2, 1, 3, 4, 5)
    return shaped.reshape(-1, 2 * WIN * WIN, head_count, channels // head_count)


def from_blocks(blocks, row_count, col_count):
    channels = blocks.shape[2] * blocks.shape[3]
    shaped = blocks.reshape(row_count // (2 * WIN), col_count // WIN, 2 * WIN, WIN, channels)
    shaped = shaped.transpose(0, 2, 1, 3, 4)
    return shaped.reshape(row_count, col_count, channels)


def block_ids(lat_window, col_count):
    row_count = lat_window.shape[0]
    shaped = lat_window.reshape(row_count // (2 * WIN), 1, 2 * WIN, 1)
    shaped = jnp.broadcast_to(shaped, (row_count // (2 * WIN), col_count // WIN, 2 * WIN, WIN))
    return shaped.reshape(-1, 2 * WIN * WIN)


def window_pass(pieces):
    query_blk, key_blk, value_blk, grad_blk, window_ids = pieces
    scaling = float(HD) ** (-0.5)
    scores = (
        jnp.einsum("qhd,khd->hqk", query_blk, key_blk, preferred_element_type=jnp.float32) * scaling
    )
    allowed = window_ids[:, None] == window_ids[None, :]
    scores = jnp.where(allowed[None], scores, -1e30)
    row_max = jnp.max(scores, axis=2, keepdims=True)
    exponent = jnp.exp(scores - row_max)
    weights_full = exponent / jnp.sum(exponent, axis=2, keepdims=True)
    weights_round = weights_full.astype(jnp.bfloat16)
    attended = jnp.einsum(
        "hqk,khd->qhd", weights_round, value_blk, preferred_element_type=jnp.float32
    ).astype(jnp.bfloat16)
    grad_probs = jnp.einsum("qhd,khd->hqk", grad_blk, value_blk, preferred_element_type=jnp.float32)
    grad_value = jnp.einsum(
        "hqk,qhd->khd", weights_round, grad_blk, preferred_element_type=jnp.float32
    ).astype(jnp.bfloat16)
    inner = jnp.sum(weights_full * grad_probs, axis=2, keepdims=True)
    grad_scores = (weights_full * (grad_probs - inner) * scaling).astype(jnp.bfloat16)
    grad_query = jnp.einsum(
        "hqk,khd->qhd", grad_scores, key_blk, preferred_element_type=jnp.float32
    ).astype(jnp.bfloat16)
    grad_key = jnp.einsum(
        "hqk,qhd->khd", grad_scores, query_blk, preferred_element_type=jnp.float32
    ).astype(jnp.bfloat16)
    return (attended, grad_query, grad_key, grad_value)


def pick_cols(source, index):
    return jnp.take_along_axis(source, index[:, :, None], axis=1)


def per_device(queries, key_vectors, value_vectors, out_weight, lat_window, lon_offset, cotangent):
    row_count, slab_cols, channels = queries.shape
    head_count = channels // HD
    rim_cols = WIN - 1
    local_parts = (queries, key_vectors, value_vectors, cotangent)
    eastern = passed_along(
        (
            queries[:, :rim_cols],
            key_vectors[:, :rim_cols],
            value_vectors[:, :rim_cols],
            cotangent[:, :rim_cols],
        ),
        "lon",
        -1,
    )
    extended = [
        jnp.concatenate([local_part, far_part], axis=1)
        for local_part, far_part in zip(local_parts, eastern)
    ]
    view_index = lon_offset[:, None] + jnp.arange(slab_cols, dtype=jnp.int32)[None, :]
    query_view, key_view, value_view, grad_view = [
        pick_cols(whole_part, view_index) for whole_part in extended
    ]
    grad_attended = jnp.dot(
        grad_view.reshape(-1, channels), out_weight.T, preferred_element_type=jnp.float32
    )
    grad_attended = grad_attended.astype(jnp.bfloat16).reshape(row_count, slab_cols, channels)
    window_ids = block_ids(lat_window, slab_cols)
    results = lax.map(
        window_pass,
        (
            to_blocks(query_view, head_count),
            to_blocks(key_view, head_count),
            to_blocks(value_view, head_count),
            to_blocks(grad_attended, head_count),
            window_ids,
        ),
    )
    attended, grad_query, grad_key, grad_value = [
        from_blocks(part_blocks, row_count, slab_cols) for part_blocks in results
    ]
    mixed = jnp.dot(
        attended.reshape(-1, channels), out_weight, preferred_element_type=jnp.float32
    ).astype(jnp.bfloat16)
    mixed = mixed.reshape(row_count, slab_cols, channels)
    columns = jnp.arange(slab_cols, dtype=jnp.int32)[None, :]
    computed_parts = (mixed, grad_query, grad_key, grad_value)
    returned = passed_along(
        (
            mixed[:, slab_cols - rim_cols :],
            grad_query[:, slab_cols - rim_cols :],
            grad_key[:, slab_cols - rim_cols :],
            grad_value[:, slab_cols - rim_cols :],
        ),
        "lon",
        1,
    )
    own_index = rim_cols + columns - lon_offset[:, None]
    finals = [
        pick_cols(jnp.concatenate([from_west, computed], axis=1), own_index)
        for from_west, computed in zip(returned, computed_parts)
    ]
    grad_local = jnp.dot(
        attended.reshape(-1, channels).T,
        grad_view.reshape(-1, channels),
        preferred_element_type=jnp.float32,
    )
    weight_total = lax.psum(grad_local, "lon")
    return (finals[0], finals[1], finals[2], finals[3], weight_total)


def solution(mesh):
    placed = (
        P("groups", "lon", None),
        P("groups", "lon", None),
        P("groups", "lon", None),
        P(),
        P("groups"),
        P("groups"),
        P("groups", "lon", None),
    )
    return jax.shard_map(
        per_device,
        mesh=mesh,
        in_specs=placed,
        out_specs=(
            P("groups", "lon", None),
            P("groups", "lon", None),
            P("groups", "lon", None),
            P("groups", "lon", None),
            P("groups", None),
        ),
        check_vma=False,
    )
```

profile of v0, /device:TPU:0, one launch (start us, length us, event | category | flops | bytes accessed | tf_op | source)
XLA Modules:
  0.0 334.4 jit_solution(7047739755748672543)
XLA Ops:
  7.3 2.0 slice.27
  9.2 5.4 %collective-permute-start.3 = (bf16[48,11,512]{2,0,1:T(8,128)(2,1)}, bf16[48,11,512]{2,0,1:T(8,128)(2,1)}, u32[]{:S(2)}, u32[]{:S(2)}) collective-permute-start(bf16[48,11,512]{2,0,1:T(8,128)(2,1)} %slice.27), channel_id=1, source_target_pairs={{0,15},{1,0},{2,1},{3,2},{4,3},{5,4},{6,5},{7,6},{8,7},{9,8},{10,9... | collective-permute-start | bytes 1622024 | tf_op jit(solution)/shard_map/ppermute | solution.py:13
  14.7 1.9 slice.24
  17.2 1.9 slice.26
  21.6 17.6 %collective-permute-done.1 = bf16[48,11,512]{2,0,1:T(8,128)(2,1)S(1)} collective-permute-done((bf16[48,11,512]{2,0,1:T(8,128)(2,1)S(1)}, bf16[48,11,512]{2,0,1:T(8,128)(2,1)S(1)}, u32[]{:S(2)}, u32[]{:S(2)}) %collective-permute-start.1) | collective-permute-done | bytes 540704 | tf_op jit(solution)/shard_map/ppermute | solution.py:13
  39.2 7.6 %gather_fusion.1 = bf16[576,512]{1,0:T(8,128)(2,1)S(1)} fusion(bf16[48,23,512]{2,0,1:T(8,128)(2,1)S(1)} %pad_maximum_fusion.1, s32[576]{0:T(1024)S(1)} %reshape.186), kind=kCustom, calls=%fused_computation.1.clone | custom fusion | bytes 1184256 | tf_op jit(solution)/shard_map/jit(take_along_axis)/gather | solution.py:70
  47.0 1.3 pad_maximum_fusion.2
  48.3 7.6 %gather_fusion.2 = bf16[576,512]{1,0:T(8,128)(2,1)S(1)} fusion(bf16[48,23,512]{2,0,1:T(8,128)(2,1)S(1)} %pad_maximum_fusion.2, s32[576]{0:T(1024)S(1)} %reshape.186), kind=kCustom, calls=%fused_computation.2.clone | custom fusion | bytes 1184256 | tf_op jit(solution)/shard_map/jit(take_along_axis)/gather | solution.py:70
  56.0 1.0 reshape.197
  57.0 1.3 pad_maximum_fusion
  58.3 7.6 %gather_fusion = bf16[576,512]{1,0:T(8,128)(2,1)S(1)} fusion(bf16[48,23,512]{2,0,1:T(8,128)(2,1)S(1)} %pad_maximum_fusion, s32[576]{0:T(1024)S(1)} %reshape.186), kind=kCustom, calls=%fused_computation.clone | custom fusion | bytes 1184256 | tf_op jit(solution)/shard_map/jit(take_along_axis)/gather | solution.py:70
  65.9 1.0 reshape.189
  67.0 1.3 pad_maximum_fusion.3
  68.3 7.6 %gather_fusion.3 = bf16[576,512]{1,0:T(8,128)(2,1)S(1)} fusion(bf16[48,23,512]{2,0,1:T(8,128)(2,1)S(1)} %pad_maximum_fusion.3, s32[576]{0:T(1024)S(1)} %reshape.186), kind=kCustom, calls=%fused_computation.3.clone | custom fusion | bytes 1184256 | tf_op jit(solution)/shard_map/jit(take_along_axis)/gather | solution.py:70
  76.1 3.2 broadcast_select_fusion.4
  79.3 13.3 %reshape.136 = bf16[576,512]{1,0:T(8,128)(2,1)S(1)} reshape(bf16[48,12,512]{2,1,0:T(8,128)(2,1)} %get-tuple-element.116) | data formatting | bytes 1179648 | tf_op jit(solution)/shard_map/reshape | solution.py:97
  94.3 4.0 %reshape_transpose_reshape.19 = bf16[2,288,16,32]{3,2,1,0:T(8,128)(2,1)} reshape(bf16[48,12,512]{2,1,0:T(8,128)(2,1)} %get-tuple-element.117) | data formatting | bytes 1179648 | tf_op jit(solution)/shard_map/reshape;transpose;reshape | solution.py:22
  98.3 3.9 %copy.33 = bf16[2,288,16,32]{1,3,2,0:T(8,128)(2,1)} copy(bf16[2,288,16,32]{3,2,1,0:T(8,128)(2,1)} %reshape_transpose_reshape.19) | data formatting | bytes 1179648 | tf_op jit(solution)/shard_map/while | solution.py:101
  102.2 2.7 reshape_transpose_reshape.20
  104.9 3.9 %copy.34 = bf16[2,288,16,32]{1,3,2,0:T(8,128)(2,1)} copy(bf16[2,288,16,32]{3,2,1,0:T(8,128)(2,1)} %reshape_transpose_reshape.20) | data formatting | bytes 1179648 | tf_op jit(solution)/shard_map/while | solution.py:101
  108.8 2.7 reshape_transpose_reshape.18
  111.5 3.2 copy.32
  114.8 80.8 %while.16 = (s32[]{:T(128)}, bf16[2,288,16,32]{1,3,2,0:T(8,128)(2,1)S(1)}, bf16[2,288,16,32]{1,3,2,0:T(8,128)(2,1)}, bf16[2,288,16,32]{1,3,2,0:T(8,128)(2,1)}, b...) while((s32[]{:T(128)}, ...), condition=%wide.region_4.6_spmd, body=%wide.region_0.5_spmd.sunk | while | flops 539487104 | bytes 107689488 | solution.py:101
  115.0 6.5 %fusion.161 = (f32[16,288]{1,0:T(8,128)S(1)}, f32[16,288,288]{1,2,0:T(8,128)}) fusion(pred[288,288]{0,1:T(8,128)(4,1)S(1)} %broadcast_compare_fusion.2, bf16[2,288,16,32]{1,3,2,0:T(8,128)(2,1)} %get-tuple-element.219, s32[]{:T(128)S(6)} %copy.65, bf16[2,288,16,32]{1,3,2,0:T(8,128)(2,1)} %get-tuple-element.218), kind=kOutput, calls=%fused_computation.109.clone.1 | convolution fusion | flops 90243360 | bytes 6197248 | tf_op jit(solution)/shard_map/while/body/eval_jaxpr/sub | solution.py:48
  121.4 5.0 %fusion.166 = bf16[2,288,16,32]{1,3,2,0:T(8,128)(2,1)} fusion(bf16[2,288,16,32]{1,3,2,0:T(8,128)(2,1)} %get-tuple-element.204, s32[]{:T(128)S(6)} %copy.65, bf16[2,288,16,32]{1,3,2,0:T(8,128)(2,1)S(1)} %get-tuple-element.220, f32[16,288,288]{1,2,0:T(8,128)} %get-tuple-element.187, f32[16,288]{1,0:T(8,128)S(1)} %get-tuple-element.188), kind=kOutput, calls=%fused_computation.35.clone.1 | convolution fusion | flops 87736320 | bytes 7889920 | tf_op jit(solution)/shard_map/while/body/eval_jaxpr/hqk,qhd->khd/dot_general | solution.py:55
  127.2 4.1 %fusion.163 = f32[16,288,288]{1,2,0:T(8,128)} fusion(bf16[2,288,16,32]{1,3,2,0:T(8,128)(2,1)S(1)} %get-tuple-element.220, s32[]{:T(128)S(6)} %copy.65, bf16[2,288,16,32]{1,3,2,0:T(8,128)(2,1)S(1)} %get-tuple-element.216), kind=kOutput, calls=%fused_computation.40.clone.1 | convolution fusion | flops 84934656 | bytes 6095872 | tf_op jit(solution)/shard_map/while/body/eval_jaxpr/qhd,khd->hqk/dot_general | solution.py:54
  131.3 12.0 %fusion.165 = bf16[2,288,16,32]{1,3,2,0:T(8,128)(2,1)} fusion(bf16[2,288,16,32]{1,3,2,0:T(8,128)(2,1)} %get-tuple-element.203, s32[]{:T(128)S(6)} %copy.65, f32[16,288,288]{1,2,0:T(8,128)} %fusion.163, bf16[2,288,16,32]{1,3,2,0:T(8,128)(2,1)} %get-tuple-element.218, f32[16,288,288]{1,2,0:T(8,128)} %get-tuple-element.187, ...), kind=kOutput, calls=%fused_computation.31.clone.1 | convolution fusion | flops 94376736 | bytes 29148160 | tf_op jit(solution)/shard_map/while/body/eval_jaxpr/hqk,qhd->khd/dot_general | solution.py:63
  143.3 11.9 %fusion.164 = bf16[2,288,16,32]{1,3,2,0:T(8,128)(2,1)} fusion(bf16[2,288,16,32]{1,3,2,0:T(8,128)(2,1)} %get-tuple-element.202, s32[]{:T(128)S(6)} %copy.65, f32[16,288,288]{1,2,0:T(8,128)} %fusion.163, bf16[2,288,16,32]{1,3,2,0:T(8,128)(2,1)} %get-tuple-element.219, f32[16,288,288]{1,2,0:T(8,128)} %get-tuple-element.187, ...), kind=kOutput, calls=%fused_computation.33.clone.1 | convolution fusion | flops 94376736 | bytes 29148160 | tf_op jit(solution)/shard_map/while/body/eval_jaxpr/hqk,khd->qhd/dot_general | solution.py:60
  155.3 6.5 %fusion.161 = (f32[16,288]{1,0:T(8,128)S(1)}, f32[16,288,288]{1,2,0:T(8,128)}) fusion(pred[288,288]{0,1:T(8,128)(4,1)S(1)} %broadcast_compare_fusion.2, bf16[2,288,16,32]{1,3,2,0:T(8,128)(2,1)} %get-tuple-element.219, s32[]{:T(128)S(6)} %copy.65, bf16[2,288,16,32]{1,3,2,0:T(8,128)(2,1)} %get-tuple-element.218), kind=kOutput, calls=%fused_computation.109.clone.1 | convolution fusion | flops 90243360 | bytes 6197248 | tf_op jit(solution)/shard_map/while/body/eval_jaxpr/sub | solution.py:48
  161.8 5.0 %fusion.166 = bf16[2,288,16,32]{1,3,2,0:T(8,128)(2,1)} fusion(bf16[2,288,16,32]{1,3,2,0:T(8,128)(2,1)} %get-tuple-element.204, s32[]{:T(128)S(6)} %copy.65, bf16[2,288,16,32]{1,3,2,0:T(8,128)(2,1)S(1)} %get-tuple-element.220, f32[16,288,288]{1,2,0:T(8,128)} %get-tuple-element.187, f32[16,288]{1,0:T(8,128)S(1)} %get-tuple-element.188), kind=kOutput, calls=%fused_computation.35.clone.1 | convolution fusion | flops 87736320 | bytes 7889920 | tf_op jit(solution)/shard_map/while/body/eval_jaxpr/hqk,qhd->khd/dot_general | solution.py:55
  167.6 4.1 %fusion.163 = f32[16,288,288]{1,2,0:T(8,128)} fusion(bf16[2,288,16,32]{1,3,2,0:T(8,128)(2,1)S(1)} %get-tuple-element.220, s32[]{:T(128)S(6)} %copy.65, bf16[2,288,16,32]{1,3,2,0:T(8,128)(2,1)S(1)} %get-tuple-element.216), kind=kOutput, calls=%fused_computation.40.clone.1 | convolution fusion | flops 84934656 | bytes 6095872 | tf_op jit(solution)/shard_map/while/body/eval_jaxpr/qhd,khd->hqk/dot_general | solution.py:54
  171.7 12.0 %fusion.165 = bf16[2,288,16,32]{1,3,2,0:T(8,128)(2,1)} fusion(bf16[2,288,16,32]{1,3,2,0:T(8,128)(2,1)} %get-tuple-element.203, s32[]{:T(128)S(6)} %copy.65, f32[16,288,288]{1,2,0:T(8,128)} %fusion.163, bf16[2,288,16,32]{1,3,2,0:T(8,128)(2,1)} %get-tuple-element.218, f32[16,288,288]{1,2,0:T(8,128)} %get-tuple-element.187, ...), kind=kOutput, calls=%fused_computation.31.clone.1 | convolution fusion | flops 94376736 | bytes 29148160 | tf_op jit(solution)/shard_map/while/body/eval_jaxpr/hqk,qhd->khd/dot_general | solution.py:63
  183.7 11.9 %fusion.164 = bf16[2,288,16,32]{1,3,2,0:T(8,128)(2,1)} fusion(bf16[2,288,16,32]{1,3,2,0:T(8,128)(2,1)} %get-tuple-element.202, s32[]{:T(128)S(6)} %copy.65, f32[16,288,288]{1,2,0:T(8,128)} %fusion.163, bf16[2,288,16,32]{1,3,2,0:T(8,128)(2,1)} %get-tuple-element.219, f32[16,288,288]{1,2,0:T(8,128)} %get-tuple-element.187, ...), kind=kOutput, calls=%fused_computation.33.clone.1 | convolution fusion | flops 94376736 | bytes 29148160 | tf_op jit(solution)/shard_map/while/body/eval_jaxpr/hqk,khd->qhd/dot_general | solution.py:60
  198.0 0.9 slice.48
  199.0 3.6 %copy.45 = bf16[2,288,16,32]{3,2,1,0:T(8,128)(2,1)S(1)} copy(bf16[2,288,16,32]{1,3,2,0:T(8,128)(2,1)} %get-tuple-element.64) | data formatting | bytes 1179648 | tf_op jit(solution)/shard_map/while | solution.py:101
  202.6 3.0 reshape_transpose_reshape.23
  205.6 1.5 copy.46
  207.0 0.9 slice.51
  208.1 3.2 copy.39
  211.4 3.1 reshape_transpose_reshape.21
  214.4 1.5 copy.40
  215.9 0.9 slice.49
  216.9 3.2 copy.42
  220.2 3.1 reshape_transpose_reshape.22
  223.2 1.5 copy.43
  225.7 2.6 fusion.122
  228.4 1.1 pad_maximum_fusion.4
  229.5 7.8 %gather_fusion.4 = bf16[576,512]{1,0:T(8,128)(2,1)S(1)} fusion(bf16[48,23,512]{2,0,1:T(8,128)(2,1)S(1)} %pad_maximum_fusion.4, s32[576]{0:T(1024)S(1)} %reshape.202), kind=kCustom, calls=%fused_computation.4.clone | custom fusion | bytes 1184256 | tf_op jit(solution)/shard_map/jit(take_along_axis)/gather | solution.py:70
  237.3 1.1 reshape.205
  238.4 1.1 pad_maximum_fusion.7
  239.5 7.6 %gather_fusion.7 = bf16[576,512]{1,0:T(8,128)(2,1)S(1)} fusion(bf16[48,23,512]{2,0,1:T(8,128)(2,1)S(1)} %pad_maximum_fusion.7, s32[576]{0:T(1024)S(1)} %reshape.202), kind=kCustom, calls=%fused_computation.7.clone | custom fusion | bytes 1184256 | tf_op jit(solution)/shard_map/jit(take_along_axis)/gather | solution.py:70
  247.2 1.0 reshape.217
  248.2 1.2 pad_maximum_fusion.5
  249.4 7.6 %gather_fusion.5 = bf16[576,512]{1,0:T(8,128)(2,1)S(1)} fusion(bf16[48,23,512]{2,0,1:T(8,128)(2,1)S(1)} %pad_maximum_fusion.5, s32[576]{0:T(1024)S(1)} %reshape.202), kind=kCustom, calls=%fused_computation.5.clone | custom fusion | bytes 1184256 | tf_op jit(solution)/shard_map/jit(take_along_axis)/gather | solution.py:70
  257.0 1.0 reshape.209
  258.0 1.1 pad_maximum_fusion.6
  259.2 7.6 %gather_fusion.6 = bf16[576,512]{1,0:T(8,128)(2,1)S(1)} fusion(bf16[48,23,512]{2,0,1:T(8,128)(2,1)S(1)} %pad_maximum_fusion.6, s32[576]{0:T(1024)S(1)} %reshape.202), kind=kCustom, calls=%fused_computation.6.clone | custom fusion | bytes 1184256 | tf_op jit(solution)/shard_map/jit(take_along_axis)/gather | solution.py:70
  267.0 1.8 broadcast_select_fusion
  268.7 1.1 copy.51
  269.9 1.1 copy.49
  271.0 1.1 copy.50
  272.2 1.1 copy.48
  273.3 51.8 %all-reduce.2.cloned.1.call-done = f32[512,512]{1,0:T(8,128)} async-done(((f32[512,512]{1,0:T(8,128)}), f32[512,512]{1,0:T(8,128)}) %all-reduce.2.cloned.1.call-update) | async-done | bytes 1048592 | tf_op jit(solution)/shard_map/psum | solution.py:140
  325.1 2.3 copy.78
  (89 shorter events, 10.9 us)
Async XLA Ops:
  7.2 85.4 %copy-start = (bf16[512,512]{1,0:T(8,128)(2,1)S(1)}, bf16[512,512]{1,0:T(8,128)(2,1)}, u32[]{:S(2)}) copy-start(bf16[512,512]{1,0:T(8,128)(2,1)} %param.14) | copy-start | bytes 1572868
  7.2 11.9 %copy-start.12 = (bf16[48,12,512]{2,0,1:T(8,128)(2,1)S(1)}, bf16[48,12,512]{2,0,1:T(8,128)(2,1)}, u32[]{:S(2)}) copy-start(bf16[48,12,512]{2,0,1:T(8,128)(2,1)} %param.11) | copy-start | bytes 1769476
  7.2 12.6 %copy-start.16 = (s32[48]{0:T(128)S(1)}, s32[48]{0:T(128)}, u32[]{:S(2)}) copy-start(s32[48]{0:T(128)} %param.16) | copy-start | bytes 580
  7.2 13.3 %copy-start.17 = (s32[48]{0:T(128)S(1)}, s32[48]{0:T(128)}, u32[]{:S(2)}) copy-start(s32[48]{0:T(128)} %param.15) | copy-start | bytes 580
  7.2 317.9 %all-reduce.2.cloned.1.call-start = ((), (), s32[]{:S(2)}) async-start(), calls=%async_computation | async-start | bytes 2097152 | tf_op jit(solution)/shard_map/psum | solution.py:140
  9.2 57.7 %collective-permute-start.3 = (bf16[48,11,512]{2,0,1:T(8,128)(2,1)}, bf16[48,11,512]{2,0,1:T(8,128)(2,1)}, u32[]{:S(2)}, u32[]{:S(2)}) collective-permute-start(bf16[48,11,512]{2,0,1:T(8,128)(2,1)} %slice.27), channel_id=1, source_target_pairs={{0,15},{1,0},{2,1},{3,2},{4,3},{5,4},{6,5},{7,6},{8,7},{9,8},{10,9... | collective-permute-start | bytes 1622024 | tf_op jit(solution)/shard_map/ppermute | solution.py:13
  16.5 40.4 %collective-permute-start = (bf16[48,11,512]{2,0,1:T(8,128)(2,1)}, bf16[48,11,512]{2,0,1:T(8,128)(2,1)}, u32[]{:S(2)}, u32[]{:S(2)}) collective-permute-start(bf16[48,11,512]{2,0,1:T(8,128)(2,1)} %slice.24), channel_id=1, source_target_pairs={{0,15},{1,0},{2,1},{3,2},{4,3},{5,4},{6,5},{7,6},{8,7},{9,8},{10,9... | collective-permute-start | bytes 1622024 | tf_op jit(solution)/shard_map/ppermute | solution.py:13
  19.1 27.9 %collective-permute-start.2 = (bf16[48,11,512]{2,0,1:T(8,128)(2,1)}, bf16[48,11,512]{2,0,1:T(8,128)(2,1)}, u32[]{:S(2)}, u32[]{:S(2)}) collective-permute-start(bf16[48,11,512]{2,0,1:T(8,128)(2,1)} %slice.26), channel_id=1, source_target_pairs={{0,15},{1,0},{2,1},{3,2},{4,3},{5,4},{6,5},{7,6},{8,7},{9,8},{10,9... | collective-permute-start | bytes 1622024 | tf_op jit(solution)/shard_map/ppermute | solution.py:13
  19.1 20.0 %collective-permute-start.1 = (bf16[48,11,512]{2,0,1:T(8,128)(2,1)S(1)}, bf16[48,11,512]{2,0,1:T(8,128)(2,1)S(1)}, u32[]{:S(2)}, u32[]{:S(2)}) collective-permute-start(bf16[48,11,512]{2,0,1:T(8,128)(2,1)S(1)} %slice.25), channel_id=1, source_target_pairs={{0,15},{1,0},{2,1},{3,2},{4,3},{5,4},{6,5},{7,6},{8,7},{9,8},{10,9... | collective-permute-start | bytes 1622024 | tf_op jit(solution)/shard_map/ppermute | solution.py:13
  92.6 0.8 copy-start.1
  94.3 7.9 %copy-start.10 = (bf16[48,12,512]{2,1,0:T(8,128)(2,1)S(1)}, bf16[48,12,512]{2,1,0:T(8,128)(2,1)}, u32[]{:S(2)}) copy-start(bf16[48,12,512]{2,1,0:T(8,128)(2,1)} %get-tuple-element.118) | copy-start | bytes 1769476
  108.8 5.9 %copy-start.13 = (bf16[2,288,16,32]{1,3,2,0:T(8,128)(2,1)S(1)}, bf16[2,288,16,32]{1,3,2,0:T(8,128)(2,1)}, u32[]{:S(2)}) copy-start(bf16[2,288,16,32]{1,3,2,0:T(8,128)(2,1)} %custom-call.24) | copy-start | bytes 1769476
  121.4 5.0 %copy-start.18 = (f32[16,288,288]{1,2,0:T(8,128)S(1)}, f32[16,288,288]{1,2,0:T(8,128)}, u32[]{:S(2)}) copy-start(f32[16,288,288]{1,2,0:T(8,128)} %get-tuple-element.187) | copy-start | bytes 15925252 | tf_op jit(solution)/shard_map/while
  161.8 5.0 %copy-start.18 = (f32[16,288,288]{1,2,0:T(8,128)S(1)}, f32[16,288,288]{1,2,0:T(8,128)}, u32[]{:S(2)}) copy-start(f32[16,288,288]{1,2,0:T(8,128)} %get-tuple-element.187) | copy-start | bytes 15925252 | tf_op jit(solution)/shard_map/while
  197.0 1.9 copy-start.11
  198.0 1.0 copy-start.3
  198.9 29.4 %collective-permute-start.4 = (bf16[48,11,512]{2,0,1:T(8,128)(2,1)}, bf16[48,11,512]{2,0,1:T(8,128)(2,1)}, u32[]{:S(2)}, u32[]{:S(2)}) collective-permute-start(bf16[48,11,512]{2,0,1:T(8,128)(2,1)} %slice.48), channel_id=1, source_target_pairs={{0,1},{1,2},{2,3},{3,4},{4,5},{5,6},{6,7},{7,8},{8,9},{9,10},{10,1... | collective-permute-start | bytes 1622024 | tf_op jit(solution)/shard_map/ppermute | solution.py:13
  202.6 5.4 %copy-start.14 = (s32[48,12,1]{1,0,2:T(8,128)S(1)}, s32[48,12,1]{1,0,2:T(8,128)}, u32[]{:S(2)}) copy-start(s32[48,12,1]{1,0,2:T(8,128)} %get-tuple-element.122) | copy-start | bytes 6916
  207.0 1.0 copy-start.5
  207.9 30.4 %collective-permute-start.7 = (bf16[48,11,512]{2,0,1:T(8,128)(2,1)}, bf16[48,11,512]{2,0,1:T(8,128)(2,1)}, u32[]{:S(2)}, u32[]{:S(2)}) collective-permute-start(bf16[48,11,512]{2,0,1:T(8,128)(2,1)} %slice.51), channel_id=1, source_target_pairs={{0,1},{1,2},{2,3},{3,4},{4,5},{5,6},{6,7},{7,8},{8,9},{9,10},{10,1... | collective-permute-start | bytes 1622024 | tf_op jit(solution)/shard_map/ppermute | solution.py:13
  215.9 1.1 copy-start.7
  216.8 31.4 %collective-permute-start.5 = (bf16[48,11,512]{2,0,1:T(8,128)(2,1)}, bf16[48,11,512]{2,0,1:T(8,128)(2,1)}, u32[]{:S(2)}, u32[]{:S(2)}) collective-permute-start(bf16[48,11,512]{2,0,1:T(8,128)(2,1)} %slice.49), channel_id=1, source_target_pairs={{0,1},{1,2},{2,3},{3,4},{4,5},{5,6},{6,7},{7,8},{8,9},{9,10},{10,1... | collective-permute-start | bytes 1622024 | tf_op jit(solution)/shard_map/ppermute | solution.py:13
  220.2 5.5 %copy-start.2 = (bf16[576,512]{1,0:T(8,128)(2,1)S(1)}, bf16[576,512]{1,0:T(8,128)(2,1)}, u32[]{:S(2)}) copy-start(bf16[576,512]{1,0:T(8,128)(2,1)} %copy-done.1) | copy-start | bytes 1769476
  223.2 5.1 %copy-start.4 = (bf16[48,12,512]{2,0,1:T(8,128)(2,1)S(1)}, bf16[48,12,512]{2,0,1:T(8,128)(2,1)}, u32[]{:S(2)}) copy-start(bf16[48,12,512]{2,0,1:T(8,128)(2,1)} %copy-done.3) | copy-start | bytes 1769476
  225.6 32.4 %collective-permute-start.6 = (bf16[48,11,512]{2,0,1:T(8,128)(2,1)}, bf16[48,11,512]{2,0,1:T(8,128)(2,1)}, u32[]{:S(2)}, u32[]{:S(2)}) collective-permute-start(bf16[48,11,512]{2,0,1:T(8,128)(2,1)} %slice.50), channel_id=1, source_target_pairs={{0,1},{1,2},{2,3},{3,4},{4,5},{5,6},{6,7},{7,8},{8,9},{9,10},{10,1... | collective-permute-start | bytes 1622024 | tf_op jit(solution)/shard_map/ppermute | solution.py:13
  229.5 8.9 %copy-start.6 = (bf16[48,12,512]{2,0,1:T(8,128)(2,1)S(1)}, bf16[48,12,512]{2,0,1:T(8,128)(2,1)}, u32[]{:S(2)}) copy-start(bf16[48,12,512]{2,0,1:T(8,128)(2,1)} %copy-done.5) | copy-start | bytes 1769476
  239.5 8.7 %copy-start.8 = (bf16[48,12,512]{2,0,1:T(8,128)(2,1)S(1)}, bf16[48,12,512]{2,0,1:T(8,128)(2,1)}, u32[]{:S(2)}) copy-start(bf16[48,12,512]{2,0,1:T(8,128)(2,1)} %copy-done.7) | copy-start | bytes 1769476
  259.2 7.8 %copy-start.9 = (bf16[48,12,512]{2,1,0:T(8,128)(2,1)S(1)}, bf16[48,12,512]{2,1,0:T(8,128)(2,1)}, u32[]{:S(2)}) copy-start(bf16[48,12,512]{2,1,0:T(8,128)(2,1)} %reshape.205) | copy-start | bytes 1769476
  259.2 7.8 %copy-start.15 = (pred[48,12]{1,0:T(8,128)(4,1)S(1)}, pred[48,12]{1,0:T(8,128)(4,1)}, u32[]{:S(2)}) copy-start(pred[48,12]{1,0:T(8,128)(4,1)} %get-tuple-element.120) | copy-start | bytes 1732
Sparse Core Ops, SparseCore 0:
  228.5 96.5 all-reduce.1
where the time goes:
time: 338 us; the launch traced here: 334 us
  local copies, waits for them, and re-layouts  144 us (43%)
  matrix products  84 us (25%)
  waiting for transfers between devices  69.4 us (21%)
  other arithmetic  15.3 us (5%)
  between operations  14.7 us (4%)
  starting transfers between devices  7.07 us (2%)
    gather x18, local copies, waits for them, and re-layouts, pick_cols(): return jnp.take_along_axis(source, index[:, :, None], axis=1)  66.8 us
    psum x1, waiting for transfers between devices, per_device(): weight_total = lax.psum(grad_local, 'lon')  51.8 us
    dot_general x2, matrix products, window_pass(): jnp.einsum('hqk,qhd->khd', grad_scores, query_blk, preferred_element_type...  24 us
    dot_general x2, matrix products, window_pass(): jnp.einsum('hqk,khd->qhd', grad_scores, key_blk, preferred_element_type=j...  23.8 us
    while x8, local copies, waits for them, and re-layouts, per_device(): lax.map(window_pass, (to_blocks(query_view, head_count), to_blocks(key_vi...  22.1 us
    ppermute x8, waiting for transfers between devices, passed_along(): return lax.ppermute(value, axis, pairs)  17.6 us
    another operation x6, local copies, waits for them, and re-layouts, from_blocks(): return shaped.reshape(row_count, col_count, channels)  13.5 us
    reshape x1, local copies, waits for them, and re-layouts, per_device(): grad_view.reshape(-1, channels)  13.3 us
  transfers between devices with their start and end apart: 9, of which 2 were waited for; matrix products, arithmetic and copies ran while one was open for 32% of the time, Pallas kernels for 0%

commit v1 on v0

v1 whole, which is shorter than its diff:
```python
import functools

import jax
import jax.numpy as jnp
from jax import lax
from jax.experimental import pallas as pl
from jax.experimental.pallas import tpu as pltpu
from jax.sharding import PartitionSpec as P

HD = 32
WIN = 12
PAD = 16
LANES = 128
GH = LANES // HD
SUB = WIN * WIN
SLOTS = 14
BUF = 176
OWN = WIN * PAD
BF = jnp.bfloat16
F32 = jnp.float32
VMEM_LIMIT = 48 * 1024 * 1024
NN = (((1,), (0,)), ((), ()))
NT = (((1,), (1,)), ((), ()))
TN = (((0,), (0,)), ((), ()))


def dot(a, b, dims=NN):
    return lax.dot_general(a, b, dims, preferred_element_type=F32)


def passed_along(value, axis, steps):
    count = lax.axis_size(axis)
    pairs = [(source, (source + steps) % count) for source in range(count)]
    return lax.ppermute(value, axis, pairs)


def swapped(value, axis, bit):
    count = lax.axis_size(axis)
    return lax.ppermute(value, axis, [(source, source ^ bit) for source in range(count)])


def sub_layout(lat, lon, sub):
    base = 2 * WIN * (sub // 2)
    first = lat[base]
    leading = lat[base + WIN - 1] == first
    trailing = lat[base + WIN] == lat[base + 2 * WIN - 1]
    count = jnp.int32(0)
    for i in range(WIN):
        count += (lat[base + i] == first).astype(jnp.int32)
    start = jnp.where(leading, 0, jnp.where(trailing, WIN, count))
    if sub % 2 == 0:
        off = lon[base + start]
        return jnp.int32(WIN), off, off, lambda i: base + start + i
    row = lambda i: base + i + jnp.where(i >= start, WIN, 0)
    head = lat[row(0)]
    split = jnp.int32(0)
    for i in range(WIN):
        split += (lat[row(i)] == head).astype(jnp.int32)
    return split, lon[row(0)], lon[row(WIN - 1)], row


def west_groups(off):
    total = jnp.zeros_like(off)
    for g in range(4):
        total += (off <= 10 - 3 * g).astype(jnp.int32)
    return total


def column(count):
    return lax.broadcasted_iota(jnp.int32, (count, 1), 0)


def one_hot(target, width):
    lanes = lax.broadcasted_iota(jnp.int32, (target.shape[0], width), 1)
    return jnp.where(lanes == target, 1.0, 0.0).astype(BF)


def split_div(n, by):
    q = (n * ((1 << 20) // by + 1)) >> 20
    return q, n - q * by


def slot_places(split, off1, off2):
    i, u = split_div(column(BUF), SLOTS)
    off = jnp.where(i < split, off1, off2)
    real = i < WIN
    nw = west_groups(off)
    gw = jnp.zeros_like(off)
    ge = jnp.zeros_like(off)
    rest = WIN - off
    for k in range(1, 4):
        gw += (u >= k * off).astype(jnp.int32)
        ge += (u >= k * rest).astype(jnp.int32)
    west = (real & (u < nw * off), gw, u - gw * off)
    east = (real & (u < (4 - nw) * rest), nw + ge, off + u - ge * rest)
    return i, off, west, east


def pack_kernel(
    lat, lon, q_ref, k_ref, v_ref, cot_ref, w_ref,
    tab_ref, xf_ref, xg_ref, wf_ref, ef_ref, wg_ref, eg_ref, pad_ref,
):
    rows = q_ref.shape[0]
    for a, ref in enumerate((q_ref, k_ref, v_ref, cot_ref)):
        pad_ref[a, :, 0:WIN, :] = ref[...]
        pad_ref[a, :, WIN:PAD, :] = jnp.zeros((rows, PAD - WIN, ref.shape[2]), BF)
    cot = pad_ref[3].reshape(rows * PAD, -1)
    pad_ref[3] = dot(cot, w_ref[...], NT).astype(BF).reshape(rows, PAD, -1)
    for sub in range(rows // WIN):
        split, off1, off2, row = sub_layout(lat, lon, sub)
        tab_ref[sub, 0] = split
        tab_ref[sub, 1] = off1
        tab_ref[sub, 2] = off2
        for i in range(WIN):
            r = row(i)
            tab_ref[sub, 4 + i] = r
            for g in range(4):
                lanes = slice(g * LANES, (g + 1) * LANES)
                for a in range(3):
                    xf_ref[sub * 4 + g, i * PAD : (i + 1) * PAD, a * LANES : (a + 1) * LANES] = (
                        pad_ref[a, r, :, lanes]
                    )
                xg_ref[sub * 4 + g, i * PAD : (i + 1) * PAD, :] = pad_ref[3, r, :, lanes]
        i, off, west, east = slot_places(split, off1, off2)
        xf = xf_ref[sub * 4 : sub * 4 + 4].reshape(4 * OWN, 3 * LANES)
        xg = xg_ref[sub * 4 : sub * 4 + 4].reshape(4 * OWN, LANES)
        for (valid, group, col), f_ref, g_ref in ((west, wf_ref, wg_ref), (east, ef_ref, eg_ref)):
            pick = one_hot(jnp.where(valid, group * OWN + i * PAD + col, -1), 4 * OWN)
            f_ref[sub] = dot(pick, xf).astype(BF)
            g_ref[sub] = dot(pick, xg).astype(BF)


def window_pick(split, off1, off2, g):
    i, p = split_div(column(SUB), WIN)
    off = jnp.where(i < split, off1, off2)
    nw = west_groups(off)
    is_west = g < nw
    rest = WIN - off
    own = (is_west & (p < rest)) | ((~is_west) & (p >= rest))
    c = off + p - jnp.where(p >= rest, WIN, 0)
    t_own = jnp.where(own, i * PAD + c, -1)
    t_west = jnp.where(is_west & (p >= rest), i * SLOTS + g * off + (p - rest), -1)
    t_east = jnp.where((~is_west) & (p < rest), i * SLOTS + (g - nw) * rest + p, -1)
    return one_hot(t_own, OWN), one_hot(t_west, BUF), one_hot(t_east, BUF)


def own_pick(split, off1, off2, g):
    n = column(OWN)
    i, c = n >> 4, n & (PAD - 1)
    off = jnp.where(i < split, off1, off2)
    is_west = g < west_groups(off)
    local = ((is_west & (c >= off)) | ((~is_west) & (c < off))) & (c < WIN)
    p = c - off + jnp.where(c < off, WIN, 0)
    return one_hot(jnp.where(local, i * WIN + p, -1), SUB)


def far_pick(split, off1, off2, g):
    n = column(OWN)
    i, c = n >> 4, n & (PAD - 1)
    off = jnp.where(i < split, off1, off2)
    nw = west_groups(off)
    is_west = g < nw
    t_west = jnp.where(is_west & (c < off), i * SLOTS + g * off + c, -1)
    t_east = jnp.where(
        (~is_west) & (c >= off) & (c < WIN), i * SLOTS + (g - nw) * (WIN - off) + (c - off), -1
    )
    return one_hot(t_west, BUF), one_hot(t_east, BUF)


def return_pick(split, off1, off2, g):
    i, off, west, east = slot_places(split, off1, off2)
    t_west = jnp.where(west[0] & (west[1] == g), i * WIN + (WIN - off) + west[2], -1)
    t_east = jnp.where(east[0] & (east[1] == g), i * WIN + east[2] - off, -1)
    return one_hot(t_west, SUB), one_hot(t_east, SUB)


def by_head(x):
    lane = lax.broadcasted_iota(jnp.int32, (1, LANES), 1) // HD
    return jnp.concatenate(
        [x * jnp.where(lane == h, 1.0, 0.0).astype(BF) for h in range(GH)], axis=0
    )


def diagonal(full):
    return jnp.concatenate(
        [full[h * HD : (h + 1) * HD, h * SUB : (h + 1) * SUB] for h in range(GH)], axis=0
    )


def forward_kernel(
    tab, xf_ref, rw_ref, re_ref, probs_ref, win_ref, own_ref, bw_ref, be_ref, aw_ref, ae_ref
):
    sub = pl.program_id(0)
    g = pl.program_id(1)
    split, off1, off2 = tab[sub, 0], tab[sub, 1], tab[sub, 2]
    p_own, p_west, p_east = window_pick(split, off1, off2, g)
    cells = dot(p_own, xf_ref[0]) + dot(p_west, rw_ref[0]) + dot(p_east, re_ref[0])
    cells = cells.astype(BF)
    win_ref[0] = cells
    query, key, value = (cells[:, a * LANES : (a + 1) * LANES] for a in range(3))
    scores = dot(key, by_head(query), NT)
    shape = scores.shape
    edge = split * WIN
    lane = lax.broadcasted_iota(jnp.int32, (1, shape[1]), 1)
    cell = lane - split_div(lane, SUB)[0] * SUB
    in_first = jnp.where(cell < edge, 1, 0)
    key_first = jnp.where(column(SUB) < edge, 1, 0)
    scores = jnp.where(key_first == in_first, scores, -1e30)
    top = jnp.max(scores, axis=0, keepdims=True)
    rate = float(HD) ** -0.5 * 1.4426950408889634
    power = jnp.exp2((scores - top) * rate)
    probs = power * (1.0 / jnp.sum(power, axis=0, keepdims=True))
    probs = probs.astype(BF)
    probs_ref[0] = probs
    att = diagonal(dot(value, probs, TN)).astype(BF)
    own_ref[0] = dot(own_pick(split, off1, off2, g), att, NT).astype(BF)
    b_west, b_east = return_pick(split, off1, off2, g)
    back_w = dot(b_west, att, NT)
    back_e = dot(b_east, att, NT)

    @pl.when(g == 0)
    def _():
        aw_ref[...] = back_w
        ae_ref[...] = back_e

    @pl.when(g > 0)
    def _():
        aw_ref[...] += back_w
        ae_ref[...] += back_e

    @pl.when(g == 3)
    def _():
        bw_ref[0] = aw_ref[...].astype(BF)
        be_ref[0] = ae_ref[...].astype(BF)


def backward_kernel(
    tab, probs_ref, win_ref, xg_ref, rw_ref, re_ref, own_ref, bw_ref, be_ref, aw_ref, ae_ref
):
    sub = pl.program_id(0)
    g = pl.program_id(1)
    split, off1, off2 = tab[sub, 0], tab[sub, 1], tab[sub, 2]
    p_own, p_west, p_east = window_pick(split, off1, off2, g)
    grad = dot(p_own, xg_ref[0]) + dot(p_west, rw_ref[0]) + dot(p_east, re_ref[0])
    grads = by_head(grad.astype(BF))
    query, key, value = (win_ref[0, :, a * LANES : (a + 1) * LANES] for a in range(3))
    queries = by_head(query)
    probs_b = probs_ref[0]
    probs = probs_b.astype(F32)
    grad_probs = dot(value, grads, NT)
    inner = jnp.sum(probs * grad_probs, axis=0, keepdims=True)
    grad_scores = (probs * (grad_probs - inner) * float(HD) ** -0.5).astype(BF)
    grad_v = dot(probs_b, grads).astype(BF)
    grad_k = dot(grad_scores, queries).astype(BF)
    grad_q = diagonal(dot(key, grad_scores, TN)).astype(BF)

    def moved(pick):
        return jnp.concatenate(
            [dot(pick, grad_q, NT), dot(pick, grad_k), dot(pick, grad_v)], axis=1
        )

    own_ref[0] = moved(own_pick(split, off1, off2, g)).astype(BF)
    b_west, b_east = return_pick(split, off1, off2, g)
    back_w = moved(b_west)
    back_e = moved(b_east)

    @pl.when(g == 0)
    def _():
        aw_ref[...] = back_w
        ae_ref[...] = back_e

    @pl.when(g > 0)
    def _():
        aw_ref[...] += back_w
        ae_ref[...] += back_e

    @pl.when(g == 3)
    def _():
        bw_ref[0] = aw_ref[...].astype(BF)
        be_ref[0] = ae_ref[...].astype(BF)


def project_kernel(tab, own_ref, rw_ref, re_ref, w_ref, cot_ref, out_ref, dw_ref, pad_ref):
    rows = out_ref.shape[0]
    for sub in range(rows // WIN):
        split, off1, off2 = tab[sub, 0], tab[sub, 1], tab[sub, 2]
        for g in range(4):
            f_west, f_east = far_pick(split, off1, off2, g)
            full = dot(f_west, rw_ref[sub]) + dot(f_east, re_ref[sub])
            full = (full + own_ref[sub * 4 + g].astype(F32)).astype(BF).reshape(WIN, PAD, LANES)
            for i in range(WIN):
                pad_ref[0, tab[sub, 4 + i], :, g * LANES : (g + 1) * LANES] = full[i]
    att = pad_ref[0].reshape(rows * PAD, -1)
    mixed = dot(att, w_ref[...]).astype(BF).reshape(rows, PAD, -1)
    out_ref[...] = mixed[:, 0:WIN, :]
    pad_ref[1, :, 0:WIN, :] = cot_ref[...]
    pad_ref[1, :, WIN:PAD, :] = jnp.zeros((rows, PAD - WIN, cot_ref.shape[2]), BF)
    cot = pad_ref[1].reshape(rows * PAD, -1)
    dw_ref[...] = dot(att, cot, TN).astype(BF)


def place_kernel(tab, own_ref, rw_ref, re_ref, dq_ref, dk_ref, dv_ref):
    rows = dq_ref.shape[0]
    for sub in range(rows // WIN):
        split, off1, off2 = tab[sub, 0], tab[sub, 1], tab[sub, 2]
        for g in range(4):
            f_west, f_east = far_pick(split, off1, off2, g)
            full = dot(f_west, rw_ref[sub]) + dot(f_east, re_ref[sub])
            full = (full + own_ref[sub * 4 + g].astype(F32)).astype(BF)
            full = full.reshape(WIN, PAD, 3 * LANES)
            for i in range(WIN):
                for a, ref in enumerate((dq_ref, dk_ref, dv_ref)):
                    ref[tab[sub, 4 + i], :, g * LANES : (g + 1) * LANES] = full[
                        i, 0:WIN, a * LANES : (a + 1) * LANES
                    ]


def shape(*dims, kind=BF):
    return jax.ShapeDtypeStruct(dims, kind)


SMEM = pl.BlockSpec(memory_space=pltpu.SMEM)
VMEM = pl.BlockSpec(memory_space=pltpu.VMEM)
PARAMS = pltpu.CompilerParams(vmem_limit_bytes=VMEM_LIMIT)


def cost(flops, size, exps=0):
    return pl.CostEstimate(flops=int(flops), bytes_accessed=int(size), transcendentals=int(exps))


def summed(partial, axis):
    index = lax.axis_index(axis)
    bits = [1 << b for b in range(lax.axis_size(axis).bit_length() - 1)]
    for bit in bits:
        upper = (index & bit) != 0
        half = partial.shape[0] // 2
        low, high = partial[:half], partial[half:]
        far = swapped(jnp.where(upper, low, high), axis, bit)
        near = jnp.where(upper, high, low)
        partial = (near.astype(F32) + far.astype(F32)).astype(BF)
    for bit in bits[::-1]:
        upper = (index & bit) != 0
        far = swapped(partial, axis, bit)
        partial = jnp.where(
            upper, jnp.concatenate([far, partial]), jnp.concatenate([partial, far])
        )
    return partial.astype(F32)


def per_device(queries, key_vectors, value_vectors, out_weight, lat_window, lon_offset, cotangent):
    rows, cols, channels = queries.shape
    subs = rows // WIN
    steps = subs * 4
    buf_f, buf_g = shape(subs, BUF, 3 * LANES), shape(subs, BUF, LANES)
    tab, own_f, own_g, west_f, east_f, west_g, east_g = pl.pallas_call(
        pack_kernel,
        in_specs=[SMEM, SMEM] + [VMEM] * 5,
        out_specs=[SMEM] + [VMEM] * 6,
        out_shape=[
            shape(subs, 4 + WIN, kind=jnp.int32),
            shape(steps, OWN, 3 * LANES), shape(steps, OWN, LANES),
            buf_f, buf_f, buf_g, buf_g,
        ],
        scratch_shapes=[pltpu.VMEM((4, rows, PAD, channels), BF)],
        compiler_params=PARAMS,
        cost_estimate=cost(4e9, 10e6),
    )(lat_window, lon_offset, queries, key_vectors, value_vectors, cotangent, out_weight)

    from_east_f = passed_along(west_f, "lon", -1)
    from_west_f = passed_along(east_f, "lon", 1)
    from_east_g = passed_along(west_g, "lon", -1)
    from_west_g = passed_along(east_g, "lon", 1)

    step = lambda *dims: pl.BlockSpec((1,) + dims, lambda s, g: (s * 4 + g, 0, 0))
    each = lambda *dims: pl.BlockSpec((1,) + dims, lambda s, g: (s, 0, 0))
    probs, windows, own_a, back_e_a, back_w_a = pl.pallas_call(
        forward_kernel,
        grid=(subs, 4),
        in_specs=[SMEM, step(OWN, 3 * LANES), each(BUF, 3 * LANES), each(BUF, 3 * LANES)],
        out_specs=[
            step(SUB, GH * SUB), step(SUB, 3 * LANES), step(OWN, LANES),
            each(BUF, LANES), each(BUF, LANES),
        ],
        out_shape=[
            shape(steps, SUB, GH * SUB), shape(steps, SUB, 3 * LANES), shape(steps, OWN, LANES),
            buf_g, buf_g,
        ],
        scratch_shapes=[pltpu.VMEM((BUF, LANES), F32)] * 2,
        compiler_params=PARAMS,
        cost_estimate=cost(6e9, 10e6, 1.4e6),
    )(tab, own_f, from_east_f, from_west_f)

    home_w_a = passed_along(back_e_a, "lon", 1)
    home_e_a = passed_along(back_w_a, "lon", -1)

    own_d, back_e_d, back_w_d = pl.pallas_call(
        backward_kernel,
        grid=(subs, 4),
        in_specs=[
            SMEM, step(SUB, GH * SUB), step(SUB, 3 * LANES), step(OWN, LANES),
            each(BUF, LANES), each(BUF, LANES),
        ],
        out_specs=[step(OWN, 3 * LANES), each(BUF, 3 * LANES), each(BUF, 3 * LANES)],
        out_shape=[shape(steps, OWN, 3 * LANES), buf_f, buf_f],
        scratch_shapes=[pltpu.VMEM((BUF, 3 * LANES), F32)] * 2,
        compiler_params=PARAMS,
        cost_estimate=cost(8e9, 10e6),
    )(tab, probs, windows, own_g, from_east_g, from_west_g)

    home_w_d = passed_along(back_e_d, "lon", 1)
    home_e_d = passed_along(back_w_d, "lon", -1)

    whole = shape(rows, cols, channels)
    mixed, partial = pl.pallas_call(
        project_kernel,
        in_specs=[SMEM] + [VMEM] * 5,
        out_specs=[VMEM] * 2,
        out_shape=[whole, shape(channels, channels)],
        scratch_shapes=[pltpu.VMEM((2, rows, PAD, channels), BF)],
        compiler_params=PARAMS,
        cost_estimate=cost(2e9, 4e6),
    )(tab, own_a, home_w_a, home_e_a, out_weight, cotangent)

    grads = pl.pallas_call(
        place_kernel,
        in_specs=[SMEM] + [VMEM] * 3,
        out_specs=[VMEM] * 3,
        out_shape=[whole] * 3,
        compiler_params=PARAMS,
        cost_estimate=cost(2e9, 6e6),
    )(tab, own_d, home_w_d, home_e_d)

    return (mixed, grads[0], grads[1], grads[2], summed(partial, "lon"))


def solution(mesh):
    placed = (
        P("groups", "lon", None),
        P("groups", "lon", None),
        P("groups", "lon", None),
        P(),
        P("groups"),
        P("groups"),
        P("groups", "lon", None),
    )
    return jax.shard_map(
        per_device,
        mesh=mesh,
        in_specs=placed,
        out_specs=(
            P("groups", "lon", None),
            P("groups", "lon", None),
            P("groups", "lon", None),
            P("groups", "lon", None),
            P("groups", None),
        ),
        check_vma=False,
    )
```

time: 338 us -> 140 us (0.41)
  local copies, waits for them, and re-layouts: 144 us -> 15.5 us
  matrix products: 84 us -> 0 us
  Pallas kernels: 0 us -> 56.9 us
  waiting for transfers between devices: 69.4 us -> 44.6 us
  between operations: 14.7 us -> 0.91 us
  other arithmetic: 15.3 us -> 1.53 us
  starting transfers between devices: 7.07 us -> 19.8 us
    dot_general x13 -> x0, matrix products: 71.1 us -> none  [the longest x2 24 us: window_pass(): jnp.einsum('hqk,qhd->khd', grad_scores, query_blk, preferred_element_type...]
    gather x18 -> x0, local copies, waits for them, and re-layouts: 66.8 us -> none  [pick_cols(): return jnp.take_along_axis(source, index[:, :, None], axis=1)]
    pallas_call x0 -> x5, Pallas kernels: none -> 56.9 us  [the longest x1 23.1 us: per_device(): pl.pallas_call(backward_kernel, grid=(subs, 4), in_specs=[SMEM, step(SUB,...]
    psum x1 -> x0, waiting for transfers between devices: 51.8 us -> none  [per_device(): weight_total = lax.psum(grad_local, 'lon')]
    ppermute x0 -> x8, waiting for transfers between devices: none -> 26.3 us  [swapped(): lax.ppermute(value, axis, [(source, source ^ bit) for source in range(cou...]
    another operation x11 -> x0, local copies, waits for them, and re-layouts: 24.2 us -> none  [the longest x6 13.5 us: from_blocks(): return shaped.reshape(row_count, col_count, channels)]
    while x12 -> x0, local copies, waits for them, and re-layouts: 22.1 us -> none  [the longest x8 22.1 us: per_device(): lax.map(window_pass, (to_blocks(query_view, head_count), to_blocks(key_vi...]
    reshape x3 -> x0, local copies, waits for them, and re-layouts: 13.8 us -> none  [the longest x1 13.3 us: per_device(): grad_view.reshape(-1, channels)]
  transfers between devices with their start and end apart: 9 -> 16, of which waited for: 2 -> 10; matrix products, arithmetic and copies ran while one was open for 32% -> 3% of each run, Pallas kernels for 0% -> 19%
where the time goes in v1:
time: 140 us; the launch traced here: 139 us
  Pallas kernels  56.9 us (41%)
  waiting for transfers between devices  44.6 us (32%)
  starting transfers between devices  19.8 us (14%)
  local copies, waits for them, and re-layouts  15.5 us (11%)
  other arithmetic  1.53 us (1%)
    ppermute x8, waiting for transfers between devices, swapped(): lax.ppermute(value, axis, [(source, source ^ bit) for source in range(cou...  26.3 us
    pallas_call x1, Pallas kernels, per_device(): pl.pallas_call(backward_kernel, grid=(subs, 4), in_specs=[SMEM, step(SUB,...  23.1 us
    pallas_call x1, Pallas kernels, per_device(): pl.pallas_call(forward_kernel, grid=(subs, 4), in_specs=[SMEM, step(OWN,...  22.6 us
    ppermute x8, waiting for transfers between devices, passed_along(): return lax.ppermute(value, axis, pairs)  18.3 us
    unnamed x32, local copies, waits for them, and re-layouts  15.5 us
    ppermute x8, starting transfers between devices, passed_along(): return lax.ppermute(value, axis, pairs)  15 us
    pallas_call x1, Pallas kernels, per_device(): pl.pallas_call(pack_kernel, in_specs=[SMEM, SMEM] + [VMEM] * 5, out_specs...  4.86 us
    ppermute x8, starting transfers between devices, swapped(): lax.ppermute(value, axis, [(source, source ^ bit) for source in range(cou...  4.78 us
  transfers between devices with their start and end apart: 16, of which 10 were waited for; matrix products, arithmetic and copies ran while one was open for 3% of the time, Pallas kernels for 19%

profile of v1, /device:TPU:0, one launch (start us, length us, event | category | flops | bytes accessed | tf_op | source)
XLA Modules:
  0.0 139.3 jit_solution(6244042741218236886)
XLA Ops:
  0.6 0.0 copy-start.10
  0.6 0.0 copy-start.11
  0.7 1.5 %copy.15.cot_ref = bf16[48,12,512]{2,1,0:T(8,128)(2,1)S(1)} copy(bf16[48,12,512]{2,0,1:T(8,128)(2,1)} %param.13) | data formatting | bytes 1179648 | tf_op args[6]
  2.1 0.0 copy-start
  2.2 0.0 copy-start.1
  2.2 0.0 copy-start.2
  2.2 1.5 %copy.12.q_ref = bf16[48,12,512]{2,1,0:T(8,128)(2,1)S(1)} copy(bf16[48,12,512]{2,0,1:T(8,128)(2,1)} %param.7) | data formatting | bytes 1179648 | tf_op args[0]
  3.6 0.0 copy-done.10
  3.6 0.3 copy.13.k_ref
  4.0 0.3 copy.14.v_ref
  4.3 0.0 copy-done
  4.4 0.0 copy-done.1
  4.4 0.0 copy-done.2
  4.4 4.9 %shard_map.110 = (s32[4,16]{1,0:T(4,128)S(1)}, bf16[16,192,384]{2,1,0:T(8,128)(2,1)}, bf16[16,192,128]{2,1,0:T(8,128)(2,1)S(1)}, bf16[4,176,384]{2,1,0:T(8,128)(...) custom-call(s32[48]{0:T(128)S(1)} %copy-done.1, ...), custom_call_target="tpu_custom_call" | custom-call | flops 4000000000 | bytes 10000000 | tf_op jit(solution)/shard_map/pallas_call | solution.py:355
  9.3 0.9 copy-done.6
  10.1 5.4 %collective-permute-start = (bf16[4,176,384]{2,1,0:T(8,128)(2,1)S(1)}, bf16[4,176,384]{2,1,0:T(8,128)(2,1)S(1)}, u32[]{:S(2)}, u32[]{:S(2)}) collective-permute-start(bf16[4,176,384]{2,1,0:T(8,128)(2,1)S(1)} %get-tuple-element.27), channel_id=1, source_target_pairs={{0,15},{1,0},{2,1},{3,2},{4,3},{5,4},{6,5},{7,6},{8,7},{9,8},{10,9... | collective-permute-start | bytes 1622024 | tf_op jit(solution)/shard_map/ppermute | solution.py:34
  15.6 0.0 collective-permute-start.1
  15.6 6.9 %collective-permute-done.rw_ref = bf16[4,176,384]{2,1,0:T(8,128)(2,1)S(1)} collective-permute-done((bf16[4,176,384]{2,1,0:T(8,128)(2,1)S(1)}, bf16[4,176,384]{2,1,0:T(8,128)(2,1)S(1)}, u32[]{:S(2)}, u32[]{:S(2)}) %collective-permute-start) | collective-permute-done | bytes 540704 | tf_op jit(solution)/shard_map/ppermute | solution.py:34
  22.5 4.6 %collective-permute-done.1.re_ref = bf16[4,176,384]{2,1,0:T(8,128)(2,1)S(1)} collective-permute-done((bf16[4,176,384]{2,1,0:T(8,128)(2,1)S(1)}, bf16[4,176,384]{2,1,0:T(8,128)(2,1)S(1)}, u32[]{:S(2)}, u32[]{:S(2)}) %collective-permute-start.1) | collective-permute-done | bytes 540704 | tf_op jit(solution)/shard_map/ppermute | solution.py:34
  27.1 22.6 %shard_map.111 = (bf16[16,144,576]{2,1,0:T(8,128)(2,1)}, bf16[16,144,384]{2,1,0:T(8,128)(2,1)S(1)}, bf16[16,192,128]{2,1,0:T(8,128)(2,1)S(1)}, bf16[4,176,128]{2,1,0:T(8,128)(2,1)S(1)}, bf16[4,176,128]{2,1,0:T(8,128)(2,1)S(1)}) custom-call(s32[4,16]{1,0:T(4,128)S(1)} %get-tuple-element.25.tab, bf16[16,192,384]{2,1,0:T(8,128)(2,1)} %get-tuple-element.26.xf_ref, ...), custom_call_target="tpu_custom_call" | custom-call | flops 6000000000 | bytes 10000000 | tf_op jit(solution)/shard_map/pallas_call | solution.py:376
  49.7 0.9 copy-done.4
  50.6 1.3 copy-done.8
  51.8 0.0 collective-permute-start.2
  51.8 4.4 %collective-permute-start.3 = (bf16[4,176,128]{2,1,0:T(8,128)(2,1)S(1)}, bf16[4,176,128]{2,1,0:T(8,128)(2,1)S(1)}, u32[]{:S(2)}, u32[]{:S(2)}) collective-permute-start(bf16[4,176,128]{2,1,0:T(8,128)(2,1)S(1)} %get-tuple-element.31), channel_id=1, source_target_pairs={{0,15},{1,0},{2,1},{3,2},{4,3},{5,4},{6,5},{7,6},{8,7},{9,8},{10,9... | collective-permute-start | bytes 540680 | tf_op jit(solution)/shard_map/ppermute | solution.py:34
  56.3 3.3 %collective-permute-done.2.rw_ref = bf16[4,176,128]{2,1,0:T(8,128)(2,1)S(1)} collective-permute-done((bf16[4,176,128]{2,1,0:T(8,128)(2,1)S(1)}, bf16[4,176,128]{2,1,0:T(8,128)(2,1)S(1)}, u32[]{:S(2)}, u32[]{:S(2)}) %collective-permute-start.2) | collective-permute-done | bytes 180256 | tf_op jit(solution)/shard_map/ppermute | solution.py:34
  59.5 0.0 collective-permute-done.3.re_ref
  59.6 1.1 copy-done.5
  60.7 3.3 %shard_map.112 = (bf16[48,12,512]{2,1,0:T(8,128)(2,1)S(1)}, bf16[512,512]{1,0:T(8,128)(2,1)S(1)}) custom-call(s32[4,16]{1,0:T(4,128)S(1)} %get-tuple-element.25.tab, bf16[16,192,128]{2,1,0:T(8,128)(2,1)S(1)} %copy-done.5, bf16[4,176,128]{2,1,0:T(8,128)(2,1)S(1)} %collective-permute-done.2.rw_ref, bf16[4,176,128]{2,1,0:T(8,128)(2,1)S(1)} %collective-permute-done.3.re_ref, ...), custom_call_target="tpu_custom_call" | custom-call | flops 2000000000 | bytes 4000000 | tf_op jit(solution)/shard_map/pallas_call | solution.py:414
  64.1 0.1 collective-permute-start.8
  64.1 1.5 %collective-permute-done.8 = bf16[256,512]{1,0:T(8,128)(2,1)S(1)} collective-permute-done((bf16[256,512]{1,0:T(8,128)(2,1)S(1)}, bf16[256,512]{1,0:T(8,128)(2,1)S(1)}, u32[]{:S(2)}, u32[]{:S(2)}) %collective-permute-start.8) | collective-permute-done | bytes 262176 | tf_op jit(solution)/shard_map/ppermute | solution.py:39
  65.7 0.1 add_convert_fusion
  65.8 0.1 collective-permute-start.9
  65.9 5.5 %collective-permute-done.9 = bf16[128,512]{1,0:T(8,128)(2,1)S(1)} collective-permute-done((bf16[128,512]{1,0:T(8,128)(2,1)S(1)}, bf16[128,512]{1,0:T(8,128)(2,1)S(1)}, u32[]{:S(2)}, u32[]{:S(2)}) %collective-permute-start.9) | collective-permute-done | bytes 131104 | tf_op jit(solution)/shard_map/ppermute | solution.py:39
  71.4 0.1 add_convert_fusion.1
  71.5 0.1 collective-permute-start.10
  71.6 4.2 %collective-permute-done.10 = bf16[64,512]{1,0:T(8,128)(2,1)S(1)} collective-permute-done((bf16[64,512]{1,0:T(8,128)(2,1)S(1)}, bf16[64,512]{1,0:T(8,128)(2,1)S(1)}, u32[]{:S(2)}, u32[]{:S(2)}) %collective-permute-start.10) | collective-permute-done | bytes 65568 | tf_op jit(solution)/shard_map/ppermute | solution.py:39
  75.8 2.0 %collective-permute-start.11 = (bf16[32,512]{1,0:T(8,128)(2,1)S(1)}, bf16[32,512]{1,0:T(8,128)(2,1)S(1)}, u32[]{:S(2)}, u32[]{:S(2)}) collective-permute-start(bf16[32,512]{1,0:T(8,128)(2,1)S(1)} %broadcast_select_fusion.3), channel_id=1, source_target_pairs={{0,8},{1,9},{2,10},{3,11},{4,12},{5,13},{6,14},{7,15},{8,0},{9,1},... | collective-permute-start | bytes 98312 | tf_op jit(solution)/shard_map/ppermute | solution.py:39
  77.9 0.7 collective-permute-start.4
  78.6 0.0 collective-permute-start.5
  78.6 2.1 %collective-permute-done.11 = bf16[32,512]{1,0:T(8,128)(2,1)S(1)} collective-permute-done((bf16[32,512]{1,0:T(8,128)(2,1)S(1)}, bf16[32,512]{1,0:T(8,128)(2,1)S(1)}, u32[]{:S(2)}, u32[]{:S(2)}) %collective-permute-start.11) | collective-permute-done | bytes 32800 | tf_op jit(solution)/shard_map/ppermute | solution.py:39
  80.7 2.0 %collective-permute-start.12 = (bf16[32,512]{1,0:T(8,128)(2,1)S(1)}, bf16[32,512]{1,0:T(8,128)(2,1)S(1)}, u32[]{:S(2)}, u32[]{:S(2)}) collective-permute-start(bf16[32,512]{1,0:T(8,128)(2,1)S(1)} %add_convert_fusion.3), channel_id=1, source_target_pairs={{0,8},{1,9},{2,10},{3,11},{4,12},{5,13},{6,14},{7,15},{8,0},{9,1},... | collective-permute-start | bytes 98312 | tf_op jit(solution)/shard_map/ppermute | solution.py:39
  82.8 0.0 collective-permute-done.4.rw_ref
  82.8 3.5 %collective-permute-done.5.re_ref = bf16[4,176,128]{2,1,0:T(8,128)(2,1)S(1)} collective-permute-done((bf16[4,176,128]{2,1,0:T(8,128)(2,1)S(1)}, bf16[4,176,128]{2,1,0:T(8,128)(2,1)S(1)}, u32[]{:S(2)}, u32[]{:S(2)}) %collective-permute-start.5) | collective-permute-done | bytes 180256 | tf_op jit(solution)/shard_map/ppermute | solution.py:34
  86.3 1.5 %copy-done.9 = bf16[16,144,384]{2,1,0:T(8,128)(2,1)S(1)} copy-done((bf16[16,144,384]{2,1,0:T(8,128)(2,1)S(1)}, bf16[16,144,384]{2,1,0:T(8,128)(2,1)}, u32[]{:S(2)}) %copy-start.9) | copy-done | bytes 1769496
  87.8 23.1 %shard_map.113 = (bf16[16,192,384]{2,1,0:T(8,128)(2,1)}, bf16[4,176,384]{2,1,0:T(8,128)(2,1)S(1)}, bf16[4,176,384]{2,1,0:T(8,128)(2,1)S(1)}) custom-call(s32[4,16]{1,0:T(4,128)S(1)} %get-tuple-element.25.tab, bf16[16,144,576]{2,1,0:T(8,128)(2,1)} %get-tuple-element.33.probs_ref, bf16[16,144,384]{2,1,0:T(8,128)(2,1)S(1)} %copy-done.9, ...), custom_call_target="tpu_custom_call" | custom-call | flops 8000000000 | bytes 10000000 | tf_op jit(solution)/shard_map/pallas_call | solution.py:396
  110.9 0.0 collective-permute-start.6
  110.9 4.4 %collective-permute-start.7 = (bf16[4,176,384]{2,1,0:T(8,128)(2,1)S(1)}, bf16[4,176,384]{2,1,0:T(8,128)(2,1)S(1)}, u32[]{:S(2)}, u32[]{:S(2)}) collective-permute-start(bf16[4,176,384]{2,1,0:T(8,128)(2,1)S(1)} %get-tuple-element.40), channel_id=1, source_target_pairs={{0,15},{1,0},{2,1},{3,2},{4,3},{5,4},{6,5},{7,6},{8,7},{9,8},{10,9... | collective-permute-start | bytes 1622024 | tf_op jit(solution)/shard_map/ppermute | solution.py:34
  115.3 0.0 collective-permute-done.12
  115.3 0.1 collective-permute-start.13
  115.4 7.5 %collective-permute-done.13 = bf16[64,512]{1,0:T(8,128)(2,1)S(1)} collective-permute-done((bf16[64,512]{1,0:T(8,128)(2,1)S(1)}, bf16[64,512]{1,0:T(8,128)(2,1)S(1)}, u32[]{:S(2)}, u32[]{:S(2)}) %collective-permute-start.13) | collective-permute-done | bytes 65568 | tf_op jit(solution)/shard_map/ppermute | solution.py:39
  122.9 0.4 collective-permute-start.14
  123.3 5.4 %collective-permute-done.14 = bf16[128,512]{1,0:T(8,128)(2,1)S(1)} collective-permute-done((bf16[128,512]{1,0:T(8,128)(2,1)S(1)}, bf16[128,512]{1,0:T(8,128)(2,1)S(1)}, u32[]{:S(2)}, u32[]{:S(2)}) %collective-permute-start.14) | collective-permute-done | bytes 131104 | tf_op jit(solution)/shard_map/ppermute | solution.py:39
  128.7 0.1 maximum_select_fusion.1
  128.8 0.1 collective-permute-start.15
  128.9 1.1 copy.17
  130.0 0.0 collective-permute-done.6.rw_ref
  130.0 0.0 collective-permute-done.7.re_ref
  130.0 1.7 %copy-done.3 = bf16[16,192,384]{2,1,0:T(8,128)(2,1)S(1)} copy-done((bf16[16,192,384]{2,1,0:T(8,128)(2,1)S(1)}, bf16[16,192,384]{2,1,0:T(8,128)(2,1)}, u32[]{:S(2)}) %copy-start.3) | copy-done | bytes 2359320
  131.7 3.0 %shard_map.114 = (bf16[48,12,512]{2,1,0:T(8,128)(2,1)S(1)}, bf16[48,12,512]{2,1,0:T(8,128)(2,1)S(1)}, bf16[48,12,512]{2,1,0:T(8,128)(2,1)S(1)}) custom-call(s32[4,16]{1,0:T(4,128)S(1)} %get-tuple-element.25.tab, bf16[16,192,384]{2,1,0:T(8,128)(2,1)S(1)} %copy-done.3, bf16[4,176,384]{2,1,0:T(8,128)(2,1)S(1)} %collective-permute-done.6.rw_ref, ...), custom_call_target="tpu_custom_call" | custom-call | flops 2000000000 | bytes 6000000 | tf_op jit(solution)/shard_map/pallas_call | solution.py:424
  134.7 1.1 copy.18
  135.9 1.1 copy.19
  137.0 1.1 copy.20
  138.2 0.0 collective-permute-done.15
  138.2 1.2 fusion
  (17 shorter events, 0.2 us)
Async XLA Ops:
  0.6 3.0 %copy-start.10 = (bf16[48,12,512]{2,0,1:T(8,128)(2,1)S(1)}, bf16[48,12,512]{2,0,1:T(8,128)(2,1)}, u32[]{:S(2)}) copy-start(bf16[48,12,512]{2,0,1:T(8,128)(2,1)} %param.8) | copy-start | bytes 1769476
  0.6 3.4 %copy-start.11 = (bf16[48,12,512]{2,0,1:T(8,128)(2,1)S(1)}, bf16[48,12,512]{2,0,1:T(8,128)(2,1)}, u32[]{:S(2)}) copy-start(bf16[48,12,512]{2,0,1:T(8,128)(2,1)} %param.9) | copy-start | bytes 1769476
  2.1 2.2 %copy-start = (bf16[512,512]{1,0:T(8,128)(2,1)S(1)}, bf16[512,512]{1,0:T(8,128)(2,1)}, u32[]{:S(2)}) copy-start(bf16[512,512]{1,0:T(8,128)(2,1)} %w_ref.3) | copy-start | bytes 1572868
  2.2 2.2 %copy-start.1 = (s32[48]{0:T(128)S(1)}, s32[48]{0:T(128)}, u32[]{:S(2)}) copy-start(s32[48]{0:T(128)} %lat.1) | copy-start | bytes 580
  2.2 2.2 %copy-start.2 = (s32[48]{0:T(128)S(1)}, s32[48]{0:T(128)}, u32[]{:S(2)}) copy-start(s32[48]{0:T(128)} %lon.1) | copy-start | bytes 580
  9.2 0.9 copy-start.6
  10.1 12.3 %collective-permute-start = (bf16[4,176,384]{2,1,0:T(8,128)(2,1)S(1)}, bf16[4,176,384]{2,1,0:T(8,128)(2,1)S(1)}, u32[]{:S(2)}, u32[]{:S(2)}) collective-permute-start(bf16[4,176,384]{2,1,0:T(8,128)(2,1)S(1)} %get-tuple-element.27), channel_id=1, source_target_pairs={{0,15},{1,0},{2,1},{3,2},{4,3},{5,4},{6,5},{7,6},{8,7},{9,8},{10,9... | collective-permute-start | bytes 1622024 | tf_op jit(solution)/shard_map/ppermute | solution.py:34
  15.6 11.5 %collective-permute-start.1 = (bf16[4,176,384]{2,1,0:T(8,128)(2,1)S(1)}, bf16[4,176,384]{2,1,0:T(8,128)(2,1)S(1)}, u32[]{:S(2)}, u32[]{:S(2)}) collective-permute-start(bf16[4,176,384]{2,1,0:T(8,128)(2,1)S(1)} %get-tuple-element.28), channel_id=1, source_target_pairs={{0,1},{1,2},{2,3},{3,4},{4,5},{5,6},{6,7},{7,8},{8,9},{9,10},{10,1... | collective-permute-start | bytes 1622024 | tf_op jit(solution)/shard_map/ppermute | solution.py:34
  49.7 0.9 copy-start.4
  50.6 1.3 copy-start.8
  51.8 7.7 %collective-permute-start.2 = (bf16[4,176,128]{2,1,0:T(8,128)(2,1)S(1)}, bf16[4,176,128]{2,1,0:T(8,128)(2,1)S(1)}, u32[]{:S(2)}, u32[]{:S(2)}) collective-permute-start(bf16[4,176,128]{2,1,0:T(8,128)(2,1)S(1)} %get-tuple-element.30), channel_id=1, source_target_pairs={{0,1},{1,2},{2,3},{3,4},{4,5},{5,6},{6,7},{7,8},{8,9},{9,10},{10,1... | collective-permute-start | bytes 540680 | tf_op jit(solution)/shard_map/ppermute | solution.py:34
  51.8 7.7 %collective-permute-start.3 = (bf16[4,176,128]{2,1,0:T(8,128)(2,1)S(1)}, bf16[4,176,128]{2,1,0:T(8,128)(2,1)S(1)}, u32[]{:S(2)}, u32[]{:S(2)}) collective-permute-start(bf16[4,176,128]{2,1,0:T(8,128)(2,1)S(1)} %get-tuple-element.31), channel_id=1, source_target_pairs={{0,15},{1,0},{2,1},{3,2},{4,3},{5,4},{6,5},{7,6},{8,7},{9,8},{10,9... | collective-permute-start | bytes 540680 | tf_op jit(solution)/shard_map/ppermute | solution.py:34
  59.5 1.1 copy-start.5
  64.0 22.3 %copy-start.7 = (bf16[16,192,128]{2,1,0:T(8,128)(2,1)S(1)}, bf16[16,192,128]{2,1,0:T(8,128)(2,1)}, u32[]{:S(2)}) copy-start(bf16[16,192,128]{2,1,0:T(8,128)(2,1)} %copy-done.6) | copy-start | bytes 2359300
  64.1 1.6 %collective-permute-start.8 = (bf16[256,512]{1,0:T(8,128)(2,1)S(1)}, bf16[256,512]{1,0:T(8,128)(2,1)S(1)}, u32[]{:S(2)}, u32[]{:S(2)}) collective-permute-start(bf16[256,512]{1,0:T(8,128)(2,1)S(1)} %broadcast_select_fusion), channel_id=1, source_target_pairs={{0,1},{1,0},{2,3},{3,2},{4,5},{5,4},{6,7},{7,6},{8,9},{9,8},{10,11... | collective-permute-start | bytes 786440 | tf_op jit(solution)/shard_map/ppermute | solution.py:39
  65.8 5.6 %collective-permute-start.9 = (bf16[128,512]{1,0:T(8,128)(2,1)S(1)}, bf16[128,512]{1,0:T(8,128)(2,1)S(1)}, u32[]{:S(2)}, u32[]{:S(2)}) collective-permute-start(bf16[128,512]{1,0:T(8,128)(2,1)S(1)} %broadcast_select_fusion.1), channel_id=1, source_target_pairs={{0,2},{1,3},{2,0},{3,1},{4,6},{5,7},{6,4},{7,5},{8,10},{9,11},{10,... | collective-permute-start | bytes 393224 | tf_op jit(solution)/shard_map/ppermute | solution.py:39
  71.5 4.3 %collective-permute-start.10 = (bf16[64,512]{1,0:T(8,128)(2,1)S(1)}, bf16[64,512]{1,0:T(8,128)(2,1)S(1)}, u32[]{:S(2)}, u32[]{:S(2)}) collective-permute-start(bf16[64,512]{1,0:T(8,128)(2,1)S(1)} %broadcast_select_fusion.2), channel_id=1, source_target_pairs={{0,4},{1,5},{2,6},{3,7},{4,0},{5,1},{6,2},{7,3},{8,12},{9,13},{10,... | collective-permute-start | bytes 196616 | tf_op jit(solution)/shard_map/ppermute | solution.py:39
  75.8 4.9 %collective-permute-start.11 = (bf16[32,512]{1,0:T(8,128)(2,1)S(1)}, bf16[32,512]{1,0:T(8,128)(2,1)S(1)}, u32[]{:S(2)}, u32[]{:S(2)}) collective-permute-start(bf16[32,512]{1,0:T(8,128)(2,1)S(1)} %broadcast_select_fusion.3), channel_id=1, source_target_pairs={{0,8},{1,9},{2,10},{3,11},{4,12},{5,13},{6,14},{7,15},{8,0},{9,1},... | collective-permute-start | bytes 98312 | tf_op jit(solution)/shard_map/ppermute | solution.py:39
  77.9 4.9 %collective-permute-start.4 = (bf16[4,176,128]{2,1,0:T(8,128)(2,1)S(1)}, bf16[4,176,128]{2,1,0:T(8,128)(2,1)S(1)}, u32[]{:S(2)}, u32[]{:S(2)}) collective-permute-start(bf16[4,176,128]{2,1,0:T(8,128)(2,1)S(1)} %get-tuple-element.36), channel_id=1, source_target_pairs={{0,15},{1,0},{2,1},{3,2},{4,3},{5,4},{6,5},{7,6},{8,7},{9,8},{10,9... | collective-permute-start | bytes 540680 | tf_op jit(solution)/shard_map/ppermute | solution.py:34
  78.6 7.7 %collective-permute-start.5 = (bf16[4,176,128]{2,1,0:T(8,128)(2,1)S(1)}, bf16[4,176,128]{2,1,0:T(8,128)(2,1)S(1)}, u32[]{:S(2)}, u32[]{:S(2)}) collective-permute-start(bf16[4,176,128]{2,1,0:T(8,128)(2,1)S(1)} %get-tuple-element.37), channel_id=1, source_target_pairs={{0,1},{1,2},{2,3},{3,4},{4,5},{5,6},{6,7},{7,8},{8,9},{9,10},{10,1... | collective-permute-start | bytes 540680 | tf_op jit(solution)/shard_map/ppermute | solution.py:34
  80.7 34.6 %collective-permute-start.12 = (bf16[32,512]{1,0:T(8,128)(2,1)S(1)}, bf16[32,512]{1,0:T(8,128)(2,1)S(1)}, u32[]{:S(2)}, u32[]{:S(2)}) collective-permute-start(bf16[32,512]{1,0:T(8,128)(2,1)S(1)} %add_convert_fusion.3), channel_id=1, source_target_pairs={{0,8},{1,9},{2,10},{3,11},{4,12},{5,13},{6,14},{7,15},{8,0},{9,1},... | collective-permute-start | bytes 98312 | tf_op jit(solution)/shard_map/ppermute | solution.py:39
  86.3 1.5 %copy-start.9 = (bf16[16,144,384]{2,1,0:T(8,128)(2,1)S(1)}, bf16[16,144,384]{2,1,0:T(8,128)(2,1)}, u32[]{:S(2)}) copy-start(bf16[16,144,384]{2,1,0:T(8,128)(2,1)} %copy-done.8) | copy-start | bytes 5308420
  110.9 19.1 %collective-permute-start.6 = (bf16[4,176,384]{2,1,0:T(8,128)(2,1)S(1)}, bf16[4,176,384]{2,1,0:T(8,128)(2,1)S(1)}, u32[]{:S(2)}, u32[]{:S(2)}) collective-permute-start(bf16[4,176,384]{2,1,0:T(8,128)(2,1)S(1)} %get-tuple-element.39), channel_id=1, source_target_pairs={{0,1},{1,2},{2,3},{3,4},{4,5},{5,6},{6,7},{7,8},{8,9},{9,10},{10,1... | collective-permute-start | bytes 1622024 | tf_op jit(solution)/shard_map/ppermute | solution.py:34
  110.9 19.1 %collective-permute-start.7 = (bf16[4,176,384]{2,1,0:T(8,128)(2,1)S(1)}, bf16[4,176,384]{2,1,0:T(8,128)(2,1)S(1)}, u32[]{:S(2)}, u32[]{:S(2)}) collective-permute-start(bf16[4,176,384]{2,1,0:T(8,128)(2,1)S(1)} %get-tuple-element.40), channel_id=1, source_target_pairs={{0,15},{1,0},{2,1},{3,2},{4,3},{5,4},{6,5},{7,6},{8,7},{9,8},{10,9... | collective-permute-start | bytes 1622024 | tf_op jit(solution)/shard_map/ppermute | solution.py:34
  115.3 7.6 %collective-permute-start.13 = (bf16[64,512]{1,0:T(8,128)(2,1)S(1)}, bf16[64,512]{1,0:T(8,128)(2,1)S(1)}, u32[]{:S(2)}, u32[]{:S(2)}) collective-permute-start(bf16[64,512]{1,0:T(8,128)(2,1)S(1)} %maximum_select_fusion.3), channel_id=1, source_target_pairs={{0,4},{1,5},{2,6},{3,7},{4,0},{5,1},{6,2},{7,3},{8,12},{9,13},{10,... | collective-permute-start | bytes 196616 | tf_op jit(solution)/shard_map/ppermute | solution.py:39
  122.9 5.8 %collective-permute-start.14 = (bf16[128,512]{1,0:T(8,128)(2,1)S(1)}, bf16[128,512]{1,0:T(8,128)(2,1)S(1)}, u32[]{:S(2)}, u32[]{:S(2)}) collective-permute-start(bf16[128,512]{1,0:T(8,128)(2,1)S(1)} %maximum_select_fusion.2), channel_id=1, source_target_pairs={{0,2},{1,3},{2,0},{3,1},{4,6},{5,7},{6,4},{7,5},{8,10},{9,11},{10,... | collective-permute-start | bytes 393224 | tf_op jit(solution)/shard_map/ppermute | solution.py:39
  128.8 9.4 %collective-permute-start.15 = (bf16[256,512]{1,0:T(8,128)(2,1)S(1)}, bf16[256,512]{1,0:T(8,128)(2,1)S(1)}, u32[]{:S(2)}, u32[]{:S(2)}) collective-permute-start(bf16[256,512]{1,0:T(8,128)(2,1)S(1)} %maximum_select_fusion.1), channel_id=1, source_target_pairs={{0,1},{1,0},{2,3},{3,2},{4,5},{5,4},{6,7},{7,6},{8,9},{9,8},{10,11... | collective-permute-start | bytes 786440 | tf_op jit(solution)/shard_map/ppermute | solution.py:39
  130.0 1.7 %copy-start.3 = (bf16[16,192,384]{2,1,0:T(8,128)(2,1)S(1)}, bf16[16,192,384]{2,1,0:T(8,128)(2,1)}, u32[]{:S(2)}) copy-start(bf16[16,192,384]{2,1,0:T(8,128)(2,1)} %get-tuple-element.38.own_ref) | copy-start | bytes 7077892

commit v2 on v1

v2 whole, which is shorter than its diff:
```python
import functools

import jax
import jax.numpy as jnp
from jax import lax
from jax.experimental import pallas as pl
from jax.experimental.pallas import tpu as pltpu
from jax.sharding import PartitionSpec as P

HD = 32
WIN = 12
PAD = 16
LANES = 128
GH = LANES // HD
SUB = WIN * WIN
SLOTS = 14
BUF = 176
OWN = WIN * PAD
BF = jnp.bfloat16
F32 = jnp.float32
MIB = 1024 * 1024
NN = (((1,), (0,)), ((), ()))
NT = (((1,), (1,)), ((), ()))
TN = (((0,), (0,)), ((), ()))


def dot(a, b, dims=NN):
    return lax.dot_general(a, b, dims, preferred_element_type=F32)


def passed_along(value, axis, steps):
    count = lax.axis_size(axis)
    pairs = [(source, (source + steps) % count) for source in range(count)]
    return lax.ppermute(value, axis, pairs)


def swapped(value, axis, bit):
    count = lax.axis_size(axis)
    return lax.ppermute(value, axis, [(source, source ^ bit) for source in range(count)])


def sub_layout(lat, lon, sub):
    base = 2 * WIN * (sub // 2)
    first = lat[base]
    leading = lat[base + WIN - 1] == first
    trailing = lat[base + WIN] == lat[base + 2 * WIN - 1]
    count = jnp.int32(0)
    for i in range(WIN):
        count += (lat[base + i] == first).astype(jnp.int32)
    start = jnp.where(leading, 0, jnp.where(trailing, WIN, count))
    if sub % 2 == 0:
        off = lon[base + start]
        return jnp.int32(WIN), off, off, lambda i: base + start + i
    row = lambda i: base + i + jnp.where(i >= start, WIN, 0)
    head = lat[row(0)]
    split = jnp.int32(0)
    for i in range(WIN):
        split += (lat[row(i)] == head).astype(jnp.int32)
    return split, lon[row(0)], lon[row(WIN - 1)], row


def west_groups(off):
    total = jnp.zeros_like(off)
    for g in range(4):
        total += (off <= 10 - 3 * g).astype(jnp.int32)
    return total


def column(count):
    return lax.broadcasted_iota(jnp.int32, (count, 1), 0)


def one_hot(target, width):
    lanes = lax.broadcasted_iota(jnp.int32, (target.shape[0], width), 1)
    return jnp.where(lanes == target, 1.0, 0.0).astype(BF)


def split_div(n, by):
    q = (n * ((1 << 20) // by + 1)) >> 20
    return q, n - q * by


def slot_places(split, off1, off2):
    i, u = split_div(column(BUF), SLOTS)
    off = jnp.where(i < split, off1, off2)
    real = i < WIN
    nw = west_groups(off)
    gw = jnp.zeros_like(off)
    ge = jnp.zeros_like(off)
    rest = WIN - off
    for k in range(1, 4):
        gw += (u >= k * off).astype(jnp.int32)
        ge += (u >= k * rest).astype(jnp.int32)
    west = (real & (u < nw * off), gw, u - gw * off)
    east = (real & (u < (4 - nw) * rest), nw + ge, off + u - ge * rest)
    return i, off, west, east


def own_rows(x, pad_ref, at):
    x = jnp.swapaxes(x, 0, 1)
    pad_ref[at, :, 0:WIN, :] = x
    pad_ref[at, :, WIN:PAD, :] = jnp.zeros((x.shape[0], PAD - WIN, x.shape[2]), BF)


def send_pick(split, off1, off2):
    i, off, west, east = slot_places(split, off1, off2)
    targets = [
        jnp.where(valid, group * OWN + i * PAD + col, -1) for valid, group, col in (west, east)
    ]
    return one_hot(jnp.concatenate(targets, axis=0), 4 * OWN)


def pack_kernel(lat, lon, q_ref, k_ref, v_ref, tab_ref, own_ref, west_ref, east_ref, pad_ref):
    rows = q_ref.shape[1]
    for a, ref in enumerate((q_ref, k_ref, v_ref)):
        own_rows(ref[...], pad_ref, a)
    for sub in range(rows // WIN):
        split, off1, off2, row = sub_layout(lat, lon, sub)
        tab_ref[sub, 0] = split
        tab_ref[sub, 1] = off1
        tab_ref[sub, 2] = off2
        for i in range(WIN):
            r = row(i)
            tab_ref[sub, 4 + i] = r
            for g in range(4):
                for a in range(3):
                    own_ref[sub * 4 + g, i * PAD : (i + 1) * PAD, a * LANES : (a + 1) * LANES] = (
                        pad_ref[a, r, :, g * LANES : (g + 1) * LANES]
                    )
        own = own_ref[sub * 4 : sub * 4 + 4].reshape(4 * OWN, 3 * LANES)
        sent = dot(send_pick(split, off1, off2), own).astype(BF)
        west_ref[sub] = sent[0:BUF]
        east_ref[sub] = sent[BUF:]


def pack_grad_kernel(tab, cot_ref, w_ref, own_ref, west_ref, east_ref, pad_ref):
    cols, rows, channels = cot_ref.shape
    grad = dot(cot_ref[...].reshape(cols * rows, channels), w_ref[...], NT).astype(BF)
    own_rows(grad.reshape(cols, rows, channels), pad_ref, 0)
    for sub in range(rows // WIN):
        for i in range(WIN):
            r = tab[sub, 4 + i]
            for g in range(4):
                own_ref[sub * 4 + g, i * PAD : (i + 1) * PAD, :] = (
                    pad_ref[0, r, :, g * LANES : (g + 1) * LANES]
                )
        own = own_ref[sub * 4 : sub * 4 + 4].reshape(4 * OWN, LANES)
        sent = dot(send_pick(tab[sub, 0], tab[sub, 1], tab[sub, 2]), own).astype(BF)
        west_ref[sub] = sent[0:BUF]
        east_ref[sub] = sent[BUF:]


def prepare_kernel(tab, own_ref, win_ref, pick_ref, fw_ref, fe_ref, move_ref, hw_ref, he_ref):
    sub = pl.program_id(0)
    split, off1, off2 = tab[sub, 0], tab[sub, 1], tab[sub, 2]
    i, p = split_div(column(SUB), WIN)
    off = jnp.where(i < split, off1, off2)
    nw = west_groups(off)
    rest = WIN - off
    c = off + p - jnp.where(p >= rest, WIN, 0)
    n = column(OWN)
    j, k = n >> 4, n & (PAD - 1)
    off_o = jnp.where(j < split, off1, off2)
    nw_o = west_groups(off_o)
    before = k < off_o
    real = k < WIN
    p_o = k - off_o + jnp.where(before, WIN, 0)
    _, off_s, west, east = slot_places(split, off1, off2)
    i_s = split_div(column(BUF), SLOTS)[0]
    for g in range(4):
        is_west = g < nw
        own = (is_west & (p < rest)) | ((~is_west) & (p >= rest))
        pick = one_hot(jnp.where(own, i * PAD + c, -1), OWN)
        win_ref[g] = dot(pick, own_ref[g]).astype(BF)
        pick_ref[g] = pick
        t_west = jnp.where(is_west & (p >= rest), i * SLOTS + g * off + (p - rest), -1)
        t_east = jnp.where((~is_west) & (p < rest), i * SLOTS + (g - nw) * rest + p, -1)
        fw_ref[g] = one_hot(t_west, BUF)
        fe_ref[g] = one_hot(t_east, BUF)
        t_west = jnp.where(west[0] & (west[1] == g), i_s * WIN + (WIN - off_s) + west[2], -1)
        t_east = jnp.where(east[0] & (east[1] == g), i_s * WIN + east[2] - off_s, -1)
        is_west = g < nw_o
        local = ((is_west & (~before)) | ((~is_west) & before)) & real
        move_ref[g, 0:BUF] = one_hot(t_west, SUB)
        move_ref[g, BUF : 2 * BUF] = one_hot(t_east, SUB)
        move_ref[g, 2 * BUF :] = one_hot(jnp.where(local, j * WIN + p_o, -1), SUB)
        t_west = jnp.where(is_west & before, j * SLOTS + g * off_o + k, -1)
        t_east = jnp.where(
            (~is_west) & (~before) & real, j * SLOTS + (g - nw_o) * (WIN - off_o) + (k - off_o), -1
        )
        hw_ref[g] = one_hot(t_west, BUF)
        he_ref[g] = one_hot(t_east, BUF)


def by_head(x):
    lane = lax.broadcasted_iota(jnp.int32, (1, LANES), 1) // HD
    return jnp.concatenate(
        [x * jnp.where(lane == h, 1.0, 0.0).astype(BF) for h in range(GH)], axis=0
    )


def diagonal(full):
    return jnp.concatenate(
        [full[h * HD : (h + 1) * HD, h * SUB : (h + 1) * SUB] for h in range(GH)], axis=0
    )


def forward_kernel(
    tab, win_ref, fw_ref, fe_ref, move_ref, rw_ref, re_ref,
    probs_ref, cells_ref, own_ref, bw_ref, be_ref,
):
    sub = pl.program_id(0)
    edge = tab[sub, 0] * WIN
    lane = lax.broadcasted_iota(jnp.int32, (1, GH * SUB), 1)
    cell = lane - split_div(lane, SUB)[0] * SUB
    in_first = jnp.where(cell < edge, 1, 0)
    key_first = jnp.where(column(SUB) < edge, 1, 0)
    rate = float(HD) ** -0.5 * 1.4426950408889634
    far = dot(fw_ref[...].reshape(4 * SUB, BUF), rw_ref[0])
    far += dot(fe_ref[...].reshape(4 * SUB, BUF), re_ref[0])
    for g in range(4):
        cells_ref[g] = (win_ref[g].astype(F32) + far[g * SUB : (g + 1) * SUB]).astype(BF)
    scores = [
        dot(cells_ref[g, :, LANES : 2 * LANES], by_head(cells_ref[g, :, 0:LANES]), NT)
        for g in range(4)
    ]
    for g in range(4):
        x = jnp.where(key_first == in_first, scores[g], -1e30)
        power = jnp.exp2((x - jnp.max(x, axis=0, keepdims=True)) * rate)
        probs_ref[g] = (power * (1.0 / jnp.sum(power, axis=0, keepdims=True))).astype(BF)
    full = [dot(cells_ref[g, :, 2 * LANES :], probs_ref[g], TN) for g in range(4)]
    att = [diagonal(x).astype(BF) for x in full]
    moved = [dot(move_ref[g], att[g], NT) for g in range(4)]
    for g in range(4):
        own_ref[g] = moved[g][2 * BUF :].astype(BF)
    back = (moved[0] + moved[1]) + (moved[2] + moved[3])
    bw_ref[0] = back[0:BUF].astype(BF)
    be_ref[0] = back[BUF : 2 * BUF].astype(BF)


def backward_kernel(
    probs_ref, cells_ref, og_ref, pick_ref, fw_ref, fe_ref, move_ref, rw_ref, re_ref,
    own_ref, bw_ref, be_ref,
):
    grads = []
    far = dot(fw_ref[...].reshape(4 * SUB, BUF), rw_ref[0])
    far += dot(fe_ref[...].reshape(4 * SUB, BUF), re_ref[0])
    for g in range(4):
        grads.append(by_head((dot(pick_ref[g], og_ref[g]) + far[g * SUB : (g + 1) * SUB]).astype(BF)))
    grad_probs = [dot(cells_ref[g, :, 2 * LANES :], grads[g], NT) for g in range(4)]
    grad_v = [dot(probs_ref[g], grads[g]).astype(BF) for g in range(4)]
    grad_scores = []
    for g in range(4):
        probs = probs_ref[g].astype(F32)
        inner = jnp.sum(probs * grad_probs[g], axis=0, keepdims=True)
        grad_scores.append((probs * (grad_probs[g] - inner) * float(HD) ** -0.5).astype(BF))
    grad_k = [dot(grad_scores[g], by_head(cells_ref[g, :, 0:LANES])).astype(BF) for g in range(4)]
    full = [dot(cells_ref[g, :, LANES : 2 * LANES], grad_scores[g], TN) for g in range(4)]
    grad_q = [diagonal(x).astype(BF) for x in full]
    back = None
    for g in range(4):
        pick = move_ref[g]
        pair = jnp.concatenate([grad_k[g], grad_v[g]], axis=1)
        moved = jnp.concatenate([dot(pick, grad_q[g], NT), dot(pick, pair)], axis=1)
        own_ref[g] = moved[2 * BUF :].astype(BF)
        far = moved[0 : 2 * BUF]
        back = far if back is None else back + far
    bw_ref[0] = back[0:BUF].astype(BF)
    be_ref[0] = back[BUF:].astype(BF)


def project_kernel(
    tab, own_ref, hw_ref, he_ref, rw_ref, re_ref, w_ref, cot_ref, out_ref, dw_ref, pad_ref
):
    cols, rows, channels = out_ref.shape
    for sub in range(rows // WIN):
        for g in range(4):
            s = sub * 4 + g
            full = dot(hw_ref[s], rw_ref[sub]) + dot(he_ref[s], re_ref[sub])
            full = (full + own_ref[s].astype(F32)).astype(BF).reshape(WIN, PAD, LANES)
            for i in range(WIN):
                pad_ref[tab[sub, 4 + i], :, g * LANES : (g + 1) * LANES] = full[i]
    att = jnp.swapaxes(pad_ref[:, 0:WIN, :], 0, 1).reshape(cols * rows, channels)
    out_ref[...] = dot(att, w_ref[...]).astype(BF).reshape(cols, rows, channels)
    dw_ref[...] = dot(att, cot_ref[...].reshape(cols * rows, channels), TN).astype(BF)


def place_kernel(tab, own_ref, hw_ref, he_ref, rw_ref, re_ref, dq_ref, dk_ref, dv_ref, pad_ref):
    cols, rows, channels = dq_ref.shape
    for sub in range(rows // WIN):
        for g in range(4):
            s = sub * 4 + g
            full = dot(hw_ref[s], rw_ref[sub]) + dot(he_ref[s], re_ref[sub])
            full = (full + own_ref[s].astype(F32)).astype(BF).reshape(WIN, PAD, 3 * LANES)
            for i in range(WIN):
                for a in range(3):
                    pad_ref[a, tab[sub, 4 + i], :, g * LANES : (g + 1) * LANES] = full[
                        i, :, a * LANES : (a + 1) * LANES
                    ]
    for a, ref in enumerate((dq_ref, dk_ref, dv_ref)):
        ref[...] = jnp.swapaxes(pad_ref[a, :, 0:WIN, :], 0, 1)


def shape(*dims, kind=BF):
    return jax.ShapeDtypeStruct(dims, kind)


SMEM = pl.BlockSpec(memory_space=pltpu.SMEM)
VMEM = pl.BlockSpec(memory_space=pltpu.VMEM)


def params(mib):
    return pltpu.CompilerParams(vmem_limit_bytes=mib * MIB)


WHOLE, SHARED = params(63), params(20)


def cost(flops, size, exps=0):
    return pl.CostEstimate(flops=int(flops), bytes_accessed=int(size), transcendentals=int(exps))


def sum_stages(count):
    stages, bit = [(1, 2)], 2
    while bit < count:
        ways = 4 if 4 * bit <= count else 2
        stages.append((bit, ways))
        bit *= ways
    return stages


def scattered_sum(partial, axis, bit, ways):
    place = (lax.axis_index(axis) // bit) % ways
    part = partial.shape[0] // ways
    piece = lambda k: lax.dynamic_slice_in_dim(partial, (place ^ k) * part, part, 0)
    total = piece(0).astype(F32)
    for far in [swapped(piece(k), axis, k * bit) for k in range(ways - 1, 0, -1)]:
        total = total + far.astype(F32)
    return total.astype(BF)


def gathered_back(partial, axis, bit, ways):
    place = (lax.axis_index(axis) // bit) % ways
    parts = [partial] + [swapped(partial, axis, k * bit) for k in range(1, ways)]
    rows = []
    for slot in range(ways):
        x = parts[0]
        for k in range(1, ways):
            x = jnp.where(place == slot ^ k, parts[k], x)
        rows.append(x)
    return jnp.concatenate(rows)


def turned(x):
    return jnp.transpose(x, (1, 0, 2))


def per_device(queries, key_vectors, value_vectors, out_weight, lat_window, lon_offset, cotangent):
    rows, cols, channels = queries.shape
    subs = rows // WIN
    steps = subs * 4
    buf_f, buf_g = shape(subs, BUF, 3 * LANES), shape(subs, BUF, LANES)
    cot_t = turned(cotangent)
    tab, own, west_f, east_f = pl.pallas_call(
        pack_kernel,
        in_specs=[SMEM, SMEM] + [VMEM] * 3,
        out_specs=[SMEM] + [VMEM] * 3,
        out_shape=[
            shape(subs, 4 + WIN, kind=jnp.int32), shape(steps, OWN, 3 * LANES), buf_f, buf_f,
        ],
        scratch_shapes=[pltpu.VMEM((3, rows, PAD, channels), BF)],
        compiler_params=WHOLE,
        cost_estimate=cost(4e9, 8e6),
    )(lat_window, lon_offset, turned(queries), turned(key_vectors), turned(value_vectors))

    from_east_f = passed_along(west_f, "lon", -1)
    from_west_f = passed_along(east_f, "lon", 1)

    own_g, west_g, east_g = pl.pallas_call(
        pack_grad_kernel,
        in_specs=[SMEM] + [VMEM] * 2,
        out_specs=[VMEM] * 3,
        out_shape=[shape(steps, OWN, LANES), buf_g, buf_g],
        scratch_shapes=[pltpu.VMEM((1, rows, PAD, channels), BF)],
        compiler_params=WHOLE,
        cost_estimate=cost(4e9, 3e6),
    )(tab, cot_t, out_weight)

    from_east_g = passed_along(west_g, "lon", -1)
    from_west_g = passed_along(east_g, "lon", 1)

    group = lambda *dims: pl.BlockSpec((4,) + dims, lambda s: (s, 0, 0))
    each = lambda *dims: pl.BlockSpec((1,) + dims, lambda s: (s, 0, 0))
    windows, pick, far_w, far_e, move, home_w, home_e = pl.pallas_call(
        prepare_kernel,
        grid=(subs,),
        in_specs=[SMEM, group(OWN, 3 * LANES)],
        out_specs=[
            group(SUB, 3 * LANES), group(SUB, OWN), group(SUB, BUF), group(SUB, BUF), group(2 * BUF + OWN, SUB),
            group(OWN, BUF), group(OWN, BUF),
        ],
        out_shape=[
            shape(steps, SUB, 3 * LANES), shape(steps, SUB, OWN), shape(steps, SUB, BUF),
            shape(steps, SUB, BUF),
            shape(steps, 2 * BUF + OWN, SUB), shape(steps, OWN, BUF), shape(steps, OWN, BUF),
        ],
        compiler_params=SHARED,
        cost_estimate=cost(6e9, 20e6),
    )(tab, own)

    probs, cells, own_a, back_e_a, back_w_a = pl.pallas_call(
        forward_kernel,
        grid=(subs,),
        in_specs=[
            SMEM, group(SUB, 3 * LANES), group(SUB, BUF), group(SUB, BUF),
            group(2 * BUF + OWN, SUB), each(BUF, 3 * LANES), each(BUF, 3 * LANES),
        ],
        out_specs=[
            group(SUB, GH * SUB), group(SUB, 3 * LANES), group(OWN, LANES),
            each(BUF, LANES), each(BUF, LANES),
        ],
        out_shape=[
            shape(steps, SUB, GH * SUB), shape(steps, SUB, 3 * LANES), shape(steps, OWN, LANES),
            buf_g, buf_g,
        ],
        compiler_params=SHARED,
        cost_estimate=cost(6e9, 10e6, 1.4e6),
    )(tab, windows, far_w, far_e, move, from_east_f, from_west_f)

    home_w_a = passed_along(back_e_a, "lon", 1)
    home_e_a = passed_along(back_w_a, "lon", -1)

    own_d, back_e_d, back_w_d = pl.pallas_call(
        backward_kernel,
        grid=(subs,),
        in_specs=[
            group(SUB, GH * SUB), group(SUB, 3 * LANES),
            group(OWN, LANES), group(SUB, OWN), group(SUB, BUF), group(SUB, BUF),
            group(2 * BUF + OWN, SUB), each(BUF, LANES), each(BUF, LANES),
        ],
        out_specs=[group(OWN, 3 * LANES), each(BUF, 3 * LANES), each(BUF, 3 * LANES)],
        out_shape=[shape(steps, OWN, 3 * LANES), buf_f, buf_f],
        compiler_params=SHARED,
        cost_estimate=cost(8e9, 10e6),
    )(probs, cells, own_g, pick, far_w, far_e, move, from_east_g, from_west_g)

    home_w_d = passed_along(back_e_d, "lon", 1)
    home_e_d = passed_along(back_w_d, "lon", -1)

    home_w_a, home_e_a, own_d = lax.optimization_barrier((home_w_a, home_e_a, own_d))
    whole = shape(cols, rows, channels)
    mixed, partial = pl.pallas_call(
        project_kernel,
        in_specs=[SMEM] + [VMEM] * 7,
        out_specs=[VMEM] * 2,
        out_shape=[whole, shape(channels, channels)],
        scratch_shapes=[pltpu.VMEM((rows, PAD, channels), BF)],
        compiler_params=SHARED,
        cost_estimate=cost(2e9, 4e6),
    )(tab, own_a, home_w, home_e, home_w_a, home_e_a, out_weight, cot_t)

    stages = sum_stages(lax.axis_size("lon"))
    for bit, ways in stages:
        partial = scattered_sum(partial, "lon", bit, ways)
    partial, home_w_d, home_e_d = lax.optimization_barrier((partial, home_w_d, home_e_d))
    partial = gathered_back(partial, "lon", *stages[-1])
    grads = pl.pallas_call(
        place_kernel,
        in_specs=[SMEM] + [VMEM] * 5,
        out_specs=[VMEM] * 3,
        out_shape=[whole] * 3,
        scratch_shapes=[pltpu.VMEM((3, rows, PAD, channels), BF)],
        compiler_params=SHARED,
        cost_estimate=cost(2e9, 6e6),
    )(tab, own_d, home_w, home_e, home_w_d, home_e_d)

    partial, grads = lax.optimization_barrier((partial, grads))
    for bit, ways in stages[-2::-1]:
        partial = gathered_back(partial, "lon", bit, ways)
    total = partial.astype(F32)

    return (turned(mixed),) + tuple(turned(x) for x in grads) + (total,)


def solution(mesh):
    placed = (
        P("groups", "lon", None),
        P("groups", "lon", None),
        P("groups", "lon", None),
        P(),
        P("groups"),
        P("groups"),
        P("groups", "lon", None),
    )
    return jax.shard_map(
        per_device,
        mesh=mesh,
        in_specs=placed,
        out_specs=(
            P("groups", "lon", None),
            P("groups", "lon", None),
            P("groups", "lon", None),
            P("groups", "lon", None),
            P("groups", None),
        ),
        check_vma=False,
    )
```

time: 140 us -> 91.7 us (0.66)
  waiting for transfers between devices: 44.6 us -> 12.8 us
  Pallas kernels: 56.9 us -> 40.6 us
  starting transfers between devices: 19.8 us -> 29.5 us
  local copies, waits for them, and re-layouts: 15.5 us -> 6.23 us
    ppermute x8, waiting for transfers between devices: 18.3 us -> 0.32 us  [passed_along(): return lax.ppermute(value, axis, pairs)]
    pallas_call x5 -> x7, Pallas kernels: 56.9 us -> 40.6 us  [the longest x1 9.99 us: per_device(): pl.pallas_call(backward_kernel, grid=(subs,), in_specs=[group(SUB, GH * S...]
    ppermute x8 -> x10, waiting for transfers between devices: 26.3 us -> 12.4 us  [swapped(): lax.ppermute(value, axis, [(source, source ^ bit) for source in range(cou...]
    unnamed x32 -> x22, local copies, waits for them, and re-layouts: 15.5 us -> 6.18 us
    ppermute x8 -> x10, starting transfers between devices: 4.78 us -> 10.6 us  [swapped(): lax.ppermute(value, axis, [(source, source ^ bit) for source in range(cou...]
    ppermute x8, starting transfers between devices: 15 us -> 18.9 us  [passed_along(): return lax.ppermute(value, axis, pairs)]
  transfers between devices with their start and end apart: 16 -> 18, of which waited for: 10 -> 6; matrix products, arithmetic and copies ran while one was open for 3% -> 0% of each run, Pallas kernels for 19% -> 35%
where the time goes in v2:
time: 91.7 us; the launch traced here: 91.4 us
  Pallas kernels  40.6 us (44%)
  starting transfers between devices  29.5 us (32%)
  waiting for transfers between devices  12.8 us (14%)
  local copies, waits for them, and re-layouts  6.23 us (7%)
  other arithmetic  1.39 us (2%)
  between operations  0.98 us (1%)
    ppermute x8, starting transfers between devices, passed_along(): return lax.ppermute(value, axis, pairs)  18.9 us
    ppermute x10, waiting for transfers between devices, swapped(): lax.ppermute(value, axis, [(source, source ^ bit) for source in range(cou...  12.4 us
    ppermute x10, starting transfers between devices, swapped(): lax.ppermute(value, axis, [(source, source ^ bit) for source in range(cou...  10.6 us
    pallas_call x1, Pallas kernels, per_device(): pl.pallas_call(backward_kernel, grid=(subs,), in_specs=[group(SUB, GH * S...  9.99 us
    pallas_call x1, Pallas kernels, per_device(): pl.pallas_call(forward_kernel, grid=(subs,), in_specs=[SMEM, group(SUB, 3...  8.1 us
    pallas_call x1, Pallas kernels, per_device(): pl.pallas_call(prepare_kernel, grid=(subs,), in_specs=[SMEM, group(OWN, 3...  6.8 us
    unnamed x22, local copies, waits for them, and re-layouts  6.18 us
    pallas_call x1, Pallas kernels, per_device(): pl.pallas_call(pack_kernel, in_specs=[SMEM, SMEM] + [VMEM] * 3, out_specs...  5.36 us
  transfers between devices with their start and end apart: 18, of which 6 were waited for; matrix products, arithmetic and copies ran while one was open for 0% of the time, Pallas kernels for 35%

profile of v2, /device:TPU:0, one launch (start us, length us, event | category | flops | bytes accessed | tf_op | source)
XLA Modules:
  0.0 91.4 jit_solution(15010499909741129842)
XLA Ops:
  0.6 5.4 %shard_map.110 = (s32[4,16]{1,0:T(4,128)}, bf16[16,192,384]{2,1,0:T(8,128)(2,1)}, bf16[4,176,384]{2,1,0:T(8,128)(2,1)}, bf16[4,176,384]{2,1,0:T(8,128)(2,1)}) custom-call(s32[48]{0:T(128)} %lat.1, s32[48]{0:T(128)} %lon.1, bf16[12,48,512]{2,1,0:T(8,128)(2,1)} %bitcast.10, bf16[12,48,512]{2,1,0:T(8,128)(2,1)} %bitcast.11, bf16[12,48,512]{2,1,0:T(8,128)(2,1)} %bitcast.12), custom_call_target="tpu_custom_call" | custom-call | flops 4000000000 | bytes 8000000 | tf_op jit(solution)/shard_map/pallas_call | solution.py:364
  6.0 5.5 %collective-permute-start = (bf16[4,176,384]{2,1,0:T(8,128)(2,1)}, bf16[4,176,384]{2,1,0:T(8,128)(2,1)S(1)}, u32[]{:S(2)}, u32[]{:S(2)}) collective-permute-start(bf16[4,176,384]{2,1,0:T(8,128)(2,1)} %get-tuple-element.48), channel_id=1, source_target_pairs={{0,15},{1,0},{2,1},{3,2},{4,3},{5,4},{6,5},{7,6},{8,7},{9,8},{10,9... | collective-permute-start | bytes 1622024 | tf_op jit(solution)/shard_map/ppermute | solution.py:34
  11.5 0.0 collective-permute-start.1
  11.5 0.0 copy-start.10
  11.5 3.7 %shard_map.113 = (bf16[16,192,128]{2,1,0:T(8,128)(2,1)}, bf16[4,176,128]{2,1,0:T(8,128)(2,1)}, bf16[4,176,128]{2,1,0:T(8,128)(2,1)}) custom-call(s32[4,16]{1,0:T(4,128)} %get-tuple-element.42.tab, bf16[12,48,512]{2,1,0:T(8,128)(2,1)} %bitcast.8, bf16[512,512]{1,0:T(8,128)(2,1)} %w_ref.3), custom_call_target="tpu_custom_call" | custom-call | flops 4000000000 | bytes 3000000 | tf_op jit(solution)/shard_map/pallas_call | solution.py:379
  15.2 4.4 %collective-permute-start.4 = (bf16[4,176,128]{2,1,0:T(8,128)(2,1)}, bf16[4,176,128]{2,1,0:T(8,128)(2,1)S(1)}, u32[]{:S(2)}, u32[]{:S(2)}) collective-permute-start(bf16[4,176,128]{2,1,0:T(8,128)(2,1)} %get-tuple-element.59), channel_id=1, source_target_pairs={{0,15},{1,0},{2,1},{3,2},{4,3},{5,4},{6,5},{7,6},{8,7},{9,8},{10,9... | collective-permute-start | bytes 540680 | tf_op jit(solution)/shard_map/ppermute | solution.py:34
  19.6 0.0 collective-permute-start.5
  19.6 0.0 copy-done.10
  19.6 1.7 %copy-done.8 = bf16[16,192,384]{2,1,0:T(8,128)(2,1)S(1)} copy-done((bf16[16,192,384]{2,1,0:T(8,128)(2,1)S(1)}, bf16[16,192,384]{2,1,0:T(8,128)(2,1)}, u32[]{:S(2)}) %copy-start.8) | copy-done | bytes 2359320
  21.3 6.8 %shard_map.111 = (bf16[16,144,384]{2,1,0:T(8,128)(2,1)S(1)}, bf16[16,144,192]{2,1,0:T(8,128)(2,1)S(1)}, bf16[16,144,176]{2,1,0:T(8,128)(2,1)S(1)}, bf16[16,144,1...) custom-call(s32[4,16]{1,0:T(4,128)S(1)} %copy-done.10, ...), custom_call_target="tpu_custom_call" | custom-call | flops 6000000000 | bytes 20000000 | tf_op jit(solution)/shard_map/pallas_call | solution.py:394
  28.1 0.0 copy-start.4
  28.1 0.0 copy-start.6
  28.1 0.0 collective-permute-done.rw_ref
  28.1 0.0 collective-permute-done.1.re_ref
  28.1 0.0 copy-start.9
  28.1 8.1 %shard_map.112 = (bf16[16,144,576]{2,1,0:T(8,128)(2,1)S(1)}, bf16[16,144,384]{2,1,0:T(8,128)(2,1)S(1)}, bf16[16,192,128]{2,1,0:T(8,128)(2,1)S(1)}, bf16[4,176,12...) custom-call(s32[4,16]{1,0:T(4,128)S(1)} %copy-done.10, bf16[16,144,384]{2,1,0:T(8,128)(2,1)S(1)} %get-tuple-element.44.win_ref, ...), custom_call_target="tpu_custom_call" | custom-call | flops 6000000000 | bytes 10000000 | tf_op jit(solution)/shard_map/pallas_call | solution.py:411
  36.2 0.1 collective-permute-start.2
  36.3 4.5 %collective-permute-start.3 = (bf16[4,176,128]{2,1,0:T(8,128)(2,1)S(1)}, bf16[4,176,128]{2,1,0:T(8,128)(2,1)S(1)}, u32[]{:S(2)}, u32[]{:S(2)}) collective-permute-start(bf16[4,176,128]{2,1,0:T(8,128)(2,1)S(1)} %get-tuple-element.54), channel_id=1, source_target_pairs={{0,15},{1,0},{2,1},{3,2},{4,3},{5,4},{6,5},{7,6},{8,7},{9,8},{10,9... | collective-permute-start | bytes 540680 | tf_op jit(solution)/shard_map/ppermute | solution.py:34
  40.8 0.0 collective-permute-done.4.rw_ref
  40.8 0.0 collective-permute-done.5.re_ref
  40.8 0.0 copy-done.9
  40.8 0.0 copy-start
  40.8 0.0 copy-start.1
  40.8 10.0 %shard_map.114 = (bf16[16,192,384]{2,1,0:T(8,128)(2,1)S(1)}, bf16[4,176,384]{2,1,0:T(8,128)(2,1)S(1)}, bf16[4,176,384]{2,1,0:T(8,128)(2,1)S(1)}) custom-call(bf16[16,144,576]{2,1,0:T(8,128)(2,1)S(1)} %get-tuple-element.55.probs_ref, bf16[16,144,384]{2,1,0:T(8,128)(2,1)S(1)} %get-tuple-element.56.cells_ref, bf16[16,192,128]{2,1,0:T(8,128)(2,1)S(1)} %copy-done.9, ...), custom_call_target="tpu_custom_call" | custom-call | flops 8000000000 | bytes 10000000 | tf_op jit(solution)/shard_map/pallas_call | solution.py:433
  50.8 0.0 copy-start.2
  50.8 0.0 collective-permute-done.2.rw_ref
  50.8 0.0 collective-permute-done.3.re_ref
  50.9 0.0 copy-done.4
  50.9 0.0 copy-done.6
  50.9 0.0 copy-done
  50.9 0.0 copy-done.1
  50.9 2.9 %shard_map.115 = (bf16[12,48,512]{2,1,0:T(8,128)(2,1)}, bf16[512,512]{1,0:T(8,128)(2,1)S(1)}) custom-call(s32[4,16]{1,0:T(4,128)S(1)} %copy-done.10, bf16[16,192,128]{2,1,0:T(8,128)(2,1)S(1)} %get-tuple-element.50.own_ref, bf16[16,192,176]{2,1,0:T(8,128)(2,1)S(1)} %get-tuple-element.51.hw_ref, bf16[16,192,176]{2,1,0:T(8,128)(2,1)S(1)} %get-tuple-element.52.he_ref, ...), custom_call_target="tpu_custom_call" | custom-call | flops 2000000000 | bytes 4000000 | tf_op jit(solution)/shard_map/pallas_call | solution.py:452
  53.8 0.0 copy-done.2
  53.8 0.1 collective-permute-start.6
  53.9 1.5 %collective-permute-done.6 = bf16[256,512]{1,0:T(8,128)(2,1)S(1)} collective-permute-done((bf16[256,512]{1,0:T(8,128)(2,1)S(1)}, bf16[256,512]{1,0:T(8,128)(2,1)S(1)}, u32[]{:S(2)}, u32[]{:S(2)}) %collective-permute-start.6) | collective-permute-done | bytes 262176 | tf_op jit(solution)/shard_map/ppermute | solution.py:39
  55.4 0.1 add_convert_fusion
  55.5 0.1 collective-permute-start.9
  55.6 0.1 collective-permute-start.8
  55.7 3.4 %collective-permute-start.7 = (bf16[64,512]{1,0:T(8,128)(2,1)S(1)}, bf16[64,512]{1,0:T(8,128)(2,1)S(1)}, u32[]{:S(2)}, u32[]{:S(2)}) collective-permute-start(bf16[64,512]{1,0:T(8,128)(2,1)S(1)} %get-tuple-element.85), channel_id=1, source_target_pairs={{0,6},{1,7},{2,4},{3,5},{4,2},{5,3},{6,0},{7,1},{8,14},{9,15},{10,... | collective-permute-start | bytes 196616 | tf_op jit(solution)/shard_map/ppermute | solution.py:39
  59.1 0.0 collective-permute-start.11
  59.1 4.4 %collective-permute-start.12 = (bf16[4,176,384]{2,1,0:T(8,128)(2,1)S(1)}, bf16[4,176,384]{2,1,0:T(8,128)(2,1)S(1)}, u32[]{:S(2)}, u32[]{:S(2)}) collective-permute-start(bf16[4,176,384]{2,1,0:T(8,128)(2,1)S(1)} %get-tuple-element.67), channel_id=1, source_target_pairs={{0,15},{1,0},{2,1},{3,2},{4,3},{5,4},{6,5},{7,6},{8,7},{9,8},{10,9... | collective-permute-start | bytes 1622024 | tf_op jit(solution)/shard_map/ppermute | solution.py:34
  63.5 0.0 collective-permute-done.9
  63.5 0.0 collective-permute-done.8
  63.5 0.0 collective-permute-done.7
  63.6 0.1 collective-permute-start.10
  63.7 7.1 %collective-permute-done.10 = bf16[32,512]{1,0:T(8,128)(2,1)S(1)} collective-permute-done((bf16[32,512]{1,0:T(8,128)(2,1)S(1)}, bf16[32,512]{1,0:T(8,128)(2,1)S(1)}, u32[]{:S(2)}, u32[]{:S(2)}) %collective-permute-start.10) | collective-permute-done | bytes 32800 | tf_op jit(solution)/shard_map/ppermute | solution.py:39
  70.8 0.3 collective-permute-done.11.rw_ref
  71.1 0.0 collective-permute-done.12.re_ref
  71.1 3.3 %collective-permute-start.13 = (bf16[32,512]{1,0:T(8,128)(2,1)S(1)}, bf16[32,512]{1,0:T(8,128)(2,1)S(1)}, u32[]{:S(2)}, u32[]{:S(2)}) collective-permute-start(bf16[32,512]{1,0:T(8,128)(2,1)S(1)} %add_convert_fusion.2), channel_id=1, source_target_pairs={{0,8},{1,9},{2,10},{3,11},{4,12},{5,13},{6,14},{7,15},{8,0},{9,1},... | collective-permute-start | bytes 98312 | tf_op jit(solution)/shard_map/ppermute | solution.py:39
  74.3 1.7 %copy-done.3 = bf16[16,192,384]{2,1,0:T(8,128)(2,1)S(1)} copy-done((bf16[16,192,384]{2,1,0:T(8,128)(2,1)S(1)}, bf16[16,192,384]{2,1,0:T(8,128)(2,1)}, u32[]{:S(2)}) %copy-start.3) | copy-done | bytes 2359320
  76.0 1.4 %copy-done.5 = bf16[16,192,176]{2,1,0:T(8,128)(2,1)S(1)} copy-done((bf16[16,192,176]{2,1,0:T(8,128)(2,1)S(1)}, bf16[16,192,176]{2,1,0:T(8,128)(2,1)}, u32[]{:S(2)}) %copy-start.5) | copy-done | bytes 1081368
  77.4 1.4 %copy-done.7 = bf16[16,192,176]{2,1,0:T(8,128)(2,1)S(1)} copy-done((bf16[16,192,176]{2,1,0:T(8,128)(2,1)S(1)}, bf16[16,192,176]{2,1,0:T(8,128)(2,1)}, u32[]{:S(2)}) %copy-start.7) | copy-done | bytes 1081368
  78.8 3.8 %shard_map.116 = (bf16[12,48,512]{2,1,0:T(8,128)(2,1)}, bf16[12,48,512]{2,1,0:T(8,128)(2,1)}, bf16[12,48,512]{2,1,0:T(8,128)(2,1)}) custom-call(s32[4,16]{1,0:T(4,128)S(1)} %copy-done.10, bf16[16,192,384]{2,1,0:T(8,128)(2,1)S(1)} %copy-done.3, bf16[16,192,176]{2,1,0:T(8,128)(2,1)S(1)} %copy-done.5, bf16[16,192,176]{2,1,0:T(8,128)(2,1)S(1)} %copy-done.7, ...), custom_call_target="tpu_custom_call" | custom-call | flops 2000000000 | bytes 6000000 | tf_op jit(solution)/shard_map/pallas_call | solution.py:467
  82.6 0.0 collective-permute-done.13
  82.6 0.8 collective-permute-start.14
  83.4 0.8 collective-permute-start.15
  84.2 2.0 %collective-permute-start.16 = (bf16[64,512]{1,0:T(8,128)(2,1)S(1)}, bf16[64,512]{1,0:T(8,128)(2,1)S(1)}, u32[]{:S(2)}, u32[]{:S(2)}) collective-permute-start(bf16[64,512]{1,0:T(8,128)(2,1)S(1)} %pad_maximum_fusion.1), channel_id=1, source_target_pairs={{0,2},{1,3},{2,0},{3,1},{4,6},{5,7},{6,4},{7,5},{8,10},{9,11},{10,... | collective-permute-start | bytes 196616 | tf_op jit(solution)/shard_map/ppermute | solution.py:39
  86.2 1.7 %collective-permute-done.14 = bf16[64,512]{1,0:T(8,128)(2,1)S(1)} collective-permute-done((bf16[64,512]{1,0:T(8,128)(2,1)S(1)}, bf16[64,512]{1,0:T(8,128)(2,1)S(1)}, u32[]{:S(2)}, u32[]{:S(2)}) %collective-permute-start.14) | collective-permute-done | bytes 65568 | tf_op jit(solution)/shard_map/ppermute | solution.py:39
  87.9 0.0 collective-permute-done.15
  87.9 0.7 collective-permute-done.16
  88.6 0.1 collective-permute-start.17
  88.7 1.5 %collective-permute-done.17 = bf16[256,512]{1,0:T(8,128)(2,1)S(1)} collective-permute-done((bf16[256,512]{1,0:T(8,128)(2,1)S(1)}, bf16[256,512]{1,0:T(8,128)(2,1)S(1)}, u32[]{:S(2)}, u32[]{:S(2)}) %collective-permute-start.17) | collective-permute-done | bytes 262176 | tf_op jit(solution)/shard_map/ppermute | solution.py:39
  90.2 0.1 broadcast_select_fusion.1
  90.3 1.1 %maximum_convert_fusion = f32[512,512]{1,0:T(8,128)} fusion(bf16[256,512]{1,0:T(8,128)(2,1)S(1)} %get-tuple-element.80, bf16[256,512]{1,0:T(8,128)(2,1)S(1)} %get-tuple-element.79), kind=kLoop, calls=%fused_computation | loop fusion | flops 1048576 | bytes 1572864 | tf_op jit(solution)/shard_map/convert_element_type | solution.py:480
  (13 shorter events, 0.2 us)
Async XLA Ops:
  6.0 22.1 %collective-permute-start = (bf16[4,176,384]{2,1,0:T(8,128)(2,1)}, bf16[4,176,384]{2,1,0:T(8,128)(2,1)S(1)}, u32[]{:S(2)}, u32[]{:S(2)}) collective-permute-start(bf16[4,176,384]{2,1,0:T(8,128)(2,1)} %get-tuple-element.48), channel_id=1, source_target_pairs={{0,15},{1,0},{2,1},{3,2},{4,3},{5,4},{6,5},{7,6},{8,7},{9,8},{10,9... | collective-permute-start | bytes 1622024 | tf_op jit(solution)/shard_map/ppermute | solution.py:34
  11.5 16.6 %collective-permute-start.1 = (bf16[4,176,384]{2,1,0:T(8,128)(2,1)}, bf16[4,176,384]{2,1,0:T(8,128)(2,1)}, u32[]{:S(2)}, u32[]{:S(2)}) collective-permute-start(bf16[4,176,384]{2,1,0:T(8,128)(2,1)} %get-tuple-element.49), channel_id=1, source_target_pairs={{0,1},{1,2},{2,3},{3,4},{4,5},{5,6},{6,7},{7,8},{8,9},{9,10},{10,1... | collective-permute-start | bytes 1622024 | tf_op jit(solution)/shard_map/ppermute | solution.py:34
  11.5 8.1 %copy-start.10 = (s32[4,16]{1,0:T(4,128)S(1)}, s32[4,16]{1,0:T(4,128)}, u32[]{:S(2)}) copy-start(s32[4,16]{1,0:T(4,128)} %get-tuple-element.42.tab) | copy-start | bytes 772
  15.2 25.6 %collective-permute-start.4 = (bf16[4,176,128]{2,1,0:T(8,128)(2,1)}, bf16[4,176,128]{2,1,0:T(8,128)(2,1)S(1)}, u32[]{:S(2)}, u32[]{:S(2)}) collective-permute-start(bf16[4,176,128]{2,1,0:T(8,128)(2,1)} %get-tuple-element.59), channel_id=1, source_target_pairs={{0,15},{1,0},{2,1},{3,2},{4,3},{5,4},{6,5},{7,6},{8,7},{9,8},{10,9... | collective-permute-start | bytes 540680 | tf_op jit(solution)/shard_map/ppermute | solution.py:34
  19.6 21.2 %collective-permute-start.5 = (bf16[4,176,128]{2,1,0:T(8,128)(2,1)}, bf16[4,176,128]{2,1,0:T(8,128)(2,1)S(1)}, u32[]{:S(2)}, u32[]{:S(2)}) collective-permute-start(bf16[4,176,128]{2,1,0:T(8,128)(2,1)} %get-tuple-element.60), channel_id=1, source_target_pairs={{0,1},{1,2},{2,3},{3,4},{4,5},{5,6},{6,7},{7,8},{8,9},{9,10},{10,1... | collective-permute-start | bytes 540680 | tf_op jit(solution)/shard_map/ppermute | solution.py:34
  19.6 1.7 %copy-start.8 = (bf16[16,192,384]{2,1,0:T(8,128)(2,1)S(1)}, bf16[16,192,384]{2,1,0:T(8,128)(2,1)}, u32[]{:S(2)}) copy-start(bf16[16,192,384]{2,1,0:T(8,128)(2,1)} %get-tuple-element.43.own_ref) | copy-start | bytes 7077892
  28.1 22.8 %copy-start.4 = (bf16[16,192,176]{2,1,0:T(8,128)(2,1)}, bf16[16,192,176]{2,1,0:T(8,128)(2,1)S(1)}, u32[]{:S(2)}) copy-start(bf16[16,192,176]{2,1,0:T(8,128)(2,1)S(1)} %get-tuple-element.51.hw_ref) | copy-start | bytes 3244036
  28.1 22.8 %copy-start.6 = (bf16[16,192,176]{2,1,0:T(8,128)(2,1)}, bf16[16,192,176]{2,1,0:T(8,128)(2,1)S(1)}, u32[]{:S(2)}) copy-start(bf16[16,192,176]{2,1,0:T(8,128)(2,1)S(1)} %get-tuple-element.52.he_ref) | copy-start | bytes 3244036
  28.1 12.7 %copy-start.9 = (bf16[16,192,128]{2,1,0:T(8,128)(2,1)S(1)}, bf16[16,192,128]{2,1,0:T(8,128)(2,1)}, u32[]{:S(2)}) copy-start(bf16[16,192,128]{2,1,0:T(8,128)(2,1)} %get-tuple-element.57.og_ref) | copy-start | bytes 2359300
  36.2 14.6 %collective-permute-start.2 = (bf16[4,176,128]{2,1,0:T(8,128)(2,1)S(1)}, bf16[4,176,128]{2,1,0:T(8,128)(2,1)S(1)}, u32[]{:S(2)}, u32[]{:S(2)}) collective-permute-start(bf16[4,176,128]{2,1,0:T(8,128)(2,1)S(1)} %get-tuple-element.53), channel_id=1, source_target_pairs={{0,1},{1,2},{2,3},{3,4},{4,5},{5,6},{6,7},{7,8},{8,9},{9,10},{10,1... | collective-permute-start | bytes 540680 | tf_op jit(solution)/shard_map/ppermute | solution.py:34
  36.3 14.5 %collective-permute-start.3 = (bf16[4,176,128]{2,1,0:T(8,128)(2,1)S(1)}, bf16[4,176,128]{2,1,0:T(8,128)(2,1)S(1)}, u32[]{:S(2)}, u32[]{:S(2)}) collective-permute-start(bf16[4,176,128]{2,1,0:T(8,128)(2,1)S(1)} %get-tuple-element.54), channel_id=1, source_target_pairs={{0,15},{1,0},{2,1},{3,2},{4,3},{5,4},{6,5},{7,6},{8,7},{9,8},{10,9... | collective-permute-start | bytes 540680 | tf_op jit(solution)/shard_map/ppermute | solution.py:34
  40.8 10.1 %copy-start = (bf16[48,12,512]{2,0,1:T(8,128)(2,1)S(1)}, bf16[48,12,512]{2,0,1:T(8,128)(2,1)}, u32[]{:S(2)}) copy-start(bf16[48,12,512]{2,0,1:T(8,128)(2,1)} %param.13) | copy-start | bytes 1769476
  40.8 10.1 %copy-start.1 = (bf16[512,512]{1,0:T(8,128)(2,1)S(1)}, bf16[512,512]{1,0:T(8,128)(2,1)}, u32[]{:S(2)}) copy-start(bf16[512,512]{1,0:T(8,128)(2,1)} %w_ref.3) | copy-start | bytes 1572868
  50.8 3.0 %copy-start.2 = (bf16[16,192,384]{2,1,0:T(8,128)(2,1)}, bf16[16,192,384]{2,1,0:T(8,128)(2,1)S(1)}, u32[]{:S(2)}) copy-start(bf16[16,192,384]{2,1,0:T(8,128)(2,1)S(1)} %get-tuple-element.69.own_ref) | copy-start | bytes 7077892
  53.8 1.6 %collective-permute-start.6 = (bf16[256,512]{1,0:T(8,128)(2,1)S(1)}, bf16[256,512]{1,0:T(8,128)(2,1)S(1)}, u32[]{:S(2)}, u32[]{:S(2)}) collective-permute-start(bf16[256,512]{1,0:T(8,128)(2,1)S(1)} %constant_dynamic-slice_fusion.4), channel_id=1, source_target_pairs={{0,1},{1,0},{2,3},{3,2},{4,5},{5,4},{6,7},{7,6},{8,9},{9,8},{10,11... | collective-permute-start | bytes 786440 | tf_op jit(solution)/shard_map/ppermute | solution.py:39
  55.5 8.0 %collective-permute-start.9 = (bf16[64,512]{1,0:T(8,128)(2,1)S(1)}, bf16[64,512]{1,0:T(8,128)(2,1)S(1)}, u32[]{:S(2)}, u32[]{:S(2)}) collective-permute-start(bf16[64,512]{1,0:T(8,128)(2,1)S(1)} %get-tuple-element.86), channel_id=1, source_target_pairs={{0,2},{1,3},{2,0},{3,1},{4,6},{5,7},{6,4},{7,5},{8,10},{9,11},{10,... | collective-permute-start | bytes 196616 | tf_op jit(solution)/shard_map/ppermute | solution.py:39
  55.6 7.9 %collective-permute-start.8 = (bf16[64,512]{1,0:T(8,128)(2,1)S(1)}, bf16[64,512]{1,0:T(8,128)(2,1)S(1)}, u32[]{:S(2)}, u32[]{:S(2)}) collective-permute-start(bf16[64,512]{1,0:T(8,128)(2,1)S(1)} %get-tuple-element.87), channel_id=1, source_target_pairs={{0,4},{1,5},{2,6},{3,7},{4,0},{5,1},{6,2},{7,3},{8,12},{9,13},{10,... | collective-permute-start | bytes 196616 | tf_op jit(solution)/shard_map/ppermute | solution.py:39
  55.7 7.8 %collective-permute-start.7 = (bf16[64,512]{1,0:T(8,128)(2,1)S(1)}, bf16[64,512]{1,0:T(8,128)(2,1)S(1)}, u32[]{:S(2)}, u32[]{:S(2)}) collective-permute-start(bf16[64,512]{1,0:T(8,128)(2,1)S(1)} %get-tuple-element.85), channel_id=1, source_target_pairs={{0,6},{1,7},{2,4},{3,5},{4,2},{5,3},{6,0},{7,1},{8,14},{9,15},{10,... | collective-permute-start | bytes 196616 | tf_op jit(solution)/shard_map/ppermute | solution.py:39
  59.1 12.0 %collective-permute-start.11 = (bf16[4,176,384]{2,1,0:T(8,128)(2,1)S(1)}, bf16[4,176,384]{2,1,0:T(8,128)(2,1)S(1)}, u32[]{:S(2)}, u32[]{:S(2)}) collective-permute-start(bf16[4,176,384]{2,1,0:T(8,128)(2,1)S(1)} %get-tuple-element.66), channel_id=1, source_target_pairs={{0,1},{1,2},{2,3},{3,4},{4,5},{5,6},{6,7},{7,8},{8,9},{9,10},{10,1... | collective-permute-start | bytes 1622024 | tf_op jit(solution)/shard_map/ppermute | solution.py:34
  59.1 12.0 %collective-permute-start.12 = (bf16[4,176,384]{2,1,0:T(8,128)(2,1)S(1)}, bf16[4,176,384]{2,1,0:T(8,128)(2,1)S(1)}, u32[]{:S(2)}, u32[]{:S(2)}) collective-permute-start(bf16[4,176,384]{2,1,0:T(8,128)(2,1)S(1)} %get-tuple-element.67), channel_id=1, source_target_pairs={{0,15},{1,0},{2,1},{3,2},{4,3},{5,4},{6,5},{7,6},{8,7},{9,8},{10,9... | collective-permute-start | bytes 1622024 | tf_op jit(solution)/shard_map/ppermute | solution.py:34
  63.6 7.1 %collective-permute-start.10 = (bf16[32,512]{1,0:T(8,128)(2,1)S(1)}, bf16[32,512]{1,0:T(8,128)(2,1)S(1)}, u32[]{:S(2)}, u32[]{:S(2)}) collective-permute-start(bf16[32,512]{1,0:T(8,128)(2,1)S(1)} %constant_dynamic-slice_fusion), channel_id=1, source_target_pairs={{0,8},{1,9},{2,10},{3,11},{4,12},{5,13},{6,14},{7,15},{8,0},{9,1},... | collective-permute-start | bytes 98312 | tf_op jit(solution)/shard_map/ppermute | solution.py:39
  71.1 11.5 %collective-permute-start.13 = (bf16[32,512]{1,0:T(8,128)(2,1)S(1)}, bf16[32,512]{1,0:T(8,128)(2,1)S(1)}, u32[]{:S(2)}, u32[]{:S(2)}) collective-permute-start(bf16[32,512]{1,0:T(8,128)(2,1)S(1)} %add_convert_fusion.2), channel_id=1, source_target_pairs={{0,8},{1,9},{2,10},{3,11},{4,12},{5,13},{6,14},{7,15},{8,0},{9,1},... | collective-permute-start | bytes 98312 | tf_op jit(solution)/shard_map/ppermute | solution.py:39
  74.3 1.7 %copy-start.3 = (bf16[16,192,384]{2,1,0:T(8,128)(2,1)S(1)}, bf16[16,192,384]{2,1,0:T(8,128)(2,1)}, u32[]{:S(2)}) copy-start(bf16[16,192,384]{2,1,0:T(8,128)(2,1)} %copy-done.2) | copy-start | bytes 7077892
  76.0 1.4 %copy-start.5 = (bf16[16,192,176]{2,1,0:T(8,128)(2,1)S(1)}, bf16[16,192,176]{2,1,0:T(8,128)(2,1)}, u32[]{:S(2)}) copy-start(bf16[16,192,176]{2,1,0:T(8,128)(2,1)} %copy-done.4) | copy-start | bytes 3244036
  77.4 1.4 %copy-start.7 = (bf16[16,192,176]{2,1,0:T(8,128)(2,1)S(1)}, bf16[16,192,176]{2,1,0:T(8,128)(2,1)}, u32[]{:S(2)}) copy-start(bf16[16,192,176]{2,1,0:T(8,128)(2,1)} %copy-done.6) | copy-start | bytes 3244036
  82.6 5.2 %collective-permute-start.14 = (bf16[64,512]{1,0:T(8,128)(2,1)S(1)}, bf16[64,512]{1,0:T(8,128)(2,1)S(1)}, u32[]{:S(2)}, u32[]{:S(2)}) collective-permute-start(bf16[64,512]{1,0:T(8,128)(2,1)S(1)} %pad_maximum_fusion.1), channel_id=1, source_target_pairs={{0,6},{1,7},{2,4},{3,5},{4,2},{5,3},{6,0},{7,1},{8,14},{9,15},{10,... | collective-permute-start | bytes 196616 | tf_op jit(solution)/shard_map/ppermute | solution.py:39
  83.4 4.4 %collective-permute-start.15 = (bf16[64,512]{1,0:T(8,128)(2,1)S(1)}, bf16[64,512]{1,0:T(8,128)(2,1)S(1)}, u32[]{:S(2)}, u32[]{:S(2)}) collective-permute-start(bf16[64,512]{1,0:T(8,128)(2,1)S(1)} %pad_maximum_fusion.1), channel_id=1, source_target_pairs={{0,4},{1,5},{2,6},{3,7},{4,0},{5,1},{6,2},{7,3},{8,12},{9,13},{10,... | collective-permute-start | bytes 196616 | tf_op jit(solution)/shard_map/ppermute | solution.py:39
  84.2 4.3 %collective-permute-start.16 = (bf16[64,512]{1,0:T(8,128)(2,1)S(1)}, bf16[64,512]{1,0:T(8,128)(2,1)S(1)}, u32[]{:S(2)}, u32[]{:S(2)}) collective-permute-start(bf16[64,512]{1,0:T(8,128)(2,1)S(1)} %pad_maximum_fusion.1), channel_id=1, source_target_pairs={{0,2},{1,3},{2,0},{3,1},{4,6},{5,7},{6,4},{7,5},{8,10},{9,11},{10,... | collective-permute-start | bytes 196616 | tf_op jit(solution)/shard_map/ppermute | solution.py:39
  88.6 1.6 %collective-permute-start.17 = (bf16[256,512]{1,0:T(8,128)(2,1)S(1)}, bf16[256,512]{1,0:T(8,128)(2,1)S(1)}, u32[]{:S(2)}, u32[]{:S(2)}) collective-permute-start(bf16[256,512]{1,0:T(8,128)(2,1)S(1)} %pad_maximum_fusion), channel_id=1, source_target_pairs={{0,1},{1,0},{2,3},{3,2},{4,5},{5,4},{6,7},{7,6},{8,9},{9,8},{10,11... | collective-permute-start | bytes 786440 | tf_op jit(solution)/shard_map/ppermute | solution.py:39

commit v3 on v2

--- a/solution.py
+++ b/solution.py
@@ -253,6 +253,7 @@
     for g in range(4):
         probs = probs_ref[g].astype(F32)
         inner = jnp.sum(probs * grad_probs[g], axis=0, keepdims=True)
+        inner = inner / jnp.sum(probs, axis=0, keepdims=True)
         grad_scores.append((probs * (grad_probs[g] - inner) * float(HD) ** -0.5).astype(BF))
     grad_k = [dot(grad_scores[g], by_head(cells_ref[g, :, 0:LANES])).astype(BF) for g in range(4)]
     full = [dot(cells_ref[g, :, LANES : 2 * LANES], grad_scores[g], TN) for g in range(4)]
@@ -286,19 +287,21 @@
 
 
 def place_kernel(tab, own_ref, hw_ref, he_ref, rw_ref, re_ref, dq_ref, dk_ref, dv_ref, pad_ref):
-    cols, rows, channels = dq_ref.shape
-    for sub in range(rows // WIN):
-        for g in range(4):
-            s = sub * 4 + g
-            full = dot(hw_ref[s], rw_ref[sub]) + dot(he_ref[s], re_ref[sub])
-            full = (full + own_ref[s].astype(F32)).astype(BF).reshape(WIN, PAD, 3 * LANES)
-            for i in range(WIN):
-                for a in range(3):
-                    pad_ref[a, tab[sub, 4 + i], :, g * LANES : (g + 1) * LANES] = full[
-                        i, :, a * LANES : (a + 1) * LANES
-                    ]
-    for a, ref in enumerate((dq_ref, dk_ref, dv_ref)):
-        ref[...] = jnp.swapaxes(pad_ref[a, :, 0:WIN, :], 0, 1)
+    sub = pl.program_id(0)
+    for g in range(4):
+        full = dot(hw_ref[g], rw_ref[0]) + dot(he_ref[g], re_ref[0])
+        full = (full + own_ref[g].astype(F32)).astype(BF).reshape(WIN, PAD, 3 * LANES)
+        for i in range(WIN):
+            row = tab[sub, 4 + i]
+            for a in range(3):
+                pad_ref[a, row, :, g * LANES : (g + 1) * LANES] = full[
+                    i, :, a * LANES : (a + 1) * LANES
+                ]
+
+    @pl.when(sub == pl.num_programs(0) - 1)
+    def _():
+        for a, ref in enumerate((dq_ref, dk_ref, dv_ref)):
+            ref[...] = jnp.swapaxes(pad_ref[a, :, 0:WIN, :], 0, 1)
 
 
 def shape(*dims, kind=BF):
@@ -464,20 +467,25 @@
         partial = scattered_sum(partial, "lon", bit, ways)
     partial, home_w_d, home_e_d = lax.optimization_barrier((partial, home_w_d, home_e_d))
     partial = gathered_back(partial, "lon", *stages[-1])
+    partial, home_w_d, home_e_d = lax.optimization_barrier((partial, home_w_d, home_e_d))
     grads = pl.pallas_call(
         place_kernel,
-        in_specs=[SMEM] + [VMEM] * 5,
+        grid=(subs,),
+        in_specs=[
+            SMEM, group(OWN, 3 * LANES), group(OWN, BUF), group(OWN, BUF),
+            each(BUF, 3 * LANES), each(BUF, 3 * LANES),
+        ],
         out_specs=[VMEM] * 3,
         out_shape=[whole] * 3,
         scratch_shapes=[pltpu.VMEM((3, rows, PAD, channels), BF)],
-        compiler_params=SHARED,
-        cost_estimate=cost(2e9, 6e6),
+        compiler_params=WHOLE,
+        cost_estimate=cost(4e9, 6e6),
     )(tab, own_d, home_w, home_e, home_w_d, home_e_d)
 
+    for bit, ways in stages[-2:0:-1]:
+        partial = gathered_back(partial, "lon", bit, ways)
     partial, grads = lax.optimization_barrier((partial, grads))
-    for bit, ways in stages[-2::-1]:
-        partial = gathered_back(partial, "lon", bit, ways)
-    total = partial.astype(F32)
+    total = gathered_back(partial, "lon", *stages[0]).astype(F32)
 
     return (turned(mixed),) + tuple(turned(x) for x in grads) + (total,)
 

time: 91.7 us -> 90.4 us (0.986)
  local copies, waits for them, and re-layouts: 6.23 us -> 1.76 us
  Pallas kernels: 40.6 us -> 43.2 us
  starting transfers between devices: 29.5 us -> 30.5 us
    unnamed x22 -> x20, local copies, waits for them, and re-layouts: 6.18 us -> 1.71 us
    pallas_call x1, Pallas kernels: 3.77 us -> 6.41 us  [per_device(): pl.pallas_call(place_kernel, grid=(subs,), in_specs=[SMEM, group(OWN, 3 *...]
    ppermute x10, starting transfers between devices: 10.6 us -> 11.6 us  [swapped(): lax.ppermute(value, axis, [(source, source ^ bit) for source in range(cou...]
  transfers between devices with their start and end apart: 18 -> 18, of which waited for: 6 -> 5; matrix products, arithmetic and copies ran while one was open for 0% -> 0% of each run, Pallas kernels for 35% -> 39%
where the time goes in v3:
time: 90.4 us; the launch traced here: 90.1 us
  Pallas kernels  43.2 us (48%)
  starting transfers between devices  30.5 us (34%)
  waiting for transfers between devices  12.3 us (14%)
  local copies, waits for them, and re-layouts  1.76 us (2%)
  other arithmetic  1.34 us (1%)
  between operations  0.99 us (1%)
    ppermute x8, starting transfers between devices, passed_along(): return lax.ppermute(value, axis, pairs)  19 us
    ppermute x10, waiting for transfers between devices, swapped(): lax.ppermute(value, axis, [(source, source ^ bit) for source in range(cou...  12 us
    ppermute x10, starting transfers between devices, swapped(): lax.ppermute(value, axis, [(source, source ^ bit) for source in range(cou...  11.6 us
    pallas_call x1, Pallas kernels, per_device(): pl.pallas_call(backward_kernel, grid=(subs,), in_specs=[group(SUB, GH * S...  9.97 us
    pallas_call x1, Pallas kernels, per_device(): pl.pallas_call(forward_kernel, grid=(subs,), in_specs=[SMEM, group(SUB, 3...  8.1 us
    pallas_call x1, Pallas kernels, per_device(): pl.pallas_call(prepare_kernel, grid=(subs,), in_specs=[SMEM, group(OWN, 3...  6.8 us
    pallas_call x1, Pallas kernels, per_device(): pl.pallas_call(place_kernel, grid=(subs,), in_specs=[SMEM, group(OWN, 3 *...  6.41 us
    pallas_call x1, Pallas kernels, per_device(): pl.pallas_call(pack_kernel, in_specs=[SMEM, SMEM] + [VMEM] * 3, out_specs...  5.34 us
  transfers between devices with their start and end apart: 18, of which 5 were waited for; matrix products, arithmetic and copies ran while one was open for 0% of the time, Pallas kernels for 39%

profile of v3, /device:TPU:0, one launch (start us, length us, event | category | flops | bytes accessed | tf_op | source)
XLA Modules:
  0.0 90.1 jit_solution(11909842745766159293)
XLA Ops:
  0.6 5.3 %shard_map.110 = (s32[4,16]{1,0:T(4,128)}, bf16[16,192,384]{2,1,0:T(8,128)(2,1)}, bf16[4,176,384]{2,1,0:T(8,128)(2,1)}, bf16[4,176,384]{2,1,0:T(8,128)(2,1)}) custom-call(s32[48]{0:T(128)} %lat.1, s32[48]{0:T(128)} %lon.1, bf16[12,48,512]{2,1,0:T(8,128)(2,1)} %bitcast.10, bf16[12,48,512]{2,1,0:T(8,128)(2,1)} %bitcast.11, bf16[12,48,512]{2,1,0:T(8,128)(2,1)} %bitcast.12), custom_call_target="tpu_custom_call" | custom-call | flops 4000000000 | bytes 8000000 | tf_op jit(solution)/shard_map/pallas_call | solution.py:367
  6.0 5.5 %collective-permute-start = (bf16[4,176,384]{2,1,0:T(8,128)(2,1)}, bf16[4,176,384]{2,1,0:T(8,128)(2,1)S(1)}, u32[]{:S(2)}, u32[]{:S(2)}) collective-permute-start(bf16[4,176,384]{2,1,0:T(8,128)(2,1)} %get-tuple-element.51), channel_id=1, source_target_pairs={{0,15},{1,0},{2,1},{3,2},{4,3},{5,4},{6,5},{7,6},{8,7},{9,8},{10,9... | collective-permute-start | bytes 1622024 | tf_op jit(solution)/shard_map/ppermute | solution.py:34
  11.5 0.0 collective-permute-start.1
  11.5 0.0 copy-start.7
  11.5 3.7 %shard_map.113 = (bf16[16,192,128]{2,1,0:T(8,128)(2,1)}, bf16[4,176,128]{2,1,0:T(8,128)(2,1)}, bf16[4,176,128]{2,1,0:T(8,128)(2,1)}) custom-call(s32[4,16]{1,0:T(4,128)} %get-tuple-element.45.tab, bf16[12,48,512]{2,1,0:T(8,128)(2,1)} %bitcast.8, bf16[512,512]{1,0:T(8,128)(2,1)} %w_ref.3), custom_call_target="tpu_custom_call" | custom-call | flops 4000000000 | bytes 3000000 | tf_op jit(solution)/shard_map/pallas_call | solution.py:382
  15.2 4.4 %collective-permute-start.4 = (bf16[4,176,128]{2,1,0:T(8,128)(2,1)}, bf16[4,176,128]{2,1,0:T(8,128)(2,1)S(1)}, u32[]{:S(2)}, u32[]{:S(2)}) collective-permute-start(bf16[4,176,128]{2,1,0:T(8,128)(2,1)} %get-tuple-element.62), channel_id=1, source_target_pairs={{0,15},{1,0},{2,1},{3,2},{4,3},{5,4},{6,5},{7,6},{8,7},{9,8},{10,9... | collective-permute-start | bytes 540680 | tf_op jit(solution)/shard_map/ppermute | solution.py:34
  19.6 0.0 collective-permute-start.5
  19.6 0.0 copy-done.7
  19.6 0.0 copy-start.5
  19.6 1.7 %copy-done.5 = bf16[16,192,384]{2,1,0:T(8,128)(2,1)S(1)} copy-done((bf16[16,192,384]{2,1,0:T(8,128)(2,1)S(1)}, bf16[16,192,384]{2,1,0:T(8,128)(2,1)}, u32[]{:S(2)}) %copy-start.5) | copy-done | bytes 2359320
  21.3 6.8 %shard_map.111 = (bf16[16,144,384]{2,1,0:T(8,128)(2,1)S(1)}, bf16[16,144,192]{2,1,0:T(8,128)(2,1)S(1)}, bf16[16,144,176]{2,1,0:T(8,128)(2,1)S(1)}, bf16[16,144,1...) custom-call(s32[4,16]{1,0:T(4,128)S(1)} %copy-done.7, ...), custom_call_target="tpu_custom_call" | custom-call | flops 6000000000 | bytes 20000000 | tf_op jit(solution)/shard_map/pallas_call | solution.py:397
  28.1 0.0 copy-start.2
  28.1 0.0 copy-start.3
  28.1 0.0 collective-permute-done.rw_ref
  28.1 0.0 collective-permute-done.1.re_ref
  28.1 0.0 copy-start.6
  28.1 8.1 %shard_map.112 = (bf16[16,144,576]{2,1,0:T(8,128)(2,1)S(1)}, bf16[16,144,384]{2,1,0:T(8,128)(2,1)S(1)}, bf16[16,192,128]{2,1,0:T(8,128)(2,1)S(1)}, bf16[4,176,12...) custom-call(s32[4,16]{1,0:T(4,128)S(1)} %copy-done.7, bf16[16,144,384]{2,1,0:T(8,128)(2,1)S(1)} %get-tuple-element.47.win_ref, ...), custom_call_target="tpu_custom_call" | custom-call | flops 6000000000 | bytes 10000000 | tf_op jit(solution)/shard_map/pallas_call | solution.py:414
  36.3 0.1 collective-permute-start.2
  36.3 4.5 %collective-permute-start.3 = (bf16[4,176,128]{2,1,0:T(8,128)(2,1)S(1)}, bf16[4,176,128]{2,1,0:T(8,128)(2,1)S(1)}, u32[]{:S(2)}, u32[]{:S(2)}) collective-permute-start(bf16[4,176,128]{2,1,0:T(8,128)(2,1)S(1)} %get-tuple-element.57), channel_id=1, source_target_pairs={{0,15},{1,0},{2,1},{3,2},{4,3},{5,4},{6,5},{7,6},{8,7},{9,8},{10,9... | collective-permute-start | bytes 540680 | tf_op jit(solution)/shard_map/ppermute | solution.py:34
  40.8 0.0 collective-permute-done.4.rw_ref
  40.8 0.0 collective-permute-done.5.re_ref
  40.8 0.0 copy-done.6
  40.8 0.0 copy-start
  40.8 0.0 copy-start.1
  40.9 10.0 %shard_map.114 = (bf16[16,192,384]{2,1,0:T(8,128)(2,1)S(1)}, bf16[4,176,384]{2,1,0:T(8,128)(2,1)S(1)}, bf16[4,176,384]{2,1,0:T(8,128)(2,1)S(1)}) custom-call(bf16[16,144,576]{2,1,0:T(8,128)(2,1)S(1)} %get-tuple-element.58.probs_ref, bf16[16,144,384]{2,1,0:T(8,128)(2,1)S(1)} %get-tuple-element.59.cells_ref, bf16[16,192,128]{2,1,0:T(8,128)(2,1)S(1)} %copy-done.6, ...), custom_call_target="tpu_custom_call" | custom-call | flops 8000000000 | bytes 10000000 | tf_op jit(solution)/shard_map/pallas_call | solution.py:436
  50.8 0.0 copy-start.4
  50.8 0.0 collective-permute-done.2.rw_ref
  50.8 0.0 collective-permute-done.3.re_ref
  50.9 0.0 copy-done.2
  50.9 0.0 copy-done.3
  50.9 0.0 copy-done
  50.9 0.0 copy-done.1
  50.9 2.9 %shard_map.115 = (bf16[12,48,512]{2,1,0:T(8,128)(2,1)}, bf16[512,512]{1,0:T(8,128)(2,1)S(1)}) custom-call(s32[4,16]{1,0:T(4,128)S(1)} %copy-done.7, bf16[16,192,128]{2,1,0:T(8,128)(2,1)S(1)} %get-tuple-element.53.own_ref, bf16[16,192,176]{2,1,0:T(8,128)(2,1)S(1)} %get-tuple-element.54.hw_ref, bf16[16,192,176]{2,1,0:T(8,128)(2,1)S(1)} %get-tuple-element.55.he_ref, ...), custom_call_target="tpu_custom_call" | custom-call | flops 2000000000 | bytes 4000000 | tf_op jit(solution)/shard_map/pallas_call | solution.py:455
  53.8 0.0 copy-done.4
  53.8 0.1 collective-permute-start.6
  54.0 1.5 %collective-permute-done.6 = bf16[256,512]{1,0:T(8,128)(2,1)S(1)} collective-permute-done((bf16[256,512]{1,0:T(8,128)(2,1)S(1)}, bf16[256,512]{1,0:T(8,128)(2,1)S(1)}, u32[]{:S(2)}, u32[]{:S(2)}) %collective-permute-start.6) | collective-permute-done | bytes 262176 | tf_op jit(solution)/shard_map/ppermute | solution.py:39
  55.4 0.1 add_convert_fusion
  55.5 0.1 collective-permute-start.9
  55.6 0.1 collective-permute-start.8
  55.7 3.4 %collective-permute-start.7 = (bf16[64,512]{1,0:T(8,128)(2,1)S(1)}, bf16[64,512]{1,0:T(8,128)(2,1)S(1)}, u32[]{:S(2)}, u32[]{:S(2)}) collective-permute-start(bf16[64,512]{1,0:T(8,128)(2,1)S(1)} %get-tuple-element.91), channel_id=1, source_target_pairs={{0,6},{1,7},{2,4},{3,5},{4,2},{5,3},{6,0},{7,1},{8,14},{9,15},{10,... | collective-permute-start | bytes 196616 | tf_op jit(solution)/shard_map/ppermute | solution.py:39
  59.1 0.0 collective-permute-start.11
  59.1 4.4 %collective-permute-start.12 = (bf16[4,176,384]{2,1,0:T(8,128)(2,1)S(1)}, bf16[4,176,384]{2,1,0:T(8,128)(2,1)S(1)}, u32[]{:S(2)}, u32[]{:S(2)}) collective-permute-start(bf16[4,176,384]{2,1,0:T(8,128)(2,1)S(1)} %get-tuple-element.70), channel_id=1, source_target_pairs={{0,15},{1,0},{2,1},{3,2},{4,3},{5,4},{6,5},{7,6},{8,7},{9,8},{10,9... | collective-permute-start | bytes 1622024 | tf_op jit(solution)/shard_map/ppermute | solution.py:34
  63.5 0.0 collective-permute-done.9
  63.5 0.0 collective-permute-done.8
  63.5 0.0 collective-permute-done.7
  63.6 0.1 collective-permute-start.10
  63.7 7.1 %collective-permute-done.10 = bf16[32,512]{1,0:T(8,128)(2,1)S(1)} collective-permute-done((bf16[32,512]{1,0:T(8,128)(2,1)S(1)}, bf16[32,512]{1,0:T(8,128)(2,1)S(1)}, u32[]{:S(2)}, u32[]{:S(2)}) %collective-permute-start.10) | collective-permute-done | bytes 32800 | tf_op jit(solution)/shard_map/ppermute | solution.py:39
  70.8 0.3 collective-permute-done.11.rw_ref
  71.1 0.0 copy-start.8
  71.1 0.0 collective-permute-done.12.re_ref
  71.1 3.3 %collective-permute-start.13 = (bf16[32,512]{1,0:T(8,128)(2,1)S(1)}, bf16[32,512]{1,0:T(8,128)(2,1)S(1)}, u32[]{:S(2)}, u32[]{:S(2)}) collective-permute-start(bf16[32,512]{1,0:T(8,128)(2,1)S(1)} %add_convert_fusion.2), channel_id=1, source_target_pairs={{0,8},{1,9},{2,10},{3,11},{4,12},{5,13},{6,14},{7,15},{8,0},{9,1},... | collective-permute-start | bytes 98312 | tf_op jit(solution)/shard_map/ppermute | solution.py:39
  74.4 1.9 %collective-permute-done.13 = bf16[32,512]{1,0:T(8,128)(2,1)S(1)} collective-permute-done((bf16[32,512]{1,0:T(8,128)(2,1)S(1)}, bf16[32,512]{1,0:T(8,128)(2,1)S(1)}, u32[]{:S(2)}, u32[]{:S(2)}) %collective-permute-start.13) | collective-permute-done | bytes 32800 | tf_op jit(solution)/shard_map/ppermute | solution.py:39
  76.3 3.8 %collective-permute-start.14 = (bf16[64,512]{1,0:T(8,128)(2,1)S(1)}, bf16[64,512]{1,0:T(8,128)(2,1)S(1)}, u32[]{:S(2)}, u32[]{:S(2)}) collective-permute-start(bf16[64,512]{1,0:T(8,128)(2,1)S(1)} %pad_maximum_fusion.1), channel_id=1, source_target_pairs={{0,6},{1,7},{2,4},{3,5},{4,2},{5,3},{6,0},{7,1},{8,14},{9,15},{10,... | collective-permute-start | bytes 196616 | tf_op jit(solution)/shard_map/ppermute | solution.py:39
  80.0 0.0 copy-done.9
  80.0 0.8 collective-permute-start.15
  80.8 0.0 collective-permute-start.16
  80.8 0.0 copy-done.8
  80.8 6.4 %shard_map.116 = (bf16[12,48,512]{2,1,0:T(8,128)(2,1)}, bf16[12,48,512]{2,1,0:T(8,128)(2,1)}, bf16[12,48,512]{2,1,0:T(8,128)(2,1)}) custom-call(s32[4,16]{1,0:T(4,128)} %get-tuple-element.45.tab, bf16[16,192,384]{2,1,0:T(8,128)(2,1)} %copy-done.4, bf16[16,192,176]{2,1,0:T(8,128)(2,1)} %copy-done.2, bf16[16,192,176]{2,1,0:T(8,128)(2,1)} %copy-done.3, ...), custom_call_target="tpu_custom_call" | custom-call | flops 4000000000 | bytes 6000000 | tf_op jit(solution)/shard_map/pallas_call | solution.py:471
  87.2 0.0 collective-permute-done.14
  87.3 0.0 collective-permute-done.15
  87.3 0.0 collective-permute-done.16
  87.3 0.1 collective-permute-start.17
  87.4 1.5 %collective-permute-done.17 = bf16[256,512]{1,0:T(8,128)(2,1)S(1)} collective-permute-done((bf16[256,512]{1,0:T(8,128)(2,1)S(1)}, bf16[256,512]{1,0:T(8,128)(2,1)S(1)}, u32[]{:S(2)}, u32[]{:S(2)}) %collective-permute-start.17) | collective-permute-done | bytes 262176 | tf_op jit(solution)/shard_map/ppermute | solution.py:39
  89.0 1.1 %maximum_convert_fusion = f32[512,512]{1,0:T(8,128)} fusion(bf16[256,512]{1,0:T(8,128)(2,1)S(1)} %get-tuple-element.86, bf16[256,512]{1,0:T(8,128)(2,1)S(1)} %get-tuple-element.85), kind=kLoop, calls=%fused_computation | loop fusion | flops 1048576 | bytes 1572864 | tf_op jit(solution)/shard_map/convert_element_type | solution.py:488
  (11 shorter events, 0.2 us)
Async XLA Ops:
  6.0 22.1 %collective-permute-start = (bf16[4,176,384]{2,1,0:T(8,128)(2,1)}, bf16[4,176,384]{2,1,0:T(8,128)(2,1)S(1)}, u32[]{:S(2)}, u32[]{:S(2)}) collective-permute-start(bf16[4,176,384]{2,1,0:T(8,128)(2,1)} %get-tuple-element.51), channel_id=1, source_target_pairs={{0,15},{1,0},{2,1},{3,2},{4,3},{5,4},{6,5},{7,6},{8,7},{9,8},{10,9... | collective-permute-start | bytes 1622024 | tf_op jit(solution)/shard_map/ppermute | solution.py:34
  11.5 16.6 %collective-permute-start.1 = (bf16[4,176,384]{2,1,0:T(8,128)(2,1)}, bf16[4,176,384]{2,1,0:T(8,128)(2,1)}, u32[]{:S(2)}, u32[]{:S(2)}) collective-permute-start(bf16[4,176,384]{2,1,0:T(8,128)(2,1)} %get-tuple-element.52), channel_id=1, source_target_pairs={{0,1},{1,2},{2,3},{3,4},{4,5},{5,6},{6,7},{7,8},{8,9},{9,10},{10,1... | collective-permute-start | bytes 1622024 | tf_op jit(solution)/shard_map/ppermute | solution.py:34
  11.5 8.1 %copy-start.7 = (s32[4,16]{1,0:T(4,128)S(1)}, s32[4,16]{1,0:T(4,128)}, u32[]{:S(2)}) copy-start(s32[4,16]{1,0:T(4,128)} %get-tuple-element.45.tab) | copy-start | bytes 772
  15.2 25.7 %collective-permute-start.4 = (bf16[4,176,128]{2,1,0:T(8,128)(2,1)}, bf16[4,176,128]{2,1,0:T(8,128)(2,1)S(1)}, u32[]{:S(2)}, u32[]{:S(2)}) collective-permute-start(bf16[4,176,128]{2,1,0:T(8,128)(2,1)} %get-tuple-element.62), channel_id=1, source_target_pairs={{0,15},{1,0},{2,1},{3,2},{4,3},{5,4},{6,5},{7,6},{8,7},{9,8},{10,9... | collective-permute-start | bytes 540680 | tf_op jit(solution)/shard_map/ppermute | solution.py:34
  19.6 21.2 %collective-permute-start.5 = (bf16[4,176,128]{2,1,0:T(8,128)(2,1)}, bf16[4,176,128]{2,1,0:T(8,128)(2,1)S(1)}, u32[]{:S(2)}, u32[]{:S(2)}) collective-permute-start(bf16[4,176,128]{2,1,0:T(8,128)(2,1)} %get-tuple-element.63), channel_id=1, source_target_pairs={{0,1},{1,2},{2,3},{3,4},{4,5},{5,6},{6,7},{7,8},{8,9},{9,10},{10,1... | collective-permute-start | bytes 540680 | tf_op jit(solution)/shard_map/ppermute | solution.py:34
  19.6 1.7 %copy-start.5 = (bf16[16,192,384]{2,1,0:T(8,128)(2,1)S(1)}, bf16[16,192,384]{2,1,0:T(8,128)(2,1)}, u32[]{:S(2)}) copy-start(bf16[16,192,384]{2,1,0:T(8,128)(2,1)} %get-tuple-element.46.own_ref) | copy-start | bytes 7077892
  28.1 22.8 %copy-start.2 = (bf16[16,192,176]{2,1,0:T(8,128)(2,1)}, bf16[16,192,176]{2,1,0:T(8,128)(2,1)S(1)}, u32[]{:S(2)}) copy-start(bf16[16,192,176]{2,1,0:T(8,128)(2,1)S(1)} %get-tuple-element.54.hw_ref) | copy-start | bytes 3244036
  28.1 22.8 %copy-start.3 = (bf16[16,192,176]{2,1,0:T(8,128)(2,1)}, bf16[16,192,176]{2,1,0:T(8,128)(2,1)S(1)}, u32[]{:S(2)}) copy-start(bf16[16,192,176]{2,1,0:T(8,128)(2,1)S(1)} %get-tuple-element.55.he_ref) | copy-start | bytes 3244036
  28.1 12.7 %copy-start.6 = (bf16[16,192,128]{2,1,0:T(8,128)(2,1)S(1)}, bf16[16,192,128]{2,1,0:T(8,128)(2,1)}, u32[]{:S(2)}) copy-start(bf16[16,192,128]{2,1,0:T(8,128)(2,1)} %get-tuple-element.60.og_ref) | copy-start | bytes 2359300
  36.3 14.6 %collective-permute-start.2 = (bf16[4,176,128]{2,1,0:T(8,128)(2,1)S(1)}, bf16[4,176,128]{2,1,0:T(8,128)(2,1)S(1)}, u32[]{:S(2)}, u32[]{:S(2)}) collective-permute-start(bf16[4,176,128]{2,1,0:T(8,128)(2,1)S(1)} %get-tuple-element.56), channel_id=1, source_target_pairs={{0,1},{1,2},{2,3},{3,4},{4,5},{5,6},{6,7},{7,8},{8,9},{9,10},{10,1... | collective-permute-start | bytes 540680 | tf_op jit(solution)/shard_map/ppermute | solution.py:34
  36.3 14.5 %collective-permute-start.3 = (bf16[4,176,128]{2,1,0:T(8,128)(2,1)S(1)}, bf16[4,176,128]{2,1,0:T(8,128)(2,1)S(1)}, u32[]{:S(2)}, u32[]{:S(2)}) collective-permute-start(bf16[4,176,128]{2,1,0:T(8,128)(2,1)S(1)} %get-tuple-element.57), channel_id=1, source_target_pairs={{0,15},{1,0},{2,1},{3,2},{4,3},{5,4},{6,5},{7,6},{8,7},{9,8},{10,9... | collective-permute-start | bytes 540680 | tf_op jit(solution)/shard_map/ppermute | solution.py:34
  40.8 10.1 %copy-start = (bf16[48,12,512]{2,0,1:T(8,128)(2,1)S(1)}, bf16[48,12,512]{2,0,1:T(8,128)(2,1)}, u32[]{:S(2)}) copy-start(bf16[48,12,512]{2,0,1:T(8,128)(2,1)} %param.13) | copy-start | bytes 1769476
  40.8 10.0 %copy-start.1 = (bf16[512,512]{1,0:T(8,128)(2,1)S(1)}, bf16[512,512]{1,0:T(8,128)(2,1)}, u32[]{:S(2)}) copy-start(bf16[512,512]{1,0:T(8,128)(2,1)} %w_ref.3) | copy-start | bytes 1572868
  50.8 3.0 %copy-start.4 = (bf16[16,192,384]{2,1,0:T(8,128)(2,1)}, bf16[16,192,384]{2,1,0:T(8,128)(2,1)S(1)}, u32[]{:S(2)}) copy-start(bf16[16,192,384]{2,1,0:T(8,128)(2,1)S(1)} %get-tuple-element.75.own_ref) | copy-start | bytes 7077892
  53.8 1.6 %collective-permute-start.6 = (bf16[256,512]{1,0:T(8,128)(2,1)S(1)}, bf16[256,512]{1,0:T(8,128)(2,1)S(1)}, u32[]{:S(2)}, u32[]{:S(2)}) collective-permute-start(bf16[256,512]{1,0:T(8,128)(2,1)S(1)} %constant_dynamic-slice_fusion.4), channel_id=1, source_target_pairs={{0,1},{1,0},{2,3},{3,2},{4,5},{5,4},{6,7},{7,6},{8,9},{9,8},{10,11... | collective-permute-start | bytes 786440 | tf_op jit(solution)/shard_map/ppermute | solution.py:39
  55.5 8.0 %collective-permute-start.9 = (bf16[64,512]{1,0:T(8,128)(2,1)S(1)}, bf16[64,512]{1,0:T(8,128)(2,1)S(1)}, u32[]{:S(2)}, u32[]{:S(2)}) collective-permute-start(bf16[64,512]{1,0:T(8,128)(2,1)S(1)} %get-tuple-element.92), channel_id=1, source_target_pairs={{0,2},{1,3},{2,0},{3,1},{4,6},{5,7},{6,4},{7,5},{8,10},{9,11},{10,... | collective-permute-start | bytes 196616 | tf_op jit(solution)/shard_map/ppermute | solution.py:39
  55.6 7.9 %collective-permute-start.8 = (bf16[64,512]{1,0:T(8,128)(2,1)S(1)}, bf16[64,512]{1,0:T(8,128)(2,1)S(1)}, u32[]{:S(2)}, u32[]{:S(2)}) collective-permute-start(bf16[64,512]{1,0:T(8,128)(2,1)S(1)} %get-tuple-element.93), channel_id=1, source_target_pairs={{0,4},{1,5},{2,6},{3,7},{4,0},{5,1},{6,2},{7,3},{8,12},{9,13},{10,... | collective-permute-start | bytes 196616 | tf_op jit(solution)/shard_map/ppermute | solution.py:39
  55.7 7.8 %collective-permute-start.7 = (bf16[64,512]{1,0:T(8,128)(2,1)S(1)}, bf16[64,512]{1,0:T(8,128)(2,1)S(1)}, u32[]{:S(2)}, u32[]{:S(2)}) collective-permute-start(bf16[64,512]{1,0:T(8,128)(2,1)S(1)} %get-tuple-element.91), channel_id=1, source_target_pairs={{0,6},{1,7},{2,4},{3,5},{4,2},{5,3},{6,0},{7,1},{8,14},{9,15},{10,... | collective-permute-start | bytes 196616 | tf_op jit(solution)/shard_map/ppermute | solution.py:39
  59.1 12.0 %collective-permute-start.11 = (bf16[4,176,384]{2,1,0:T(8,128)(2,1)S(1)}, bf16[4,176,384]{2,1,0:T(8,128)(2,1)S(1)}, u32[]{:S(2)}, u32[]{:S(2)}) collective-permute-start(bf16[4,176,384]{2,1,0:T(8,128)(2,1)S(1)} %get-tuple-element.69), channel_id=1, source_target_pairs={{0,1},{1,2},{2,3},{3,4},{4,5},{5,6},{6,7},{7,8},{8,9},{9,10},{10,1... | collective-permute-start | bytes 1622024 | tf_op jit(solution)/shard_map/ppermute | solution.py:34
  59.1 12.0 %collective-permute-start.12 = (bf16[4,176,384]{2,1,0:T(8,128)(2,1)S(1)}, bf16[4,176,384]{2,1,0:T(8,128)(2,1)S(1)}, u32[]{:S(2)}, u32[]{:S(2)}) collective-permute-start(bf16[4,176,384]{2,1,0:T(8,128)(2,1)S(1)} %get-tuple-element.70), channel_id=1, source_target_pairs={{0,15},{1,0},{2,1},{3,2},{4,3},{5,4},{6,5},{7,6},{8,7},{9,8},{10,9... | collective-permute-start | bytes 1622024 | tf_op jit(solution)/shard_map/ppermute | solution.py:34
  63.6 7.1 %collective-permute-start.10 = (bf16[32,512]{1,0:T(8,128)(2,1)S(1)}, bf16[32,512]{1,0:T(8,128)(2,1)S(1)}, u32[]{:S(2)}, u32[]{:S(2)}) collective-permute-start(bf16[32,512]{1,0:T(8,128)(2,1)S(1)} %constant_dynamic-slice_fusion), channel_id=1, source_target_pairs={{0,8},{1,9},{2,10},{3,11},{4,12},{5,13},{6,14},{7,15},{8,0},{9,1},... | collective-permute-start | bytes 98312 | tf_op jit(solution)/shard_map/ppermute | solution.py:39
  71.1 9.8 %copy-start.8 = (bf16[4,176,384]{2,1,0:T(8,128)(2,1)}, bf16[4,176,384]{2,1,0:T(8,128)(2,1)S(1)}, u32[]{:S(2)}) copy-start(bf16[4,176,384]{2,1,0:T(8,128)(2,1)S(1)} %collective-permute-done.11.rw_ref) | copy-start | bytes 1622020
  71.1 9.0 %copy-start.9 = (bf16[4,176,384]{2,1,0:T(8,128)(2,1)}, bf16[4,176,384]{2,1,0:T(8,128)(2,1)S(1)}, u32[]{:S(2)}) copy-start(bf16[4,176,384]{2,1,0:T(8,128)(2,1)S(1)} %collective-permute-done.12.re_ref) | copy-start | bytes 1622020
  71.1 5.2 %collective-permute-start.13 = (bf16[32,512]{1,0:T(8,128)(2,1)S(1)}, bf16[32,512]{1,0:T(8,128)(2,1)S(1)}, u32[]{:S(2)}, u32[]{:S(2)}) collective-permute-start(bf16[32,512]{1,0:T(8,128)(2,1)S(1)} %add_convert_fusion.2), channel_id=1, source_target_pairs={{0,8},{1,9},{2,10},{3,11},{4,12},{5,13},{6,14},{7,15},{8,0},{9,1},... | collective-permute-start | bytes 98312 | tf_op jit(solution)/shard_map/ppermute | solution.py:39
  76.3 11.0 %collective-permute-start.14 = (bf16[64,512]{1,0:T(8,128)(2,1)S(1)}, bf16[64,512]{1,0:T(8,128)(2,1)S(1)}, u32[]{:S(2)}, u32[]{:S(2)}) collective-permute-start(bf16[64,512]{1,0:T(8,128)(2,1)S(1)} %pad_maximum_fusion.1), channel_id=1, source_target_pairs={{0,6},{1,7},{2,4},{3,5},{4,2},{5,3},{6,0},{7,1},{8,14},{9,15},{10,... | collective-permute-start | bytes 196616 | tf_op jit(solution)/shard_map/ppermute | solution.py:39
  80.0 7.2 %collective-permute-start.15 = (bf16[64,512]{1,0:T(8,128)(2,1)S(1)}, bf16[64,512]{1,0:T(8,128)(2,1)S(1)}, u32[]{:S(2)}, u32[]{:S(2)}) collective-permute-start(bf16[64,512]{1,0:T(8,128)(2,1)S(1)} %pad_maximum_fusion.1), channel_id=1, source_target_pairs={{0,4},{1,5},{2,6},{3,7},{4,0},{5,1},{6,2},{7,3},{8,12},{9,13},{10,... | collective-permute-start | bytes 196616 | tf_op jit(solution)/shard_map/ppermute | solution.py:39
  80.8 6.4 %collective-permute-start.16 = (bf16[64,512]{1,0:T(8,128)(2,1)S(1)}, bf16[64,512]{1,0:T(8,128)(2,1)S(1)}, u32[]{:S(2)}, u32[]{:S(2)}) collective-permute-start(bf16[64,512]{1,0:T(8,128)(2,1)S(1)} %pad_maximum_fusion.1), channel_id=1, source_target_pairs={{0,2},{1,3},{2,0},{3,1},{4,6},{5,7},{6,4},{7,5},{8,10},{9,11},{10,... | collective-permute-start | bytes 196616 | tf_op jit(solution)/shard_map/ppermute | solution.py:39
  87.3 1.6 %collective-permute-start.17 = (bf16[256,512]{1,0:T(8,128)(2,1)S(1)}, bf16[256,512]{1,0:T(8,128)(2,1)S(1)}, u32[]{:S(2)}, u32[]{:S(2)}) collective-permute-start(bf16[256,512]{1,0:T(8,128)(2,1)S(1)} %pad_maximum_fusion), channel_id=1, source_target_pairs={{0,1},{1,0},{2,3},{3,2},{4,5},{5,4},{6,7},{7,6},{8,9},{9,8},{10,11... | collective-permute-start | bytes 786440 | tf_op jit(solution)/shard_map/ppermute | solution.py:39

commit v4 on v3

--- a/solution.py
+++ b/solution.py
@@ -326,7 +326,7 @@
 def sum_stages(count):
     stages, bit = [(1, 2)], 2
     while bit < count:
-        ways = 4 if 4 * bit <= count else 2
+        ways = 4 if bit > 2 and 4 * bit <= count else 2
         stages.append((bit, ways))
         bit *= ways
     return stages

time: 90.4 us -> 90.1 us (level)
  transfers between devices with their start and end apart: 18 -> 18, of which waited for: 5 -> 9; matrix products, arithmetic and copies ran while one was open for 0% -> 0% of each run, Pallas kernels for 39% -> 39%
where the time goes in v4:
time: 90.1 us; the launch traced here: 89.8 us
  Pallas kernels  43.2 us (48%)
  starting transfers between devices  30.5 us (34%)
  waiting for transfers between devices  12 us (13%)
  local copies, waits for them, and re-layouts  1.77 us (2%)
  other arithmetic  1.35 us (1%)
  between operations  1.04 us (1%)
    ppermute x8, starting transfers between devices, passed_along(): return lax.ppermute(value, axis, pairs)  19 us
    ppermute x10, waiting for transfers between devices, swapped(): lax.ppermute(value, axis, [(source, source ^ bit) for source in range(cou...  12 us
    ppermute x10, starting transfers between devices, swapped(): lax.ppermute(value, axis, [(source, source ^ bit) for source in range(cou...  11.5 us
    pallas_call x1, Pallas kernels, per_device(): pl.pallas_call(backward_kernel, grid=(subs,), in_specs=[group(SUB, GH * S...  9.97 us
    pallas_call x1, Pallas kernels, per_device(): pl.pallas_call(forward_kernel, grid=(subs,), in_specs=[SMEM, group(SUB, 3...  8.1 us
    pallas_call x1, Pallas kernels, per_device(): pl.pallas_call(prepare_kernel, grid=(subs,), in_specs=[SMEM, group(OWN, 3...  6.8 us
    pallas_call x1, Pallas kernels, per_device(): pl.pallas_call(place_kernel, grid=(subs,), in_specs=[SMEM, group(OWN, 3 *...  6.4 us
    pallas_call x1, Pallas kernels, per_device(): pl.pallas_call(pack_kernel, in_specs=[SMEM, SMEM] + [VMEM] * 3, out_specs...  5.33 us
  transfers between devices with their start and end apart: 18, of which 9 were waited for; matrix products, arithmetic and copies ran while one was open for 0% of the time, Pallas kernels for 39%

profile of v4, /device:TPU:0, one launch (start us, length us, event | category | flops | bytes accessed | tf_op | source)
XLA Modules:
  0.0 89.8 jit_solution(16729651648927026026)
XLA Ops:
  0.6 5.3 %shard_map.110 = (s32[4,16]{1,0:T(4,128)}, bf16[16,192,384]{2,1,0:T(8,128)(2,1)}, bf16[4,176,384]{2,1,0:T(8,128)(2,1)}, bf16[4,176,384]{2,1,0:T(8,128)(2,1)}) custom-call(s32[48]{0:T(128)} %lat.1, s32[48]{0:T(128)} %lon.1, bf16[12,48,512]{2,1,0:T(8,128)(2,1)} %bitcast.10, bf16[12,48,512]{2,1,0:T(8,128)(2,1)} %bitcast.11, bf16[12,48,512]{2,1,0:T(8,128)(2,1)} %bitcast.12), custom_call_target="tpu_custom_call" | custom-call | flops 4000000000 | bytes 8000000 | tf_op jit(solution)/shard_map/pallas_call | solution.py:367
  6.0 5.5 %collective-permute-start = (bf16[4,176,384]{2,1,0:T(8,128)(2,1)}, bf16[4,176,384]{2,1,0:T(8,128)(2,1)S(1)}, u32[]{:S(2)}, u32[]{:S(2)}) collective-permute-start(bf16[4,176,384]{2,1,0:T(8,128)(2,1)} %get-tuple-element.51), channel_id=1, source_target_pairs={{0,15},{1,0},{2,1},{3,2},{4,3},{5,4},{6,5},{7,6},{8,7},{9,8},{10,9... | collective-permute-start | bytes 1622024 | tf_op jit(solution)/shard_map/ppermute | solution.py:34
  11.5 0.0 collective-permute-start.1
  11.5 0.0 copy-start.7
  11.5 3.7 %shard_map.113 = (bf16[16,192,128]{2,1,0:T(8,128)(2,1)}, bf16[4,176,128]{2,1,0:T(8,128)(2,1)}, bf16[4,176,128]{2,1,0:T(8,128)(2,1)}) custom-call(s32[4,16]{1,0:T(4,128)} %get-tuple-element.45.tab, bf16[12,48,512]{2,1,0:T(8,128)(2,1)} %bitcast.8, bf16[512,512]{1,0:T(8,128)(2,1)} %w_ref.3), custom_call_target="tpu_custom_call" | custom-call | flops 4000000000 | bytes 3000000 | tf_op jit(solution)/shard_map/pallas_call | solution.py:382
  15.2 4.4 %collective-permute-start.4 = (bf16[4,176,128]{2,1,0:T(8,128)(2,1)}, bf16[4,176,128]{2,1,0:T(8,128)(2,1)S(1)}, u32[]{:S(2)}, u32[]{:S(2)}) collective-permute-start(bf16[4,176,128]{2,1,0:T(8,128)(2,1)} %get-tuple-element.62), channel_id=1, source_target_pairs={{0,15},{1,0},{2,1},{3,2},{4,3},{5,4},{6,5},{7,6},{8,7},{9,8},{10,9... | collective-permute-start | bytes 540680 | tf_op jit(solution)/shard_map/ppermute | solution.py:34
  19.6 0.0 collective-permute-start.5
  19.6 0.0 copy-done.7
  19.6 1.7 %copy-done.5 = bf16[16,192,384]{2,1,0:T(8,128)(2,1)S(1)} copy-done((bf16[16,192,384]{2,1,0:T(8,128)(2,1)S(1)}, bf16[16,192,384]{2,1,0:T(8,128)(2,1)}, u32[]{:S(2)}) %copy-start.5) | copy-done | bytes 2359320
  21.3 6.8 %shard_map.111 = (bf16[16,144,384]{2,1,0:T(8,128)(2,1)S(1)}, bf16[16,144,192]{2,1,0:T(8,128)(2,1)S(1)}, bf16[16,144,176]{2,1,0:T(8,128)(2,1)S(1)}, bf16[16,144,1...) custom-call(s32[4,16]{1,0:T(4,128)S(1)} %copy-done.7, ...), custom_call_target="tpu_custom_call" | custom-call | flops 6000000000 | bytes 20000000 | tf_op jit(solution)/shard_map/pallas_call | solution.py:397
  28.1 0.0 copy-start.2
  28.1 0.0 copy-start.3
  28.1 0.0 collective-permute-done.rw_ref
  28.1 0.0 collective-permute-done.1.re_ref
  28.1 0.0 copy-start.6
  28.1 8.1 %shard_map.112 = (bf16[16,144,576]{2,1,0:T(8,128)(2,1)S(1)}, bf16[16,144,384]{2,1,0:T(8,128)(2,1)S(1)}, bf16[16,192,128]{2,1,0:T(8,128)(2,1)S(1)}, bf16[4,176,12...) custom-call(s32[4,16]{1,0:T(4,128)S(1)} %copy-done.7, bf16[16,144,384]{2,1,0:T(8,128)(2,1)S(1)} %get-tuple-element.47.win_ref, ...), custom_call_target="tpu_custom_call" | custom-call | flops 6000000000 | bytes 10000000 | tf_op jit(solution)/shard_map/pallas_call | solution.py:414
  36.2 0.1 collective-permute-start.2
  36.3 4.5 %collective-permute-start.3 = (bf16[4,176,128]{2,1,0:T(8,128)(2,1)S(1)}, bf16[4,176,128]{2,1,0:T(8,128)(2,1)S(1)}, u32[]{:S(2)}, u32[]{:S(2)}) collective-permute-start(bf16[4,176,128]{2,1,0:T(8,128)(2,1)S(1)} %get-tuple-element.57), channel_id=1, source_target_pairs={{0,15},{1,0},{2,1},{3,2},{4,3},{5,4},{6,5},{7,6},{8,7},{9,8},{10,9... | collective-permute-start | bytes 540680 | tf_op jit(solution)/shard_map/ppermute | solution.py:34
  40.8 0.0 collective-permute-done.4.rw_ref
  40.8 0.0 collective-permute-done.5.re_ref
  40.8 0.0 copy-done.6
  40.8 0.0 copy-start
  40.8 0.0 copy-start.1
  40.8 10.0 %shard_map.114 = (bf16[16,192,384]{2,1,0:T(8,128)(2,1)S(1)}, bf16[4,176,384]{2,1,0:T(8,128)(2,1)S(1)}, bf16[4,176,384]{2,1,0:T(8,128)(2,1)S(1)}) custom-call(bf16[16,144,576]{2,1,0:T(8,128)(2,1)S(1)} %get-tuple-element.58.probs_ref, bf16[16,144,384]{2,1,0:T(8,128)(2,1)S(1)} %get-tuple-element.59.cells_ref, bf16[16,192,128]{2,1,0:T(8,128)(2,1)S(1)} %copy-done.6, ...), custom_call_target="tpu_custom_call" | custom-call | flops 8000000000 | bytes 10000000 | tf_op jit(solution)/shard_map/pallas_call | solution.py:436
  50.8 0.0 copy-start.4
  50.8 0.0 collective-permute-done.2.rw_ref
  50.8 0.0 collective-permute-done.3.re_ref
  50.8 0.0 copy-done.2
  50.9 0.0 copy-done.3
  50.9 0.0 copy-done
  50.9 0.0 copy-done.1
  50.9 2.9 %shard_map.115 = (bf16[12,48,512]{2,1,0:T(8,128)(2,1)}, bf16[512,512]{1,0:T(8,128)(2,1)S(1)}) custom-call(s32[4,16]{1,0:T(4,128)S(1)} %copy-done.7, bf16[16,192,128]{2,1,0:T(8,128)(2,1)S(1)} %get-tuple-element.53.own_ref, bf16[16,192,176]{2,1,0:T(8,128)(2,1)S(1)} %get-tuple-element.54.hw_ref, bf16[16,192,176]{2,1,0:T(8,128)(2,1)S(1)} %get-tuple-element.55.he_ref, ...), custom_call_target="tpu_custom_call" | custom-call | flops 2000000000 | bytes 4000000 | tf_op jit(solution)/shard_map/pallas_call | solution.py:455
  53.8 0.0 copy-done.4
  53.8 0.1 collective-permute-start.6
  53.9 1.5 %collective-permute-done.6 = bf16[256,512]{1,0:T(8,128)(2,1)S(1)} collective-permute-done((bf16[256,512]{1,0:T(8,128)(2,1)S(1)}, bf16[256,512]{1,0:T(8,128)(2,1)S(1)}, u32[]{:S(2)}, u32[]{:S(2)}) %collective-permute-start.6) | collective-permute-done | bytes 262176 | tf_op jit(solution)/shard_map/ppermute | solution.py:39
  55.4 0.1 add_convert_fusion
  55.5 0.1 collective-permute-start.7
  55.6 0.2 collective-permute-start.11
  55.8 4.3 %collective-permute-start.12 = (bf16[4,176,384]{2,1,0:T(8,128)(2,1)S(1)}, bf16[4,176,384]{2,1,0:T(8,128)(2,1)S(1)}, u32[]{:S(2)}, u32[]{:S(2)}) collective-permute-start(bf16[4,176,384]{2,1,0:T(8,128)(2,1)S(1)} %get-tuple-element.70), channel_id=1, source_target_pairs={{0,15},{1,0},{2,1},{3,2},{4,3},{5,4},{6,5},{7,6},{8,7},{9,8},{10,9... | collective-permute-start | bytes 1622024 | tf_op jit(solution)/shard_map/ppermute | solution.py:34
  60.1 1.0 %collective-permute-done.7 = bf16[128,512]{1,0:T(8,128)(2,1)S(1)} collective-permute-done((bf16[128,512]{1,0:T(8,128)(2,1)S(1)}, bf16[128,512]{1,0:T(8,128)(2,1)S(1)}, u32[]{:S(2)}, u32[]{:S(2)}) %collective-permute-start.7) | collective-permute-done | bytes 131104 | tf_op jit(solution)/shard_map/ppermute | solution.py:39
  61.2 0.1 collective-permute-start.10
  61.3 5.2 %collective-permute-start.9 = (bf16[32,512]{1,0:T(8,128)(2,1)S(1)}, bf16[32,512]{1,0:T(8,128)(2,1)S(1)}, u32[]{:S(2)}, u32[]{:S(2)}) collective-permute-start(bf16[32,512]{1,0:T(8,128)(2,1)S(1)} %get-tuple-element.95), channel_id=1, source_target_pairs={{0,8},{1,9},{2,10},{3,11},{4,12},{5,13},{6,14},{7,15},{8,0},{9,1},... | collective-permute-start | bytes 98312 | tf_op jit(solution)/shard_map/ppermute | solution.py:39
  66.4 0.0 collective-permute-start.8
  66.4 1.8 %collective-permute-done.10 = bf16[32,512]{1,0:T(8,128)(2,1)S(1)} collective-permute-done((bf16[32,512]{1,0:T(8,128)(2,1)S(1)}, bf16[32,512]{1,0:T(8,128)(2,1)S(1)}, u32[]{:S(2)}, u32[]{:S(2)}) %collective-permute-start.10) | collective-permute-done | bytes 32800 | tf_op jit(solution)/shard_map/ppermute | solution.py:39
  68.3 0.4 collective-permute-done.9
  68.7 3.5 %collective-permute-done.8 = bf16[32,512]{1,0:T(8,128)(2,1)S(1)} collective-permute-done((bf16[32,512]{1,0:T(8,128)(2,1)S(1)}, bf16[32,512]{1,0:T(8,128)(2,1)S(1)}, u32[]{:S(2)}, u32[]{:S(2)}) %collective-permute-start.8) | collective-permute-done | bytes 32800 | tf_op jit(solution)/shard_map/ppermute | solution.py:39
  72.2 0.0 collective-permute-done.11.rw_ref
  72.2 0.0 copy-start.8
  72.2 0.0 collective-permute-done.12.re_ref
  72.2 0.0 copy-start.9
  72.2 1.6 %collective-permute-start.13 = (bf16[32,512]{1,0:T(8,128)(2,1)S(1)}, bf16[32,512]{1,0:T(8,128)(2,1)S(1)}, u32[]{:S(2)}, u32[]{:S(2)}) collective-permute-start(bf16[32,512]{1,0:T(8,128)(2,1)S(1)} %add_convert_fusion.2), channel_id=1, source_target_pairs={{0,12},{1,13},{2,14},{3,15},{4,8},{5,9},{6,10},{7,11},{8,4},{9,5},... | collective-permute-start | bytes 98312 | tf_op jit(solution)/shard_map/ppermute | solution.py:39
  73.8 0.0 collective-permute-start.14
  73.8 2.9 %collective-permute-start.15 = (bf16[32,512]{1,0:T(8,128)(2,1)S(1)}, bf16[32,512]{1,0:T(8,128)(2,1)S(1)}, u32[]{:S(2)}, u32[]{:S(2)}) collective-permute-start(bf16[32,512]{1,0:T(8,128)(2,1)S(1)} %add_convert_fusion.2), channel_id=1, source_target_pairs={{0,4},{1,5},{2,6},{3,7},{4,0},{5,1},{6,2},{7,3},{8,12},{9,13},{10,... | collective-permute-start | bytes 98312 | tf_op jit(solution)/shard_map/ppermute | solution.py:39
  76.7 1.4 %collective-permute-done.13 = bf16[32,512]{1,0:T(8,128)(2,1)S(1)} collective-permute-done((bf16[32,512]{1,0:T(8,128)(2,1)S(1)}, bf16[32,512]{1,0:T(8,128)(2,1)S(1)}, u32[]{:S(2)}, u32[]{:S(2)}) %collective-permute-start.13) | collective-permute-done | bytes 32800 | tf_op jit(solution)/shard_map/ppermute | solution.py:39
  78.1 0.8 collective-permute-done.14
  78.9 0.1 collective-permute-done.15
  79.0 0.0 copy-done.9
  79.0 1.6 %collective-permute-start.16 = (bf16[128,512]{1,0:T(8,128)(2,1)S(1)}, bf16[128,512]{1,0:T(8,128)(2,1)S(1)}, u32[]{:S(2)}, u32[]{:S(2)}) collective-permute-start(bf16[128,512]{1,0:T(8,128)(2,1)S(1)} %pad_maximum_fusion.1), channel_id=1, source_target_pairs={{0,2},{1,3},{2,0},{3,1},{4,6},{5,7},{6,4},{7,5},{8,10},{9,11},{10,... | collective-permute-start | bytes 393224 | tf_op jit(solution)/shard_map/ppermute | solution.py:39
  80.6 0.0 copy-done.8
  80.6 6.4 %shard_map.116 = (bf16[12,48,512]{2,1,0:T(8,128)(2,1)}, bf16[12,48,512]{2,1,0:T(8,128)(2,1)}, bf16[12,48,512]{2,1,0:T(8,128)(2,1)}) custom-call(s32[4,16]{1,0:T(4,128)} %get-tuple-element.45.tab, bf16[16,192,384]{2,1,0:T(8,128)(2,1)} %copy-done.4, bf16[16,192,176]{2,1,0:T(8,128)(2,1)} %copy-done.2, bf16[16,192,176]{2,1,0:T(8,128)(2,1)} %copy-done.3, ...), custom_call_target="tpu_custom_call" | custom-call | flops 4000000000 | bytes 6000000 | tf_op jit(solution)/shard_map/pallas_call | solution.py:471
  87.0 0.0 collective-permute-done.16
  87.1 0.1 collective-permute-start.17
  87.1 1.5 %collective-permute-done.17 = bf16[256,512]{1,0:T(8,128)(2,1)S(1)} collective-permute-done((bf16[256,512]{1,0:T(8,128)(2,1)S(1)}, bf16[256,512]{1,0:T(8,128)(2,1)S(1)}, u32[]{:S(2)}, u32[]{:S(2)}) %collective-permute-start.17) | collective-permute-done | bytes 262176 | tf_op jit(solution)/shard_map/ppermute | solution.py:39
  88.7 1.1 %maximum_convert_fusion = f32[512,512]{1,0:T(8,128)} fusion(bf16[256,512]{1,0:T(8,128)(2,1)S(1)} %get-tuple-element.86, bf16[256,512]{1,0:T(8,128)(2,1)S(1)} %get-tuple-element.85), kind=kLoop, calls=%fused_computation | loop fusion | flops 1048576 | bytes 1572864 | tf_op jit(solution)/shard_map/convert_element_type | solution.py:488
  (11 shorter events, 0.2 us)
Async XLA Ops:
  6.0 22.1 %collective-permute-start = (bf16[4,176,384]{2,1,0:T(8,128)(2,1)}, bf16[4,176,384]{2,1,0:T(8,128)(2,1)S(1)}, u32[]{:S(2)}, u32[]{:S(2)}) collective-permute-start(bf16[4,176,384]{2,1,0:T(8,128)(2,1)} %get-tuple-element.51), channel_id=1, source_target_pairs={{0,15},{1,0},{2,1},{3,2},{4,3},{5,4},{6,5},{7,6},{8,7},{9,8},{10,9... | collective-permute-start | bytes 1622024 | tf_op jit(solution)/shard_map/ppermute | solution.py:34
  11.5 16.6 %collective-permute-start.1 = (bf16[4,176,384]{2,1,0:T(8,128)(2,1)}, bf16[4,176,384]{2,1,0:T(8,128)(2,1)}, u32[]{:S(2)}, u32[]{:S(2)}) collective-permute-start(bf16[4,176,384]{2,1,0:T(8,128)(2,1)} %get-tuple-element.52), channel_id=1, source_target_pairs={{0,1},{1,2},{2,3},{3,4},{4,5},{5,6},{6,7},{7,8},{8,9},{9,10},{10,1... | collective-permute-start | bytes 1622024 | tf_op jit(solution)/shard_map/ppermute | solution.py:34
  11.5 8.1 %copy-start.7 = (s32[4,16]{1,0:T(4,128)S(1)}, s32[4,16]{1,0:T(4,128)}, u32[]{:S(2)}) copy-start(s32[4,16]{1,0:T(4,128)} %get-tuple-element.45.tab) | copy-start | bytes 772
  15.2 25.6 %collective-permute-start.4 = (bf16[4,176,128]{2,1,0:T(8,128)(2,1)}, bf16[4,176,128]{2,1,0:T(8,128)(2,1)S(1)}, u32[]{:S(2)}, u32[]{:S(2)}) collective-permute-start(bf16[4,176,128]{2,1,0:T(8,128)(2,1)} %get-tuple-element.62), channel_id=1, source_target_pairs={{0,15},{1,0},{2,1},{3,2},{4,3},{5,4},{6,5},{7,6},{8,7},{9,8},{10,9... | collective-permute-start | bytes 540680 | tf_op jit(solution)/shard_map/ppermute | solution.py:34
  19.6 21.2 %collective-permute-start.5 = (bf16[4,176,128]{2,1,0:T(8,128)(2,1)}, bf16[4,176,128]{2,1,0:T(8,128)(2,1)S(1)}, u32[]{:S(2)}, u32[]{:S(2)}) collective-permute-start(bf16[4,176,128]{2,1,0:T(8,128)(2,1)} %get-tuple-element.63), channel_id=1, source_target_pairs={{0,1},{1,2},{2,3},{3,4},{4,5},{5,6},{6,7},{7,8},{8,9},{9,10},{10,1... | collective-permute-start | bytes 540680 | tf_op jit(solution)/shard_map/ppermute | solution.py:34
  19.6 1.7 %copy-start.5 = (bf16[16,192,384]{2,1,0:T(8,128)(2,1)S(1)}, bf16[16,192,384]{2,1,0:T(8,128)(2,1)}, u32[]{:S(2)}) copy-start(bf16[16,192,384]{2,1,0:T(8,128)(2,1)} %get-tuple-element.46.own_ref) | copy-start | bytes 7077892
  28.1 22.8 %copy-start.2 = (bf16[16,192,176]{2,1,0:T(8,128)(2,1)}, bf16[16,192,176]{2,1,0:T(8,128)(2,1)S(1)}, u32[]{:S(2)}) copy-start(bf16[16,192,176]{2,1,0:T(8,128)(2,1)S(1)} %get-tuple-element.54.hw_ref) | copy-start | bytes 3244036
  28.1 22.8 %copy-start.3 = (bf16[16,192,176]{2,1,0:T(8,128)(2,1)}, bf16[16,192,176]{2,1,0:T(8,128)(2,1)S(1)}, u32[]{:S(2)}) copy-start(bf16[16,192,176]{2,1,0:T(8,128)(2,1)S(1)} %get-tuple-element.55.he_ref) | copy-start | bytes 3244036
  28.1 12.7 %copy-start.6 = (bf16[16,192,128]{2,1,0:T(8,128)(2,1)S(1)}, bf16[16,192,128]{2,1,0:T(8,128)(2,1)}, u32[]{:S(2)}) copy-start(bf16[16,192,128]{2,1,0:T(8,128)(2,1)} %get-tuple-element.60.og_ref) | copy-start | bytes 2359300
  36.2 14.6 %collective-permute-start.2 = (bf16[4,176,128]{2,1,0:T(8,128)(2,1)S(1)}, bf16[4,176,128]{2,1,0:T(8,128)(2,1)S(1)}, u32[]{:S(2)}, u32[]{:S(2)}) collective-permute-start(bf16[4,176,128]{2,1,0:T(8,128)(2,1)S(1)} %get-tuple-element.56), channel_id=1, source_target_pairs={{0,1},{1,2},{2,3},{3,4},{4,5},{5,6},{6,7},{7,8},{8,9},{9,10},{10,1... | collective-permute-start | bytes 540680 | tf_op jit(solution)/shard_map/ppermute | solution.py:34
  36.3 14.5 %collective-permute-start.3 = (bf16[4,176,128]{2,1,0:T(8,128)(2,1)S(1)}, bf16[4,176,128]{2,1,0:T(8,128)(2,1)S(1)}, u32[]{:S(2)}, u32[]{:S(2)}) collective-permute-start(bf16[4,176,128]{2,1,0:T(8,128)(2,1)S(1)} %get-tuple-element.57), channel_id=1, source_target_pairs={{0,15},{1,0},{2,1},{3,2},{4,3},{5,4},{6,5},{7,6},{8,7},{9,8},{10,9... | collective-permute-start | bytes 540680 | tf_op jit(solution)/shard_map/ppermute | solution.py:34
  40.8 10.1 %copy-start = (bf16[48,12,512]{2,0,1:T(8,128)(2,1)S(1)}, bf16[48,12,512]{2,0,1:T(8,128)(2,1)}, u32[]{:S(2)}) copy-start(bf16[48,12,512]{2,0,1:T(8,128)(2,1)} %param.13) | copy-start | bytes 1769476
  40.8 10.0 %copy-start.1 = (bf16[512,512]{1,0:T(8,128)(2,1)S(1)}, bf16[512,512]{1,0:T(8,128)(2,1)}, u32[]{:S(2)}) copy-start(bf16[512,512]{1,0:T(8,128)(2,1)} %w_ref.3) | copy-start | bytes 1572868
  50.8 3.0 %copy-start.4 = (bf16[16,192,384]{2,1,0:T(8,128)(2,1)}, bf16[16,192,384]{2,1,0:T(8,128)(2,1)S(1)}, u32[]{:S(2)}) copy-start(bf16[16,192,384]{2,1,0:T(8,128)(2,1)S(1)} %get-tuple-element.75.own_ref) | copy-start | bytes 7077892
  53.8 1.6 %collective-permute-start.6 = (bf16[256,512]{1,0:T(8,128)(2,1)S(1)}, bf16[256,512]{1,0:T(8,128)(2,1)S(1)}, u32[]{:S(2)}, u32[]{:S(2)}) collective-permute-start(bf16[256,512]{1,0:T(8,128)(2,1)S(1)} %constant_dynamic-slice_fusion.4), channel_id=1, source_target_pairs={{0,1},{1,0},{2,3},{3,2},{4,5},{5,4},{6,7},{7,6},{8,9},{9,8},{10,11... | collective-permute-start | bytes 786440 | tf_op jit(solution)/shard_map/ppermute | solution.py:39
  55.5 5.6 %collective-permute-start.7 = (bf16[128,512]{1,0:T(8,128)(2,1)S(1)}, bf16[128,512]{1,0:T(8,128)(2,1)S(1)}, u32[]{:S(2)}, u32[]{:S(2)}) collective-permute-start(bf16[128,512]{1,0:T(8,128)(2,1)S(1)} %constant_dynamic-slice_fusion.3), channel_id=1, source_target_pairs={{0,2},{1,3},{2,0},{3,1},{4,6},{5,7},{6,4},{7,5},{8,10},{9,11},{10,... | collective-permute-start | bytes 393224 | tf_op jit(solution)/shard_map/ppermute | solution.py:39
  55.6 16.5 %collective-permute-start.11 = (bf16[4,176,384]{2,1,0:T(8,128)(2,1)S(1)}, bf16[4,176,384]{2,1,0:T(8,128)(2,1)S(1)}, u32[]{:S(2)}, u32[]{:S(2)}) collective-permute-start(bf16[4,176,384]{2,1,0:T(8,128)(2,1)S(1)} %get-tuple-element.69), channel_id=1, source_target_pairs={{0,1},{1,2},{2,3},{3,4},{4,5},{5,6},{6,7},{7,8},{8,9},{9,10},{10,1... | collective-permute-start | bytes 1622024 | tf_op jit(solution)/shard_map/ppermute | solution.py:34
  55.8 16.4 %collective-permute-start.12 = (bf16[4,176,384]{2,1,0:T(8,128)(2,1)S(1)}, bf16[4,176,384]{2,1,0:T(8,128)(2,1)S(1)}, u32[]{:S(2)}, u32[]{:S(2)}) collective-permute-start(bf16[4,176,384]{2,1,0:T(8,128)(2,1)S(1)} %get-tuple-element.70), channel_id=1, source_target_pairs={{0,15},{1,0},{2,1},{3,2},{4,3},{5,4},{6,5},{7,6},{8,7},{9,8},{10,9... | collective-permute-start | bytes 1622024 | tf_op jit(solution)/shard_map/ppermute | solution.py:34
  61.2 7.1 %collective-permute-start.10 = (bf16[32,512]{1,0:T(8,128)(2,1)S(1)}, bf16[32,512]{1,0:T(8,128)(2,1)S(1)}, u32[]{:S(2)}, u32[]{:S(2)}) collective-permute-start(bf16[32,512]{1,0:T(8,128)(2,1)S(1)} %get-tuple-element.94), channel_id=1, source_target_pairs={{0,4},{1,5},{2,6},{3,7},{4,0},{5,1},{6,2},{7,3},{8,12},{9,13},{10,... | collective-permute-start | bytes 98312 | tf_op jit(solution)/shard_map/ppermute | solution.py:39
  61.3 7.4 %collective-permute-start.9 = (bf16[32,512]{1,0:T(8,128)(2,1)S(1)}, bf16[32,512]{1,0:T(8,128)(2,1)S(1)}, u32[]{:S(2)}, u32[]{:S(2)}) collective-permute-start(bf16[32,512]{1,0:T(8,128)(2,1)S(1)} %get-tuple-element.95), channel_id=1, source_target_pairs={{0,8},{1,9},{2,10},{3,11},{4,12},{5,13},{6,14},{7,15},{8,0},{9,1},... | collective-permute-start | bytes 98312 | tf_op jit(solution)/shard_map/ppermute | solution.py:39
  66.4 5.7 %collective-permute-start.8 = (bf16[32,512]{1,0:T(8,128)(2,1)S(1)}, bf16[32,512]{1,0:T(8,128)(2,1)S(1)}, u32[]{:S(2)}, u32[]{:S(2)}) collective-permute-start(bf16[32,512]{1,0:T(8,128)(2,1)S(1)} %get-tuple-element.93), channel_id=1, source_target_pairs={{0,12},{1,13},{2,14},{3,15},{4,8},{5,9},{6,10},{7,11},{8,4},{9,5},... | collective-permute-start | bytes 98312 | tf_op jit(solution)/shard_map/ppermute | solution.py:39
  72.2 8.4 %copy-start.8 = (bf16[4,176,384]{2,1,0:T(8,128)(2,1)}, bf16[4,176,384]{2,1,0:T(8,128)(2,1)S(1)}, u32[]{:S(2)}) copy-start(bf16[4,176,384]{2,1,0:T(8,128)(2,1)S(1)} %collective-permute-done.11.rw_ref) | copy-start | bytes 1622020
  72.2 6.8 %copy-start.9 = (bf16[4,176,384]{2,1,0:T(8,128)(2,1)}, bf16[4,176,384]{2,1,0:T(8,128)(2,1)S(1)}, u32[]{:S(2)}) copy-start(bf16[4,176,384]{2,1,0:T(8,128)(2,1)S(1)} %collective-permute-done.12.re_ref) | copy-start | bytes 1622020
  72.2 5.8 %collective-permute-start.13 = (bf16[32,512]{1,0:T(8,128)(2,1)S(1)}, bf16[32,512]{1,0:T(8,128)(2,1)S(1)}, u32[]{:S(2)}, u32[]{:S(2)}) collective-permute-start(bf16[32,512]{1,0:T(8,128)(2,1)S(1)} %add_convert_fusion.2), channel_id=1, source_target_pairs={{0,12},{1,13},{2,14},{3,15},{4,8},{5,9},{6,10},{7,11},{8,4},{9,5},... | collective-permute-start | bytes 98312 | tf_op jit(solution)/shard_map/ppermute | solution.py:39
  73.8 5.1 %collective-permute-start.14 = (bf16[32,512]{1,0:T(8,128)(2,1)S(1)}, bf16[32,512]{1,0:T(8,128)(2,1)S(1)}, u32[]{:S(2)}, u32[]{:S(2)}) collective-permute-start(bf16[32,512]{1,0:T(8,128)(2,1)S(1)} %add_convert_fusion.2), channel_id=1, source_target_pairs={{0,8},{1,9},{2,10},{3,11},{4,12},{5,13},{6,14},{7,15},{8,0},{9,1},... | collective-permute-start | bytes 98312 | tf_op jit(solution)/shard_map/ppermute | solution.py:39
  73.8 5.2 %collective-permute-start.15 = (bf16[32,512]{1,0:T(8,128)(2,1)S(1)}, bf16[32,512]{1,0:T(8,128)(2,1)S(1)}, u32[]{:S(2)}, u32[]{:S(2)}) collective-permute-start(bf16[32,512]{1,0:T(8,128)(2,1)S(1)} %add_convert_fusion.2), channel_id=1, source_target_pairs={{0,4},{1,5},{2,6},{3,7},{4,0},{5,1},{6,2},{7,3},{8,12},{9,13},{10,... | collective-permute-start | bytes 98312 | tf_op jit(solution)/shard_map/ppermute | solution.py:39
  79.0 8.0 %collective-permute-start.16 = (bf16[128,512]{1,0:T(8,128)(2,1)S(1)}, bf16[128,512]{1,0:T(8,128)(2,1)S(1)}, u32[]{:S(2)}, u32[]{:S(2)}) collective-permute-start(bf16[128,512]{1,0:T(8,128)(2,1)S(1)} %pad_maximum_fusion.1), channel_id=1, source_target_pairs={{0,2},{1,3},{2,0},{3,1},{4,6},{5,7},{6,4},{7,5},{8,10},{9,11},{10,... | collective-permute-start | bytes 393224 | tf_op jit(solution)/shard_map/ppermute | solution.py:39
  87.1 1.6 %collective-permute-start.17 = (bf16[256,512]{1,0:T(8,128)(2,1)S(1)}, bf16[256,512]{1,0:T(8,128)(2,1)S(1)}, u32[]{:S(2)}, u32[]{:S(2)}) collective-permute-start(bf16[256,512]{1,0:T(8,128)(2,1)S(1)} %pad_maximum_fusion), channel_id=1, source_target_pairs={{0,1},{1,0},{2,3},{3,2},{4,5},{5,4},{6,7},{7,6},{8,9},{9,8},{10,11... | collective-permute-start | bytes 786440 | tf_op jit(solution)/shard_map/ppermute | solution.py:39
